TPU v7x, 256 devices: a whole 4x4x8 slice. The times are simulated.
256 devices in a mesh: tile: 64 (over y, z, core), head: 4 (over x).
Axes of the slice: x: 4, y: 4, z: 8, core: 2. Of those that a mesh axis runs over, the one named last changes fastest.
Arguments:
- obs_feat: bfloat16 [524288, 512], P('tile', 'head'), may hold values from -70 to 70, as said below
- row_valid: int32 [524288], P('tile'), may hold values 0 or 1
- block_owner: int32 [4096, 1], P('tile'), may hold values from 0 to 63; in each aligned block of 64 rows (0 to 63, 64 to 127, ...) at most 2 rows name the same one
- block_pattern: int32 [4096, 16], P('tile'), may hold values 0 or 1
- latent: bfloat16 [32768, 512], P('tile'), may hold values from -35 to 35, as said below
- w_query: bfloat16 [512, 512], P(None, 'head'), may hold values from -0.25 to 0.25
- w_key: bfloat16 [512, 512], P(None, 'head'), may hold values from -0.25 to 0.25
- w_value: bfloat16 [512, 512], P(None, 'head'), may hold values from -0.25 to 0.25
- self_bias: float32 [8], P('head'), may hold values from 2.5 to 4.5
- w_out: bfloat16 [512, 512], P('head'), may hold values from -0.25 to 0.25
- norm_gain: float32 [512], replicated, may hold values from 0.25 to 1.75
- w_inc: bfloat16 [512, 128], replicated, may hold values from -0.25 to 0.25
- target: bfloat16 [32768, 128], P('tile'), may hold values from -6 to 6
Outputs:
- increment: float32 [32768, 128], P('tile')
- head_gradient: float32 [512, 128], P('head')
Inputs may be any that keep to these rules, and one draw needn't show every extreme that they name: `obs_feat`: embedded features; rows may differ widely in scale. `latent`: latent state; rows may differ widely in scale. `block_owner`: among the 64 blocks of one shard, no tile is named by more than 2 blocks, a bound that some block reaches.
All inputs are finite; a program needn't handle non-finite values. No bound on the sum of `row_valid` or of `block_pattern` on one device may be relied on, other than what follows from the above.
Results may differ from a plain program's by a relative error of at most 0.0093.
Values may be sent and summed in bfloat16 or wider, within the bound.
No kernel may reach another device: no remote copies, remote signals or barrier semaphores. Data moves between devices by JAX's collectives and lax.ppermute only.
A program may use at most 128 MiB of HBM per device.

v0:
```python
import math

import jax
import jax.numpy as jnp
from jax import lax
from jax.sharding import PartitionSpec as P


def body(
    obs_feat,
    row_valid,
    block_owner,
    block_pattern,
    latent,
    w_query,
    w_key,
    w_value,
    self_bias,
    w_out,
    norm_gain,
    w_inc,
    target,
):
    patch_number = lax.axis_size("tile")
    head_count = lax.axis_size("head")
    block_count = block_owner.shape[0]
    block_rows = obs_feat.shape[0] // block_count
    lat_rows = latent.shape[0]
    width_of_model = latent.shape[1]
    local_heads = self_bias.shape[0]
    query_cols = w_query.shape[1]
    head_size = query_cols // local_heads
    sub_count = block_pattern.shape[1]
    capacity = max(2, 2 * block_count // patch_number)
    slot_count = patch_number * capacity
    w_pair = jnp.concatenate([w_key, w_value], axis=1)
    block_dest = block_owner[:, 0]
    onehot = (block_dest[:, None] == jnp.arange(patch_number, dtype=jnp.int32)[None, :]).astype(
        jnp.int32
    )
    slot_rank = jnp.sum((jnp.cumsum(onehot, axis=0) - onehot) * onehot, axis=1)
    slot_of = block_dest * capacity + slot_rank
    matches = slot_of[:, None] == jnp.arange(slot_count, dtype=jnp.int32)[None, :]
    source = jnp.sum(
        jnp.where(matches, jnp.arange(block_count, dtype=jnp.int32)[:, None], 0), axis=0
    )
    filled = jnp.any(matches, axis=0).astype(jnp.bfloat16)
    row_mask = (
        row_valid.reshape(block_count, block_rows, 1)
        * block_pattern.reshape(block_count, 1, sub_count)
    ).astype(jnp.bfloat16)
    send_mask = (jnp.take(row_mask, source, axis=0) * filled[:, None, None]).reshape(
        patch_number, capacity * block_rows, sub_count
    )
    projected = jnp.dot(
        lax.all_gather(obs_feat, "head", axis=1, tiled=True),
        w_pair,
        preferred_element_type=jnp.float32,
    ).astype(jnp.bfloat16)
    payload = jnp.take(projected.reshape(block_count, block_rows, w_pair.shape[1]), source, axis=0)
    payload = payload.reshape(patch_number, capacity * block_rows, w_pair.shape[1])
    arrived, arrived_mask = (
        lax.all_to_all(payload, "tile", split_axis=0, concat_axis=0, tiled=True),
        lax.all_to_all(send_mask, "tile", split_axis=0, concat_axis=0, tiled=True),
    )
    key_value = arrived.reshape(slot_count * block_rows, w_pair.shape[1])
    mask_rows = arrived_mask.reshape(slot_count * block_rows, sub_count)
    score_scale = 1.0 / math.sqrt(head_size)
    queries = jnp.dot(latent, w_query, preferred_element_type=jnp.float32).astype(jnp.bfloat16)
    own_pair = jnp.dot(latent, w_pair, preferred_element_type=jnp.float32).astype(jnp.bfloat16)
    query_heads = queries.reshape(lat_rows, local_heads, head_size)
    own_key = own_pair[:, :query_cols].reshape(lat_rows, local_heads, head_size).astype(jnp.float32)
    own_value = (
        own_pair[:, query_cols:].reshape(lat_rows, local_heads, head_size).astype(jnp.float32)
    )
    own_score = (
        jnp.sum(query_heads.astype(jnp.float32) * own_key, axis=-1).T * score_scale
        + self_bias[:, None]
    )
    member = (
        jnp.arange(lat_rows, dtype=jnp.int32)[:, None] // (lat_rows // sub_count)
        == jnp.arange(sub_count, dtype=jnp.int32)[None, :]
    ).astype(jnp.bfloat16)
    group_rows = 8 * block_rows
    group_count = slot_count * block_rows // group_rows
    key_groups = key_value[:, :query_cols].reshape(group_count, group_rows, local_heads, head_size)
    value_groups = key_value[:, query_cols:].reshape(
        group_count, group_rows, local_heads, head_size
    )
    visibility_bundles = mask_rows.reshape(group_count, group_rows, sub_count)

    def attend(running, inputs):
        row_max, denominator, numerator = running
        key_block, value_block, mask_block = inputs
        allowed = jnp.dot(member, mask_block.T, preferred_element_type=jnp.float32) > 0.5
        scores = (
            jnp.einsum("lhd,ghd->hlg", query_heads, key_block, preferred_element_type=jnp.float32)
            * score_scale
        )
        scores = jnp.where(allowed[None], scores, jnp.float32(-1e30))
        new_max = jnp.maximum(row_max, jnp.max(scores, axis=-1))
        shrink = jnp.exp(row_max - new_max)
        weights = jnp.exp(scores - new_max[..., None])
        denominator = denominator * shrink + jnp.sum(weights, axis=-1)
        numerator = numerator * shrink[..., None] + jnp.einsum(
            "hlg,ghd->hld",
            weights.astype(jnp.bfloat16),
            value_block,
            preferred_element_type=jnp.float32,
        )
        return (new_max, denominator, numerator)

    def advance(running, inputs):
        running = attend(running, inputs)
        return (running, None)

    initial_state = (
        own_score,
        jnp.ones((local_heads, lat_rows), jnp.float32),
        own_value.transpose(1, 0, 2),
    )
    final_state, _ = lax.scan(
        advance, initial_state, (key_groups, value_groups, visibility_bundles)
    )
    row_max, denominator, numerator = final_state
    attended = (
        (numerator / denominator[..., None])
        .transpose(1, 0, 2)
        .reshape(lat_rows, query_cols)
        .astype(jnp.bfloat16)
    )
    partial_out = jnp.dot(attended, w_out, preferred_element_type=jnp.float32)
    head_pos = lax.axis_index("head")
    share_width = width_of_model // head_count
    target_f32 = target.astype(jnp.float32)
    whole_out = lax.psum(partial_out, "head")
    updated = latent.astype(jnp.float32) + whole_out
    normed_all = (
        updated * lax.rsqrt(jnp.mean(updated * updated, axis=-1, keepdims=True) + 1e-06) * norm_gain
    ).astype(jnp.bfloat16)
    predicted = jnp.dot(normed_all, w_inc, preferred_element_type=jnp.float32)
    normed = lax.dynamic_slice_in_dim(normed_all, head_pos * share_width, share_width, 1)
    residual = predicted - target_f32
    local_gradient = lax.dot_general(
        normed.astype(jnp.float32),
        residual,
        (((0,), (0,)), ((), ())),
        precision=lax.Precision.HIGHEST,
    )
    gradient_result = lax.psum(local_gradient, "tile") / math.sqrt(lat_rows * patch_number)
    return (predicted, gradient_result)


def solution(mesh):
    in_specs = (
        P("tile", "head"),
        P("tile"),
        P("tile", None),
        P("tile", None),
        P("tile", None),
        P(None, "head"),
        P(None, "head"),
        P(None, "head"),
        P("head"),
        P("head", None),
        P(),
        P(),
        P("tile", None),
    )
    out_specs = (P("tile", None), P("head", None))
    return jax.shard_map(body, mesh=mesh, in_specs=in_specs, out_specs=out_specs, check_vma=False)
```

profile of v0, /device:TPU:32, one launch (start us, length us, event | category | flops | bytes accessed | tf_op | source)
XLA Modules:
  0.0 778.9 jit_solution(13414614949521932372)
XLA Ops:
  15.1 11.8 %all-to-all-start = ((bf16[64,256,16]{1,2,0:T(8,128)(2,1)}), bf16[64,256,16]{1,2,0:T(8,128)(2,1)S(1)}, u32[]{:S(2)}, u32[]{:S(2)}) async-start(bf16[64,256,16]{1,2,0:T(8,128)(2,1)} %copy.52), calls=%async_computation | async-start | bytes 1048576 | tf_op jit(solution)/shard_map/all_to_all | solution.py:64
  26.9 75.5 %all-gather.2.cloned.1.call-done = bf16[8192,512]{1,0:T(8,128)(2,1)} async-done(((bf16[8192,128]{1,0:T(8,128)(2,1)}), bf16[8192,512]{1,0:T(8,128)(2,1)}) %all-gather.2.cloned.1.call-update) | async-done | bytes 8388624 | tf_op jit(solution)/shard_map/all_gather | solution.py:56
  102.4 7.8 fusion.27
  110.2 6.4 copy.60
  116.6 8.6 %gather_fusion.1 = bf16[128,128,256]{2,1,0:T(8,128)(2,1)} fusion(bf16[64,128,256]{2,1,0:T(8,128)(2,1)} %bitcast.98, s32[1024]{0:T(1024)S(1)} %pad_clamp_fusion), kind=kCustom, calls=%fused_computation.1 | custom fusion | bytes 16777728 | tf_op jit(solution)/shard_map/jit(_take)/gather | solution.py:60
  125.2 8.0 %bitcast_select_fusion.1 = bf16[64,256,256]{2,1,0:T(8,128)(2,1)} fusion(pred[64,256]{1,0:T(8,128)(4,1)S(1)} %bitcast.103, bf16[64,256,256]{2,1,0:T(8,128)(2,1)} %bitcast.99), kind=kLoop, calls=%fused_computation.32 | loop fusion | flops 4194304 | bytes 16793600 | tf_op jit(solution)/shard_map/jit(_take)/select_n | solution.py:60
  133.2 10.8 %all-to-all-start.1 = ((bf16[64,256,256]{2,1,0:T(8,128)(2,1)}), bf16[64,256,256]{2,1,0:T(8,128)(2,1)}, u32[]{:S(2)}, u32[]{:S(2)}) async-start(bf16[64,256,256]{2,1,0:T(8,128)(2,1)} %bitcast_select_fusion.1), calls=%async_computation.1 | async-start | bytes 16777216 | tf_op jit(solution)/shard_map/all_to_all | solution.py:63
  146.0 182.2 %all-to-all-done.1 = bf16[64,256,256]{2,1,0:T(8,128)(2,1)} async-done(((bf16[64,256,256]{2,1,0:T(8,128)(2,1)}), bf16[64,256,256]{2,1,0:T(8,128)(2,1)}, u32[]{:S(2)}, u32[]{:S(2)}) %all-to-all-start.1) | async-done | bytes 8388640 | tf_op jit(solution)/shard_map/all_to_all | solution.py:63
  328.1 5.7 fusion.42
  333.8 14.7 %reshape.146 = bf16[16,1024,2,64]{3,2,1,0:T(2,128)(2,1)} reshape(bf16[16384,128]{1,0:T(8,128)(2,1)} %get-tuple-element.153) | data formatting | bytes 8388608 | tf_op jit(solution)/shard_map/reshape | solution.py:86
  348.5 20.1 %copy.57 = bf16[16,1024,2,64]{1,3,2,0:T(8,128)(2,1)} copy(bf16[16,1024,2,64]{3,2,1,0:T(2,128)(2,1)} %reshape.146) | data formatting | bytes 8388608
  368.7 14.7 %reshape.147 = bf16[16,1024,2,64]{3,2,1,0:T(2,128)(2,1)} reshape(bf16[16384,128]{1,0:T(8,128)(2,1)} %get-tuple-element.152) | data formatting | bytes 8388608 | tf_op jit(solution)/shard_map/reshape | solution.py:87
  383.4 20.2 %copy.58 = bf16[16,1024,2,64]{1,3,2,0:T(8,128)(2,1)} copy(bf16[16,1024,2,64]{3,2,1,0:T(2,128)(2,1)} %reshape.147) | data formatting | bytes 8388608
  403.5 145.6 %while.15 = (s32[]{:T(128)}, f32[2,512]{1,0:T(2,128)S(1)}, f32[2,512]{1,0:T(2,128)S(1)}, f32[2,512,64]{1,2,0:T(8,128)S(1)}, bf16[16,1024,16]{1,2,0:T(8,128)(2,1)...) while((s32[]{:T(128)}, f32[2,512]{1,0:T(2,128)S(1)}, ...), condition=%wide.region_8.9_spmd.clone, body=%wide.region_5.8_spmd.clone.sunk | while | flops 297421824 | bytes 32738456 | solution.py:122
  404.1 2.0 fusion.71
  409.1 3.5 fusion.74
  413.2 2.0 fusion.71
  418.1 3.6 fusion.74
  422.3 2.0 fusion.71
  427.2 3.5 fusion.74
  431.4 2.0 fusion.71
  436.3 3.6 fusion.74
  440.5 2.0 fusion.71
  445.4 3.5 fusion.74
  449.6 2.0 fusion.71
  454.5 3.6 fusion.74
  458.7 2.0 fusion.71
  463.6 3.5 fusion.74
  467.8 2.0 fusion.71
  472.7 3.6 fusion.74
  476.9 2.0 fusion.71
  481.8 3.5 fusion.74
  486.0 2.0 fusion.71
  490.9 3.6 fusion.74
  495.1 2.0 fusion.71
  500.0 3.5 fusion.74
  504.2 2.0 fusion.71
  509.1 3.6 fusion.74
  513.3 2.0 fusion.71
  518.2 3.5 fusion.74
  522.4 2.0 fusion.71
  527.3 3.6 fusion.74
  531.5 2.0 fusion.71
  536.4 3.5 fusion.74
  540.6 2.0 fusion.71
  545.5 3.6 fusion.74
  550.6 48.6 %all-reduce.3.cloned.1.call-done = f32[512,512]{1,0:T(8,128)} async-done(((f32[512,512]{1,0:T(8,128)}), f32[512,512]{1,0:T(8,128)}) %all-reduce.3.cloned.1.call-update) | async-done | bytes 1048592 | tf_op jit(solution)/shard_map/psum | solution.py:136
  603.4 167.5 %all-reduce.5.cloned.1.call-done = f32[128,128]{1,0:T(8,128)} async-done(((f32[128,128]{1,0:T(8,128)}), f32[128,128]{1,0:T(8,128)}) %all-reduce.5.cloned.1.call-update) | async-done | bytes 65552 | tf_op jit(solution)/shard_map/psum | solution.py:150
  (182 shorter events, 72.3 us)
Async XLA Ops:
  7.2 542.0 %copy-start = (bf16[128,512]{1,0:T(8,128)(2,1)S(1)}, bf16[128,512]{1,0:T(8,128)(2,1)}, u32[]{:S(2)}) copy-start(bf16[128,512]{1,0:T(8,128)(2,1)} %param.24) | copy-start | bytes 393220
  7.2 95.2 %all-gather.2.cloned.1.call-start = ((), (), s32[]{:S(2)}) async-start(), calls=%async_computation.2 | async-start | bytes 10485760 | tf_op jit(solution)/shard_map/all_gather | solution.py:56
  13.0 13.9 %copy-start.6 = (bf16[512,128]{1,0:T(8,128)(2,1)S(1)}, bf16[512,128]{1,0:T(8,128)(2,1)}, u32[]{:S(2)}) copy-start(bf16[512,128]{1,0:T(8,128)(2,1)} %param.21) | copy-start | bytes 393220
  13.0 13.9 %copy-start.7 = (bf16[512,128]{1,0:T(8,128)(2,1)S(1)}, bf16[512,128]{1,0:T(8,128)(2,1)}, u32[]{:S(2)}) copy-start(bf16[512,128]{1,0:T(8,128)(2,1)} %param.22) | copy-start | bytes 393220
  15.1 118.2 %all-to-all-start = ((bf16[64,256,16]{1,2,0:T(8,128)(2,1)}), bf16[64,256,16]{1,2,0:T(8,128)(2,1)S(1)}, u32[]{:S(2)}, u32[]{:S(2)}) async-start(bf16[64,256,16]{1,2,0:T(8,128)(2,1)} %copy.52), calls=%async_computation | async-start | bytes 1048576 | tf_op jit(solution)/shard_map/all_to_all | solution.py:64
  133.2 11.1 %copy-start.2 = (bf16[512,512]{1,0:T(8,128)(2,1)S(1)}, bf16[512,512]{1,0:T(8,128)(2,1)}, u32[]{:S(2)}) copy-start(bf16[512,512]{1,0:T(8,128)(2,1)} %param.19) | copy-start | bytes 1572868
  133.2 11.5 %copy-start.4 = (bf16[512,128]{1,0:T(8,128)(2,1)S(1)}, bf16[512,128]{1,0:T(8,128)(2,1)}, u32[]{:S(2)}) copy-start(bf16[512,128]{1,0:T(8,128)(2,1)} %param.20) | copy-start | bytes 393220
  133.2 11.8 %copy-start.10 = (f32[2]{0:T(128)S(1)}, f32[2]{0:T(128)}, u32[]{:S(2)}) copy-start(f32[2]{0:T(128)} %param.23) | copy-start | bytes 28
  133.2 194.9 %all-to-all-start.1 = ((bf16[64,256,256]{2,1,0:T(8,128)(2,1)}), bf16[64,256,256]{2,1,0:T(8,128)(2,1)}, u32[]{:S(2)}, u32[]{:S(2)}) async-start(bf16[64,256,256]{2,1,0:T(8,128)(2,1)} %bitcast_select_fusion.1), calls=%async_computation.1 | async-start | bytes 16777216 | tf_op jit(solution)/shard_map/all_to_all | solution.py:63
  144.1 455.1 %all-reduce.3.cloned.1.call-start = ((), (), s32[]{:S(2)}) async-start(), calls=%async_computation.3 | async-start | bytes 2097152 | tf_op jit(solution)/shard_map/psum | solution.py:136
  406.1 1.9 copy-start.1
  415.2 1.9 copy-start.1
  424.3 1.9 copy-start.1
  433.4 1.9 copy-start.1
  442.5 1.9 copy-start.1
  451.6 1.9 copy-start.1
  460.7 1.9 copy-start.1
  469.8 1.9 copy-start.1
  478.9 1.9 copy-start.1
  488.0 1.9 copy-start.1
  497.1 1.9 copy-start.1
  506.2 1.9 copy-start.1
  515.3 1.9 copy-start.1
  524.4 1.9 copy-start.1
  533.5 1.9 copy-start.1
  542.6 1.9 copy-start.1
  549.1 51.5 %copy-start.9 = (f32[512]{0:T(512)S(1)}, f32[512]{0:T(512)}, u32[]{:S(2)}) copy-start(f32[512]{0:T(512)} %param.25) | copy-start | bytes 6148
  549.1 52.9 %copy-start.5 = (bf16[512,128]{1,0:T(8,128)(2,1)S(1)}, bf16[512,128]{1,0:T(8,128)(2,1)}, u32[]{:S(2)}) copy-start(bf16[512,128]{1,0:T(8,128)(2,1)} %param.26) | copy-start | bytes 393220
  549.1 53.2 %copy-start.8 = (bf16[512,128]{1,0:T(8,128)(2,1)S(1)}, bf16[512,128]{1,0:T(8,128)(2,1)}, u32[]{:S(2)}) copy-start(bf16[512,128]{1,0:T(8,128)(2,1)} %param.27) | copy-start | bytes 393220
  550.6 220.3 %all-reduce.5.cloned.1.call-start = ((), (), s32[]{:S(2)}) async-start(), calls=%async_computation.4 | async-start | bytes 131072 | tf_op jit(solution)/shard_map/psum | solution.py:150
  602.4 170.0 %copy-start.3 = (f32[512,128]{1,0:T(8,128)}, f32[512,128]{1,0:T(8,128)S(1)}, u32[]{:S(2)}) copy-start(f32[512,128]{1,0:T(8,128)S(1)} %fusion.45) | copy-start | bytes 786436
Sparse Core Ops, SparseCore 0:
  9.8 92.5 all-gather.1
  550.7 48.4 all-reduce.2
  603.6 167.1 all-reduce.4
where the time goes:
time: 785 us; the launch traced here: 779 us
  waiting for transfers between devices  474 us (60%)
  local copies, waits for them, and re-layouts  125 us (16%)
  matrix products  109 us (14%)
  other arithmetic  32.2 us (4%)
  starting transfers between devices  22.9 us (3%)
  between operations  14.1 us (2%)
    all_to_all x1, waiting for transfers between devices, body(): lax.all_to_all(payload, 'tile', split_axis=0, concat_axis=0, tiled=True)  182 us
    psum x1, waiting for transfers between devices, body(): lax.psum(local_gradient, 'tile') / math.sqrt(lat_rows * patch_number)  167 us
    all_gather x1, waiting for transfers between devices, body(): lax.all_gather(obs_feat, 'head', axis=1, tiled=True)  75.5 us
    dot_general x16, matrix products, attend(): jnp.einsum('hlg,ghd->hld', weights.astype(jnp.bfloat16), value_block, pre...  56.8 us
    psum x1, waiting for transfers between devices, body(): whole_out = lax.psum(partial_out, 'head')  48.6 us
    unnamed x27, local copies, waits for them, and re-layouts  41.5 us
    dot_general x16, matrix products, attend(): jnp.einsum('lhd,ghd->hlg', query_heads, key_block, preferred_element_type...  32.1 us
    while x48, local copies, waits for them, and re-layouts  30.7 us
  transfers between devices with their start and end apart: 5, of which 4 were waited for; matrix products, arithmetic and copies ran while one was open for 5% of the time, Pallas kernels for 0%

commit v1 on v0

v1 whole, which is shorter than its diff:
```python
import math

import jax
import jax.numpy as jnp
from jax import lax
from jax.experimental import pallas as pl
from jax.experimental.pallas import tpu as pltpu
from jax.sharding import PartitionSpec as P

BF = jnp.bfloat16
F32 = jnp.float32
NEG = -1e30
SLOTS = 2
CHUNK = 4


def route_kernel(owner, obs, info, payload, marks, counts, sem):
    tiles = payload.shape[0]
    blocks = obs.shape[0]
    marks[...] = jnp.zeros_like(marks)

    def clear(t, carry):
        counts[t] = 0
        return carry

    lax.fori_loop(0, tiles, clear, 0)

    def send(b, carry):
        t = owner[b]
        k = jnp.minimum(counts[t], SLOTS - 1)
        counts[t] = k + 1
        pltpu.make_async_copy(obs.at[b], payload.at[t, :, k], sem).start()
        marks[t * SLOTS + k] = info[b]
        return carry

    lax.fori_loop(0, blocks, send, 0)
    pltpu.make_async_copy(obs, obs, sem).wait()


def split3(v):
    hi = v.astype(BF).astype(F32)
    mid = (v - hi).astype(BF).astype(F32)
    return hi, mid, v - hi - mid


def attend_kernel(counts, lists, first, x, bias, qw, own, lat, wv, out, xbuf, acc, top, den):
    g = pl.program_id(0)
    heads, sub, width = qw.shape
    rows = heads * sub
    quarter = x.shape[3]
    parts = x.shape[1]
    cols = x.shape[4]
    n = counts[g]
    keep = first[0].astype(F32)
    queries = qw[...].reshape(rows, width)
    top[...] = own[...].reshape(rows, 128)
    den[...] = jnp.full((rows, 128), keep, F32)
    latent = lat[...].astype(F32) * keep
    acc[...] = jnp.broadcast_to(latent[None], (heads, sub, width)).reshape(rows, width)
    lane_slot = lax.broadcasted_iota(jnp.int32, (1, CHUNK * quarter), 1) // quarter

    def step(c, carry):
        shade = jnp.full((1, CHUNK * quarter), NEG, F32)
        for u in range(CHUNK):
            place = c * CHUNK + u
            slot = lists[g, jnp.minimum(place, n - 1)]
            s, k = slot // SLOTS, slot % SLOTS
            for i in range(parts):
                xbuf[u * quarter:(u + 1) * quarter, i * cols:(i + 1) * cols] = x[s, i, k]
            live = (lane_slot == u) & (place < n)
            shade = jnp.where(live, bias[pl.ds(slot, 1), :], shade)
        rows_x = xbuf[...]
        scores = lax.dot_general(
            queries, rows_x, (((1,), (1,)), ((), ())), preferred_element_type=F32
        ) + shade
        old = top[...]
        new = jnp.maximum(old, jnp.max(scores, axis=1, keepdims=True))
        weights = jnp.exp(scores - new)
        shrink = jnp.exp(old - new)
        top[...] = new
        den[...] = den[...] * shrink + jnp.sum(weights, axis=1, keepdims=True)
        more = jnp.dot(weights.astype(BF), rows_x, preferred_element_type=F32)
        acc[...] = acc[...] * jnp.concatenate([shrink] * (width // 128), axis=1) + more
        return carry

    lax.fori_loop(0, (n + CHUNK - 1) // CHUNK, step, 0)
    mixed = jnp.dot(acc[...].astype(BF), wv[...], preferred_element_type=F32)
    mixed = mixed.reshape(heads, sub, width)
    head_of = lax.broadcasted_iota(jnp.int32, (sub, width), 1) // (width // heads)
    lane = lax.broadcasted_iota(jnp.int32, (sub, 128), 1)
    top3 = split3(top[...].reshape(heads, sub, 128))
    den3 = split3(den[...].reshape(heads, sub, 128))
    numer = jnp.zeros((sub, width), F32)
    stats = jnp.zeros((sub, 128), F32)
    for h in range(heads):
        numer = jnp.where(head_of == h, mixed[h], numer)
        for q, part in enumerate(top3 + den3):
            stats = jnp.where(lane == q * heads + h, part[h], stats)
    out[:, :width] = numer.astype(BF)
    out[:, width:] = stats.astype(BF)


def finish_kernel(place, r0, r1, r2, r3, lat, w_out, gain, w_inc, target, out):
    width = lat.shape[1]
    heads = 8
    tops, dens, nums = [], [], []
    line = lax.broadcasted_iota(jnp.int32, (128, 2 * width), 0)
    col = lax.broadcasted_iota(jnp.int32, (128, 2 * width), 1)
    kind = line // heads
    match = (line % heads == (col % width) // (width // heads)) & (
        kind // 3 == col // width
    ) & (kind < 6)
    spread = match.astype(F32).astype(BF)
    for r in (r0, r1, r2, r3):
        wide = jnp.dot(r[:, width:], spread, preferred_element_type=F32)
        tops.append(wide[:, :width])
        dens.append(wide[:, width:])
        nums.append(r[:, :width].astype(F32))
    best = jnp.maximum(jnp.maximum(tops[0], tops[1]), jnp.maximum(tops[2], tops[3]))
    scale = [jnp.exp(v - best) for v in tops]
    numer = sum(a * b for a, b in zip(scale, nums))
    denom = sum(a * b for a, b in zip(scale, dens))
    attended = (numer / denom).astype(BF)
    updated = lat[...].astype(F32) + jnp.dot(attended, w_out[...], preferred_element_type=F32)
    power = jnp.mean(updated * updated, axis=1, keepdims=True)
    normed = (updated * lax.rsqrt(power + 1e-6) * gain[...]).astype(BF)
    predicted = jnp.dot(normed, w_inc[...], preferred_element_type=F32)
    residual = predicted - target[...].astype(F32)
    high = residual.astype(BF)
    low = (residual - high.astype(F32)).astype(BF)
    dims = (((0,), (0,)), ((), ()))
    grad = lax.dot_general(normed, high, dims, preferred_element_type=F32)
    grad = grad + lax.dot_general(normed, low, dims, preferred_element_type=F32)
    rows = predicted.shape[0]
    for d in range(4):
        out[d, :128, :] = grad[d * 128:(d + 1) * 128]
        out[d, 128:128 + rows, :] = predicted


def body(
    obs_feat,
    row_valid,
    block_owner,
    block_pattern,
    latent,
    w_query,
    w_key,
    w_value,
    self_bias,
    w_out,
    norm_gain,
    w_inc,
    target,
):
    tiles = lax.axis_size("tile")
    groups = lax.axis_size("head")
    me = lax.axis_index("head")
    blocks = block_owner.shape[0]
    block_rows = obs_feat.shape[0] // blocks
    quarter = block_rows // groups
    cols = obs_feat.shape[1]
    lat_rows, width = latent.shape
    subs = block_pattern.shape[1]
    sub = lat_rows // subs
    local_heads = self_bias.shape[0]
    heads = local_heads * groups
    head_size = width // heads
    slots = tiles * SLOTS
    share = lat_rows // groups

    def swap(v, axis, mask, size):
        return lax.ppermute(v, axis, [(d, d ^ mask) for d in range(size)])

    def pick(v, which):
        return lax.dynamic_index_in_dim(v, which, 0, keepdims=False)

    valid = lax.dynamic_index_in_dim(
        row_valid.reshape(blocks, groups, quarter), me, 1, keepdims=False
    )
    info = jnp.stack(
        [
            jnp.tile(valid, (1, 128 // quarter)),
            jnp.pad(block_pattern, ((0, 0), (0, 128 - subs))),
        ],
        axis=1,
    ).astype(F32)
    payload, marks = pl.pallas_call(
        route_kernel,
        grid_spec=pltpu.PrefetchScalarGridSpec(
            num_scalar_prefetch=1,
            grid=(1,),
            in_specs=[
                pl.BlockSpec(memory_space=pl.ANY),
                pl.BlockSpec((blocks, 2, 128), lambda i, o: (0, 0, 0)),
            ],
            out_specs=[
                pl.BlockSpec(memory_space=pl.ANY),
                pl.BlockSpec((slots, 2, 128), lambda i, o: (0, 0, 0)),
            ],
            scratch_shapes=[pltpu.SMEM((tiles,), jnp.int32), pltpu.SemaphoreType.DMA],
        ),
        out_shape=[
            jax.ShapeDtypeStruct((tiles, groups, SLOTS, quarter, cols), BF),
            jax.ShapeDtypeStruct((slots, 2, 128), F32),
        ],
        name="route",
    )(block_owner[:, 0], obs_feat.reshape(blocks, groups, quarter, cols), info)

    marks = lax.all_to_all(marks, "tile", split_axis=0, concat_axis=0, tiled=True)
    arrived = lax.all_to_all(
        payload.reshape(tiles * groups, SLOTS, quarter, cols),
        ("tile", "head"),
        split_axis=0,
        concat_axis=0,
        tiled=True,
    ).reshape(tiles, groups, SLOTS, quarter, cols)

    bias = (marks[:, 0, :] - 1.0) * (-NEG)
    live = (marks[:, 1, :subs] > 0.5).T
    before = jnp.triu(jnp.ones((slots, slots), BF), 1)
    place = jnp.dot(live.astype(BF), before, preferred_element_type=F32).astype(jnp.int32)
    counts = jnp.sum(live.astype(jnp.int32), axis=1)
    order = jnp.arange(slots, dtype=jnp.int32)
    hit = live[:, None, :] & (place[:, None, :] == order[None, :, None])
    lists = jnp.sum(jnp.where(hit, order[None, None, :], 0), axis=2)

    stacked = lax.all_gather(
        jnp.concatenate([w_query, w_key, w_value, w_out.T], axis=1), "head", axis=0
    )
    wq, wk, wv, wo = [
        stacked[:, :, a * 128:(a + 1) * 128].transpose(1, 0, 2).reshape(width, width)
        for a in range(4)
    ]
    wo = wo.T
    by_distance = jnp.stack(
        [self_bias] + [swap(self_bias, "head", d, groups) for d in range(1, groups)]
    )
    turn = jnp.arange(groups, dtype=jnp.int32) ^ me
    bias_all = jnp.take(by_distance, turn, axis=0).reshape(heads)
    queries = jnp.dot(latent, wq, preferred_element_type=F32).astype(BF)
    own_key = jnp.dot(latent, wk, preferred_element_type=F32).astype(BF)
    q3 = queries.reshape(lat_rows, heads, head_size)
    k3 = wk.reshape(width, heads, head_size)
    scale = 1.0 / math.sqrt(head_size)
    qw = (
        jnp.einsum("lhd,khd->hlk", q3, k3, preferred_element_type=F32) * scale
    ).astype(BF)
    own = (
        jnp.sum(
            q3.astype(F32) * own_key.reshape(lat_rows, heads, head_size).astype(F32), axis=-1
        ).T
        * scale
        + bias_all[:, None]
    )
    own = jnp.broadcast_to(own[:, :, None], (heads, lat_rows, 128))

    whole = lambda *shape: pl.BlockSpec(shape, lambda g, *_: (0,) * len(shape))
    partial = pl.pallas_call(
        attend_kernel,
        grid_spec=pltpu.PrefetchScalarGridSpec(
            num_scalar_prefetch=3,
            grid=(subs,),
            in_specs=[
                whole(tiles, groups, SLOTS, quarter, cols),
                whole(slots, 128),
                pl.BlockSpec((heads, sub, width), lambda g, *_: (0, g, 0)),
                pl.BlockSpec((heads, sub, 128), lambda g, *_: (0, g, 0)),
                pl.BlockSpec((sub, width), lambda g, *_: (g, 0)),
                whole(width, width),
            ],
            out_specs=pl.BlockSpec((sub, width + 128), lambda g, *_: (g, 0)),
            scratch_shapes=[
                pltpu.VMEM((CHUNK * quarter, width), BF),
                pltpu.VMEM((heads * sub, width), F32),
                pltpu.VMEM((heads * sub, 128), F32),
                pltpu.VMEM((heads * sub, 128), F32),
            ],
        ),
        out_shape=jax.ShapeDtypeStruct((lat_rows, width + 128), BF),
        compiler_params=pltpu.CompilerParams(vmem_limit_bytes=40 * 1024 * 1024),
        name="attend",
    )(counts, lists, (me == 0).astype(jnp.int32)[None], arrived, bias, qw, own, latent, wv)

    partial = partial.reshape(groups, share, width + 128)
    received = [pick(partial, me)] + [
        swap(pick(partial, me ^ d), "head", d, groups) for d in range(1, groups)
    ]
    row = lambda *shape: pl.BlockSpec(shape, lambda i, m: (m[0], 0))
    full = lambda *shape: pl.BlockSpec(shape, lambda i, m: (0,) * len(shape))
    packed = pl.pallas_call(
        finish_kernel,
        grid_spec=pltpu.PrefetchScalarGridSpec(
            num_scalar_prefetch=1,
            grid=(1,),
            in_specs=[full(share, width + 128)] * 4
            + [
                row(share, width),
                full(width, width),
                full(1, width),
                full(width, 128),
                row(share, 128),
            ],
            out_specs=full(groups, 128 + share, 128),
        ),
        out_shape=jax.ShapeDtypeStruct((groups, 128 + share, 128), F32),
        compiler_params=pltpu.CompilerParams(vmem_limit_bytes=32 * 1024 * 1024),
        name="finish",
    )(
        me[None].astype(jnp.int32),
        *received,
        latent,
        wo,
        norm_gain[None, :],
        w_inc,
        target,
    )
    pieces = [pick(packed, me)] + [
        swap(pick(packed, me ^ d), "head", d, groups) for d in range(1, groups)
    ]
    grads = [p[:128] for p in pieces]
    grad = (grads[0] + grads[1]) + (grads[2] + grads[3])
    stacked_pred = jnp.stack([p[128:] for p in pieces])
    predicted = jnp.take(
        stacked_pred, jnp.arange(groups, dtype=jnp.int32) ^ me, axis=0
    ).reshape(lat_rows, 128)
    for mask in (1, 2, 4, 8, 16, 32):
        grad = grad + swap(grad, "tile", mask, tiles)
    return predicted, grad * (1.0 / math.sqrt(lat_rows * tiles))


def solution(mesh):
    in_specs = (
        P("tile", "head"),
        P("tile"),
        P("tile", None),
        P("tile", None),
        P("tile", None),
        P(None, "head"),
        P(None, "head"),
        P(None, "head"),
        P("head"),
        P("head", None),
        P(),
        P(),
        P("tile", None),
    )
    out_specs = (P("tile", None), P("head", None))
    return jax.shard_map(body, mesh=mesh, in_specs=in_specs, out_specs=out_specs, check_vma=False)
```

time: 785 us -> 291 us (0.37)
  waiting for transfers between devices: 474 us -> 123 us
  local copies, waits for them, and re-layouts: 125 us -> 8.81 us
  matrix products: 109 us -> 4.35 us
  Pallas kernels: 0 us -> 86 us
  other arithmetic: 32.2 us -> 3.82 us
  blocking collectives: 0 us -> 21.8 us
    psum x2 -> x0, waiting for transfers between devices: 216 us -> none  [the longest x1 167 us: body(): lax.psum(local_gradient, 'tile') / math.sqrt(lat_rows * patch_number)]
    all_to_all x2 -> x1, waiting for transfers between devices: 182 us -> 40.3 us  [body(): lax.all_to_all(payload.reshape(tiles * groups, SLOTS, quarter, cols), ('t...]
    dot_general x54 -> x4, matrix products: 109 us -> 4.35 us  [the longest x1 3.27 us: body(): jnp.einsum('lhd,khd->hlk', q3, k3, preferred_element_type=F32) * scale]
    pallas_call x0 -> x3, Pallas kernels: none -> 86 us  [the longest x1 67.2 us: body(): pl.pallas_call(route_kernel, grid_spec=pltpu.PrefetchScalarGridSpec(num_s...]
    ppermute x0 -> x15, waiting for transfers between devices: none -> 42.2 us  [swap(): return lax.ppermute(v, axis, [(d, d ^ mask) for d in range(size)])]
    unnamed x27 -> x23, local copies, waits for them, and re-layouts: 41.5 us -> 3.17 us
    all_gather x1, waiting for transfers between devices: 75.5 us -> 40.7 us  [body(): lax.all_gather(jnp.concatenate([w_query, w_key, w_value, w_out.T], axis=1...]
    reshape x3 -> x2, local copies, waits for them, and re-layouts: 35.8 us -> 0.96 us  [the longest x1 0.87 us: body(): row_valid.reshape(blocks, groups, quarter)]
  transfers between devices with their start and end apart: 5 -> 17, of which waited for: 4 -> 15; matrix products, arithmetic and copies ran while one was open for 5% -> 4% of each run, Pallas kernels for 0% -> 0%
where the time goes in v1:
time: 291 us; the launch traced here: 288 us
  waiting for transfers between devices  123 us (42%)
  Pallas kernels  86 us (30%)
  starting transfers between devices  26 us (9%)
  blocking collectives  21.8 us (7%)
  between operations  14.4 us (5%)
  local copies, waits for them, and re-layouts  8.81 us (3%)
  matrix products  4.35 us (1%)
  other arithmetic  3.82 us (1%)
    pallas_call x1, Pallas kernels, body(): pl.pallas_call(route_kernel, grid_spec=pltpu.PrefetchScalarGridSpec(num_s...  67.2 us
    ppermute x15, waiting for transfers between devices, swap(): return lax.ppermute(v, axis, [(d, d ^ mask) for d in range(size)])  42.2 us
    all_gather x1, waiting for transfers between devices, body(): lax.all_gather(jnp.concatenate([w_query, w_key, w_value, w_out.T], axis=1...  40.7 us
    all_to_all x1, waiting for transfers between devices, body(): lax.all_to_all(payload.reshape(tiles * groups, SLOTS, quarter, cols), ('t...  40.3 us
    all_to_all x1, blocking collectives, body(): lax.all_to_all(marks, 'tile', split_axis=0, concat_axis=0, tiled=True)  21.8 us
    pallas_call x1, Pallas kernels, body(): pl.pallas_call(attend_kernel, grid_spec=pltpu.PrefetchScalarGridSpec(num_...  17.5 us
    ppermute x15, starting transfers between devices, swap(): return lax.ppermute(v, axis, [(d, d ^ mask) for d in range(size)])  17.1 us
    all_to_all x1, starting transfers between devices, body(): lax.all_to_all(payload.reshape(tiles * groups, SLOTS, quarter, cols), ('t...  8.83 us
  transfers between devices with their start and end apart: 17, of which 15 were waited for; matrix products, arithmetic and copies ran while one was open for 4% of the time, Pallas kernels for 0%

profile of v1, /device:TPU:32, one launch (start us, length us, event | category | flops | bytes accessed | tf_op | source)
XLA Modules:
  0.0 288.3 jit_solution(16008389606275790740)
XLA Ops:
  7.2 0.8 copy.76
  7.9 0.9 reshape.94
  9.0 0.7 add_convert_fusion.info
  9.7 67.2 %route.1 = (bf16[64,4,2,32,128]{4,3,2,1,0:T(8,128)(2,1)}, f32[128,2,128]{2,1,0:T(2,128)}) custom-call(s32[64]{0:T(128)} %bitcast.107, bf16[64,4,32,128]{3,2,1,0:T(8,128)(2,1)} %bitcast.99, f32[64,2,128]{2,1,0:T(2,128)} %add_convert_fusion.info), custom_call_target="tpu_custom_call" | custom-call | tf_op jit(solution)/shard_map/route/pallas_call | solution.py:187
  77.0 21.8 %all_to_all.10 = f32[128,2,128]{2,1,0:T(2,128)S(1)} all-to-all(f32[128,2,128]{2,1,0:T(2,128)} %get-tuple-element.4), channel_id=1, replica_groups=mesh['tile'=64,'head'=4] {'tile'}, dimensions={0} | all-to-all | bytes 262144 | tf_op jit(solution)/shard_map/all_to_all | solution.py:209
  98.8 8.8 %all-to-all-start.1 = ((bf16[256,2,32,128]{3,2,1,0:T(8,128)(2,1)}), bf16[256,2,32,128]{3,2,1,0:T(8,128)(2,1)}, u32[]{:S(2)}, u32[]{:S(2)}) async-start(bf16[256,2,32,128]{3,2,1,0:T(8,128)(2,1)} %bitcast.94), calls=%async_computation.1 | async-start | bytes 8388608 | tf_op jit(solution)/shard_map/all_to_all | solution.py:210
  107.9 0.9 pad_maximum_fusion
  108.8 2.8 collective-permute-start.2
  111.6 0.8 collective-permute-start.1
  112.4 0.5 collective-permute-start
  113.0 3.4 %collective-permute-done.2 = f32[2]{0:T(128)S(1)} collective-permute-done((f32[2]{0:T(128)S(1)}, f32[2]{0:T(128)S(1)}, u32[]{:S(2)}, u32[]{:S(2)}) %collective-permute-start.2) | collective-permute-done | bytes 40 | tf_op jit(solution)/shard_map/ppermute | solution.py:172
  116.3 0.3 collective-permute-done.1
  116.6 0.6 gather_fusion
  117.8 0.4 select_reduce_fusion.lists
  118.2 40.7 %all-gather.3.cloned.1.call-done = bf16[2048,512]{1,0:T(8,128)(2,1)} async-done(((bf16[512,512]{1,0:T(8,128)(2,1)}), bf16[2048,512]{1,0:T(8,128)(2,1)}) %all-gather.3.cloned.1.call-update) | async-done | bytes 2097168 | tf_op jit(solution)/shard_map/all_gather | solution.py:227
  158.8 1.7 slice_bitcast_fusion
  160.6 0.2 copy.81
  161.1 0.5 convolution_convert_fusion.1
  161.6 0.5 multiply_reduce_fusion
  162.2 3.3 %multiply_convert_fusion.qw = bf16[8,512,512]{2,1,0:T(8,128)(2,1)} fusion(bf16[512,8,64]{0,2,1:T(8,128)(2,1)S(1)} %bitcast.95, bf16[512,8,64]{0,2,1:T(8,128)(2,1)S(1)} %bitcast.97), kind=kOutput, calls=%fused_computation.2 | convolution fusion | flops 272629760 | bytes 5242880 | tf_op jit(solution)/shard_map/lhd,khd->hlk/dot_general | solution.py:246
  165.4 40.3 %all-to-all-done.1 = bf16[256,2,32,128]{3,2,1,0:T(8,128)(2,1)} async-done(((bf16[256,2,32,128]{3,2,1,0:T(8,128)(2,1)}), bf16[256,2,32,128]{3,2,1,0:T(8,128)(2,1)}, u32[]{:S(2)}, u32[]{:S(2)}) %all-to-all-start.1) | async-done | bytes 4194336 | tf_op jit(solution)/shard_map/all_to_all | solution.py:210
  205.7 0.6 broadcast_in_dim.71.own
  206.3 2.2 copy-done
  208.5 17.5 %attend.1 = bf16[512,640]{1,0:T(8,128)(2,1)S(1)} custom-call(s32[16]{0:T(128)S(1)} %get-tuple-element.6.counts, s32[16,128]{1,0:T(8,128)S(1)} %select_reduce_fusion.lists, s32[1]{0:T(128)} %bitcast.10.first, bf16[64,4,2,32,128]{4,3,2,1,0:T(8,128)(2,1)} %bitcast.12.x, f32[128,128]{1,0:T(8,128)S(1)} %multiply_bitcast_fusion.bias, ...), custom_call_target="tpu_custom_call" | custom-call | tf_op jit(solution)/shard_map/attend/pallas_call | solution.py:258
  226.1 0.7 collective-permute-start.3
  226.8 1.1 collective-permute-start.4
  227.9 3.0 %collective-permute-start.5 = (bf16[128,640]{1,0:T(8,128)(2,1)S(1)}, bf16[128,640]{1,0:T(8,128)(2,1)S(1)}, u32[]{:S(2)}, u32[]{:S(2)}) collective-permute-start(bf16[128,640]{1,0:T(8,128)(2,1)S(1)} %get-tuple-element.12), channel_id=1, source_target_pairs={{0,3},{1,2},{2,1},{3,0},{4,7},{5,6},{6,5},{7,4},{8,11},{9,10},{10,... | collective-permute-start | bytes 491528 | tf_op jit(solution)/shard_map/ppermute | solution.py:172
  231.1 2.1 collective-permute-done.3.r1
  233.3 2.4 collective-permute-done.4.r2
  235.7 3.5 %collective-permute-done.5.r3 = bf16[128,640]{1,0:T(8,128)(2,1)S(1)} collective-permute-done((bf16[128,640]{1,0:T(8,128)(2,1)S(1)}, bf16[128,640]{1,0:T(8,128)(2,1)S(1)}, u32[]{:S(2)}, u32[]{:S(2)}) %collective-permute-start.5) | collective-permute-done | bytes 163872 | tf_op jit(solution)/shard_map/ppermute | solution.py:172
  239.2 1.3 finish.1
  240.6 3.1 %collective-permute-start.8 = (f32[256,128]{1,0:T(8,128)S(1)}, f32[256,128]{1,0:T(8,128)S(1)}, u32[]{:S(2)}, u32[]{:S(2)}) collective-permute-start(f32[256,128]{1,0:T(8,128)S(1)} %get-tuple-element.17), channel_id=1, source_target_pairs={{0,3},{1,2},{2,1},{3,0},{4,7},{5,6},{6,5},{7,4},{8,11},{9,10},{10,... | collective-permute-start | bytes 393224 | tf_op jit(solution)/shard_map/ppermute | solution.py:172
  243.7 1.3 collective-permute-start.6
  244.9 4.2 %collective-permute-done.8 = f32[256,128]{1,0:T(8,128)S(1)} collective-permute-done((f32[256,128]{1,0:T(8,128)S(1)}, f32[256,128]{1,0:T(8,128)S(1)}, u32[]{:S(2)}, u32[]{:S(2)}) %collective-permute-start.8) | collective-permute-done | bytes 131104 | tf_op jit(solution)/shard_map/ppermute | solution.py:172
  249.2 2.1 collective-permute-done.7
  251.4 1.2 collective-permute-done.9
  252.6 1.7 collective-permute-start.10
  254.3 2.7 collective-permute-done.10
  257.0 1.4 collective-permute-start.11
  258.4 3.9 %collective-permute-done.11 = f32[128,128]{1,0:T(8,128)S(1)} collective-permute-done((f32[128,128]{1,0:T(8,128)S(1)}, f32[128,128]{1,0:T(8,128)S(1)}, u32[]{:S(2)}, u32[]{:S(2)}) %collective-permute-start.11) | collective-permute-done | bytes 65568 | tf_op jit(solution)/shard_map/ppermute | solution.py:172
  262.3 0.3 collective-permute-start.12
  262.6 8.0 %collective-permute-done.12 = f32[128,128]{1,0:T(8,128)S(1)} collective-permute-done((f32[128,128]{1,0:T(8,128)S(1)}, f32[128,128]{1,0:T(8,128)S(1)}, u32[]{:S(2)}, u32[]{:S(2)}) %collective-permute-start.12) | collective-permute-done | bytes 65568 | tf_op jit(solution)/shard_map/ppermute | solution.py:172
  270.7 0.6 gather_fusion.1
  271.3 3.7 %collective-permute-done.13 = f32[128,128]{1,0:T(8,128)S(1)} collective-permute-done((f32[128,128]{1,0:T(8,128)S(1)}, f32[128,128]{1,0:T(8,128)S(1)}, u32[]{:S(2)}, u32[]{:S(2)}) %collective-permute-start.13) | collective-permute-done | bytes 65568 | tf_op jit(solution)/shard_map/ppermute | solution.py:172
  275.0 0.3 collective-permute-start.14
  275.2 0.8 bitcast_select_fusion
  276.1 4.7 %collective-permute-done.14 = f32[128,128]{1,0:T(8,128)S(1)} collective-permute-done((f32[128,128]{1,0:T(8,128)S(1)}, f32[128,128]{1,0:T(8,128)S(1)}, u32[]{:S(2)}, u32[]{:S(2)}) %collective-permute-start.14) | collective-permute-done | bytes 65568 | tf_op jit(solution)/shard_map/ppermute | solution.py:172
  280.8 0.6 add_multiply_fusion
  (59 shorter events, 2.1 us)
Async XLA Ops:
  98.8 8.9 %copy-start.5 = (bf16[128,512]{1,0:T(8,128)(2,1)S(1)}, bf16[128,512]{1,0:T(8,128)(2,1)}, u32[]{:S(2)}) copy-start(bf16[128,512]{1,0:T(8,128)(2,1)} %param.22) | copy-start | bytes 393220
  98.8 9.0 %copy-start.6 = (bf16[512,128]{1,0:T(8,128)(2,1)S(1)}, bf16[512,128]{1,0:T(8,128)(2,1)}, u32[]{:S(2)}) copy-start(bf16[512,128]{1,0:T(8,128)(2,1)} %param.20) | copy-start | bytes 393220
  98.8 9.1 %copy-start.7 = (bf16[512,128]{1,0:T(8,128)(2,1)S(1)}, bf16[512,128]{1,0:T(8,128)(2,1)}, u32[]{:S(2)}) copy-start(bf16[512,128]{1,0:T(8,128)(2,1)} %param.19) | copy-start | bytes 393220
  98.8 9.1 %copy-start.8 = (bf16[512,128]{1,0:T(8,128)(2,1)S(1)}, bf16[512,128]{1,0:T(8,128)(2,1)}, u32[]{:S(2)}) copy-start(bf16[512,128]{1,0:T(8,128)(2,1)} %param.18) | copy-start | bytes 393220
  98.8 10.0 %copy-start.9 = (f32[2]{0:T(128)S(1)}, f32[2]{0:T(128)}, u32[]{:S(2)}) copy-start(f32[2]{0:T(128)} %param.21) | copy-start | bytes 28
  98.8 106.9 %all-to-all-start.1 = ((bf16[256,2,32,128]{3,2,1,0:T(8,128)(2,1)}), bf16[256,2,32,128]{3,2,1,0:T(8,128)(2,1)}, u32[]{:S(2)}, u32[]{:S(2)}) async-start(bf16[256,2,32,128]{3,2,1,0:T(8,128)(2,1)} %bitcast.94), calls=%async_computation.1 | async-start | bytes 8388608 | tf_op jit(solution)/shard_map/all_to_all | solution.py:210
  107.7 51.2 %all-gather.3.cloned.1.call-start = ((), (), s32[]{:S(2)}) async-start(), calls=%async_computation.2 | async-start | bytes 2621440 | tf_op jit(solution)/shard_map/all_gather | solution.py:227
  108.7 52.4 %copy-start.1 = (bf16[512,512]{1,0:T(8,128)(2,1)S(1)}, bf16[512,512]{1,0:T(8,128)(2,1)}, u32[]{:S(2)}) copy-start(bf16[512,512]{1,0:T(8,128)(2,1)} %lat.3) | copy-start | bytes 1572868
  108.8 7.6 %collective-permute-start.2 = (f32[2]{0:T(128)S(1)}, f32[2]{0:T(128)S(1)}, u32[]{:S(2)}, u32[]{:S(2)}) collective-permute-start(f32[2]{0:T(128)S(1)} %copy-done.9), channel_id=1, source_target_pairs={{0,3},{1,2},{2,1},{3,0},{4,7},{5,6},{6,5},{7,4},{8,11},{9,10},{10,... | collective-permute-start | bytes 32 | tf_op jit(solution)/shard_map/ppermute | solution.py:172
  111.6 5.0 %collective-permute-start.1 = (f32[2]{0:T(128)S(1)}, f32[2]{0:T(128)S(1)}, u32[]{:S(2)}, u32[]{:S(2)}) collective-permute-start(f32[2]{0:T(128)S(1)} %copy-done.9), channel_id=1, source_target_pairs={{0,2},{1,3},{2,0},{3,1},{4,6},{5,7},{6,4},{7,5},{8,10},{9,11},{10,... | collective-permute-start | bytes 32 | tf_op jit(solution)/shard_map/ppermute | solution.py:172
  112.4 4.2 %collective-permute-start = (f32[2]{0:T(128)S(1)}, f32[2]{0:T(128)S(1)}, u32[]{:S(2)}, u32[]{:S(2)}) collective-permute-start(f32[2]{0:T(128)S(1)} %copy-done.9), channel_id=1, source_target_pairs={{0,1},{1,0},{2,3},{3,2},{4,5},{5,4},{6,7},{7,6},{8,9},{9,8},{10,11... | collective-permute-start | bytes 32 | tf_op jit(solution)/shard_map/ppermute | solution.py:172
  206.3 2.2 copy-start
  208.5 30.7 %copy-start.2 = (bf16[512,128]{1,0:T(8,128)(2,1)S(1)}, bf16[512,128]{1,0:T(8,128)(2,1)}, u32[]{:S(2)}) copy-start(bf16[512,128]{1,0:T(8,128)(2,1)} %w_inc.1) | copy-start | bytes 393220
  208.5 30.7 %copy-start.3 = (bf16[512,128]{1,0:T(8,128)(2,1)S(1)}, bf16[512,128]{1,0:T(8,128)(2,1)}, u32[]{:S(2)}) copy-start(bf16[512,128]{1,0:T(8,128)(2,1)} %target.1) | copy-start | bytes 393220
  208.5 30.7 %copy-start.4 = (f32[512]{0:T(512)S(1)}, f32[512]{0:T(512)}, u32[]{:S(2)}) copy-start(f32[512]{0:T(512)} %param.23) | copy-start | bytes 6148
  226.1 7.2 %collective-permute-start.3 = (bf16[128,640]{1,0:T(8,128)(2,1)S(1)}, bf16[128,640]{1,0:T(8,128)(2,1)S(1)}, u32[]{:S(2)}, u32[]{:S(2)}) collective-permute-start(bf16[128,640]{1,0:T(8,128)(2,1)S(1)} %get-tuple-element.14), channel_id=1, source_target_pairs={{0,1},{1,0},{2,3},{3,2},{4,5},{5,4},{6,7},{7,6},{8,9},{9,8},{10,11... | collective-permute-start | bytes 491528 | tf_op jit(solution)/shard_map/ppermute | solution.py:172
  226.8 8.9 %collective-permute-start.4 = (bf16[128,640]{1,0:T(8,128)(2,1)S(1)}, bf16[128,640]{1,0:T(8,128)(2,1)S(1)}, u32[]{:S(2)}, u32[]{:S(2)}) collective-permute-start(bf16[128,640]{1,0:T(8,128)(2,1)S(1)} %get-tuple-element.13), channel_id=1, source_target_pairs={{0,2},{1,3},{2,0},{3,1},{4,6},{5,7},{6,4},{7,5},{8,10},{9,11},{10,... | collective-permute-start | bytes 491528 | tf_op jit(solution)/shard_map/ppermute | solution.py:172
  227.9 11.3 %collective-permute-start.5 = (bf16[128,640]{1,0:T(8,128)(2,1)S(1)}, bf16[128,640]{1,0:T(8,128)(2,1)S(1)}, u32[]{:S(2)}, u32[]{:S(2)}) collective-permute-start(bf16[128,640]{1,0:T(8,128)(2,1)S(1)} %get-tuple-element.12), channel_id=1, source_target_pairs={{0,3},{1,2},{2,1},{3,0},{4,7},{5,6},{6,5},{7,4},{8,11},{9,10},{10,... | collective-permute-start | bytes 491528 | tf_op jit(solution)/shard_map/ppermute | solution.py:172
  240.6 8.6 %collective-permute-start.8 = (f32[256,128]{1,0:T(8,128)S(1)}, f32[256,128]{1,0:T(8,128)S(1)}, u32[]{:S(2)}, u32[]{:S(2)}) collective-permute-start(f32[256,128]{1,0:T(8,128)S(1)} %get-tuple-element.17), channel_id=1, source_target_pairs={{0,3},{1,2},{2,1},{3,0},{4,7},{5,6},{6,5},{7,4},{8,11},{9,10},{10,... | collective-permute-start | bytes 393224 | tf_op jit(solution)/shard_map/ppermute | solution.py:172
  243.7 7.6 %collective-permute-start.7 = (f32[256,128]{1,0:T(8,128)S(1)}, f32[256,128]{1,0:T(8,128)S(1)}, u32[]{:S(2)}, u32[]{:S(2)}) collective-permute-start(f32[256,128]{1,0:T(8,128)S(1)} %get-tuple-element.18), channel_id=1, source_target_pairs={{0,2},{1,3},{2,0},{3,1},{4,6},{5,7},{6,4},{7,5},{8,10},{9,11},{10,... | collective-permute-start | bytes 393224 | tf_op jit(solution)/shard_map/ppermute | solution.py:172
  243.7 7.6 %collective-permute-start.6 = (f32[256,128]{1,0:T(8,128)S(1)}, f32[256,128]{1,0:T(8,128)S(1)}, u32[]{:S(2)}, u32[]{:S(2)}) collective-permute-start(f32[256,128]{1,0:T(8,128)S(1)} %get-tuple-element.16), channel_id=1, source_target_pairs={{0,1},{1,0},{2,3},{3,2},{4,5},{5,4},{6,7},{7,6},{8,9},{9,8},{10,11... | collective-permute-start | bytes 393224 | tf_op jit(solution)/shard_map/ppermute | solution.py:172
  251.3 1.3 collective-permute-start.9
  252.6 4.4 %collective-permute-start.10 = (f32[128,128]{1,0:T(8,128)S(1)}, f32[128,128]{1,0:T(8,128)S(1)}, u32[]{:S(2)}, u32[]{:S(2)}) collective-permute-start(f32[128,128]{1,0:T(8,128)S(1)} %add.91), channel_id=1, source_target_pairs={{0,8},{4,12},{8,0},{12,4},{16,24},{20,28},{24,16},{28,20},{32,40},... | collective-permute-start | bytes 196616 | tf_op jit(solution)/shard_map/ppermute | solution.py:172
  257.0 5.3 %collective-permute-start.11 = (f32[128,128]{1,0:T(8,128)S(1)}, f32[128,128]{1,0:T(8,128)S(1)}, u32[]{:S(2)}, u32[]{:S(2)}) collective-permute-start(f32[128,128]{1,0:T(8,128)S(1)} %add.92), channel_id=1, source_target_pairs={{0,16},{4,20},{8,24},{12,28},{16,0},{20,4},{24,8},{28,12},{32,48},... | collective-permute-start | bytes 196616 | tf_op jit(solution)/shard_map/ppermute | solution.py:172
  262.3 8.3 %collective-permute-start.12 = (f32[128,128]{1,0:T(8,128)S(1)}, f32[128,128]{1,0:T(8,128)S(1)}, u32[]{:S(2)}, u32[]{:S(2)}) collective-permute-start(f32[128,128]{1,0:T(8,128)S(1)} %add.93), channel_id=1, source_target_pairs={{0,32},{4,36},{8,40},{12,44},{16,48},{20,52},{24,56},{28,60},{32,0... | collective-permute-start | bytes 196616 | tf_op jit(solution)/shard_map/ppermute | solution.py:172
  270.6 4.4 %collective-permute-start.13 = (f32[128,128]{1,0:T(8,128)S(1)}, f32[128,128]{1,0:T(8,128)S(1)}, u32[]{:S(2)}, u32[]{:S(2)}) collective-permute-start(f32[128,128]{1,0:T(8,128)S(1)} %add.94), channel_id=1, source_target_pairs={{0,64},{4,68},{8,72},{12,76},{16,80},{20,84},{24,88},{28,92},{32,9... | collective-permute-start | bytes 196616 | tf_op jit(solution)/shard_map/ppermute | solution.py:172
  275.0 5.9 %collective-permute-start.14 = (f32[128,128]{1,0:T(8,128)S(1)}, f32[128,128]{1,0:T(8,128)S(1)}, u32[]{:S(2)}, u32[]{:S(2)}) collective-permute-start(f32[128,128]{1,0:T(8,128)S(1)} %add.95), channel_id=1, source_target_pairs={{0,128},{4,132},{8,136},{12,140},{16,144},{20,148},{24,152},{28,15... | collective-permute-start | bytes 196616 | tf_op jit(solution)/shard_map/ppermute | solution.py:172
Sparse Core Ops, SparseCore 0:
  110.3 48.4 all-gather.2

commit v2 on v1

--- a/solution.py
+++ b/solution.py
@@ -14,10 +14,9 @@
 CHUNK = 4
 
 
-def route_kernel(owner, obs, info, payload, marks, counts, sem):
+def route_kernel(owner, obs, payload, counts):
     tiles = payload.shape[0]
     blocks = obs.shape[0]
-    marks[...] = jnp.zeros_like(marks)
 
     def clear(t, carry):
         counts[t] = 0
@@ -29,12 +28,10 @@
         t = owner[b]
         k = jnp.minimum(counts[t], SLOTS - 1)
         counts[t] = k + 1
-        pltpu.make_async_copy(obs.at[b], payload.at[t, :, k], sem).start()
-        marks[t * SLOTS + k] = info[b]
+        payload[t, :, k] = obs[b]
         return carry
 
     lax.fori_loop(0, blocks, send, 0)
-    pltpu.make_async_copy(obs, obs, sem).wait()
 
 
 def split3(v):
@@ -63,12 +60,13 @@
         shade = jnp.full((1, CHUNK * quarter), NEG, F32)
         for u in range(CHUNK):
             place = c * CHUNK + u
-            slot = lists[g, jnp.minimum(place, n - 1)]
+            item = lists[g, jnp.minimum(place, n - 1)]
+            slot, mark = item // (SLOTS * x.shape[0]), item % (SLOTS * x.shape[0])
             s, k = slot // SLOTS, slot % SLOTS
             for i in range(parts):
                 xbuf[u * quarter:(u + 1) * quarter, i * cols:(i + 1) * cols] = x[s, i, k]
             live = (lane_slot == u) & (place < n)
-            shade = jnp.where(live, bias[pl.ds(slot, 1), :], shade)
+            shade = jnp.where(live, bias[pl.ds(mark, 1), :], shade)
         rows_x = xbuf[...]
         scores = lax.dot_general(
             queries, rows_x, (((1,), (1,)), ((), ())), preferred_element_type=F32
@@ -174,39 +172,21 @@
     def pick(v, which):
         return lax.dynamic_index_in_dim(v, which, 0, keepdims=False)
 
-    valid = lax.dynamic_index_in_dim(
-        row_valid.reshape(blocks, groups, quarter), me, 1, keepdims=False
-    )
-    info = jnp.stack(
-        [
-            jnp.tile(valid, (1, 128 // quarter)),
-            jnp.pad(block_pattern, ((0, 0), (0, 128 - subs))),
-        ],
-        axis=1,
-    ).astype(F32)
-    payload, marks = pl.pallas_call(
+    tile = lax.axis_index("tile")
+    whole = lambda *shape: pl.BlockSpec(shape, lambda g, *_: (0,) * len(shape))
+    payload = pl.pallas_call(
         route_kernel,
         grid_spec=pltpu.PrefetchScalarGridSpec(
             num_scalar_prefetch=1,
             grid=(1,),
-            in_specs=[
-                pl.BlockSpec(memory_space=pl.ANY),
-                pl.BlockSpec((blocks, 2, 128), lambda i, o: (0, 0, 0)),
-            ],
-            out_specs=[
-                pl.BlockSpec(memory_space=pl.ANY),
-                pl.BlockSpec((slots, 2, 128), lambda i, o: (0, 0, 0)),
-            ],
-            scratch_shapes=[pltpu.SMEM((tiles,), jnp.int32), pltpu.SemaphoreType.DMA],
+            in_specs=[whole(blocks, groups, quarter, cols)],
+            out_specs=whole(tiles, groups, SLOTS, quarter, cols),
+            scratch_shapes=[pltpu.SMEM((tiles,), jnp.int32)],
         ),
-        out_shape=[
-            jax.ShapeDtypeStruct((tiles, groups, SLOTS, quarter, cols), BF),
-            jax.ShapeDtypeStruct((slots, 2, 128), F32),
-        ],
+        out_shape=jax.ShapeDtypeStruct((tiles, groups, SLOTS, quarter, cols), BF),
+        compiler_params=pltpu.CompilerParams(vmem_limit_bytes=32 * 1024 * 1024),
         name="route",
-    )(block_owner[:, 0], obs_feat.reshape(blocks, groups, quarter, cols), info)
-
-    marks = lax.all_to_all(marks, "tile", split_axis=0, concat_axis=0, tiled=True)
+    )(block_owner[:, 0], obs_feat.reshape(blocks, groups, quarter, cols))
     arrived = lax.all_to_all(
         payload.reshape(tiles * groups, SLOTS, quarter, cols),
         ("tile", "head"),
@@ -215,14 +195,34 @@
         tiled=True,
     ).reshape(tiles, groups, SLOTS, quarter, cols)
 
-    bias = (marks[:, 0, :] - 1.0) * (-NEG)
-    live = (marks[:, 1, :subs] > 0.5).T
+    valid = pick(row_valid.reshape(blocks, groups, quarter).transpose(1, 0, 2), me)
+    marks = jnp.concatenate([valid, block_pattern, block_owner], axis=1).astype(BF)
+    marks = jnp.pad(marks, ((0, 0), (0, 64 - marks.shape[1])))[None]
+    source = jnp.zeros((1,), jnp.int32) + tile
+    for mask in (8, 4, 2, 32, 16, 1):
+        marks = jnp.concatenate([marks, swap(marks, "tile", mask, tiles)], axis=0)
+        source = jnp.concatenate([source, source ^ mask])
+    mine = marks[:, :, quarter + subs] == tile.astype(BF)
+    earlier = jnp.triu(jnp.ones((blocks, blocks), BF), 1)
+    rank = jnp.einsum("eb,bc->ec", mine.astype(BF), earlier, preferred_element_type=F32)
+    chosen = mine[:, None, :] & (
+        rank[:, None, :] == jnp.arange(SLOTS, dtype=F32)[None, :, None]
+    )
+    marks = jnp.einsum(
+        "ekb,ebc->ekc", chosen.astype(BF), marks, preferred_element_type=F32
+    ).reshape(slots, 64)
+
+    bias = jnp.tile((marks[:, :quarter] - 1.0) * (-NEG), (1, 128 // quarter))
+    live = (marks[:, quarter:quarter + subs] > 0.5).T
     before = jnp.triu(jnp.ones((slots, slots), BF), 1)
     place = jnp.dot(live.astype(BF), before, preferred_element_type=F32).astype(jnp.int32)
     counts = jnp.sum(live.astype(jnp.int32), axis=1)
     order = jnp.arange(slots, dtype=jnp.int32)
+    entry = (source[:, None] * SLOTS + jnp.arange(SLOTS, dtype=jnp.int32)).reshape(slots)
     hit = live[:, None, :] & (place[:, None, :] == order[None, :, None])
-    lists = jnp.sum(jnp.where(hit, order[None, None, :], 0), axis=2)
+    lists = jnp.sum(
+        jnp.where(hit, (entry * slots + order)[None, None, :], 0), axis=2
+    )
 
     stacked = lax.all_gather(
         jnp.concatenate([w_query, w_key, w_value, w_out.T], axis=1), "head", axis=0
@@ -254,7 +254,6 @@
     )
     own = jnp.broadcast_to(own[:, :, None], (heads, lat_rows, 128))
 
-    whole = lambda *shape: pl.BlockSpec(shape, lambda g, *_: (0,) * len(shape))
     partial = pl.pallas_call(
         attend_kernel,
         grid_spec=pltpu.PrefetchScalarGridSpec(
@@ -314,17 +313,16 @@
         w_inc,
         target,
     )
-    pieces = [pick(packed, me)] + [
-        swap(pick(packed, me ^ d), "head", d, groups) for d in range(1, groups)
+    grads = [pick(packed, me)[:128]] + [
+        swap(pick(packed, me ^ d)[:128], "head", d, groups) for d in range(1, groups)
     ]
-    grads = [p[:128] for p in pieces]
     grad = (grads[0] + grads[1]) + (grads[2] + grads[3])
-    stacked_pred = jnp.stack([p[128:] for p in pieces])
-    predicted = jnp.take(
-        stacked_pred, jnp.arange(groups, dtype=jnp.int32) ^ me, axis=0
-    ).reshape(lat_rows, 128)
-    for mask in (1, 2, 4, 8, 16, 32):
-        grad = grad + swap(grad, "tile", mask, tiles)
+    for low, high in ((1, 2), (4, 8), (16, 32)):
+        a, b, c = (swap(grad, "tile", m, tiles) for m in (low, high, low + high))
+        grad = (grad + a) + (b + c)
+    mine = packed[0, 128:]
+    preds = jnp.stack([mine] + [swap(mine, "head", d, groups) for d in range(1, groups)])
+    predicted = jnp.take(preds, turn, axis=0).reshape(lat_rows, 128)
     return predicted, grad * (1.0 / math.sqrt(lat_rows * tiles))
 
 

time: 291 us -> 241 us (0.83); the launches traced: 288 us -> 242 us
  Pallas kernels: 86 us -> 21.9 us
  starting transfers between devices: 26 us -> 62.5 us
  blocking collectives: 21.8 us -> 0 us
  local copies, waits for them, and re-layouts: 8.81 us -> 12.5 us
  waiting for transfers between devices: 123 us -> 120 us
    ppermute x15 -> x27, waiting for transfers between devices: 42.2 us -> 120 us  [swap(): return lax.ppermute(v, axis, [(d, d ^ mask) for d in range(size)])]
    pallas_call x1, Pallas kernels: 67.2 us -> 1.75 us  [body(): pl.pallas_call(route_kernel, grid_spec=pltpu.PrefetchScalarGridSpec(num_s...]
    all_gather x1, waiting for transfers between devices: 40.7 us -> 0.02 us  [body(): lax.all_gather(jnp.concatenate([w_query, w_key, w_value, w_out.T], axis=1...]
    all_to_all x1, waiting for transfers between devices: 40.3 us -> 0.01 us  [body(): lax.all_to_all(payload.reshape(tiles * groups, SLOTS, quarter, cols), ('t...]
    ppermute x15 -> x27, starting transfers between devices: 17.1 us -> 47.1 us  [swap(): return lax.ppermute(v, axis, [(d, d ^ mask) for d in range(size)])]
    all_to_all x1 -> x0, blocking collectives: 21.8 us -> none  [body(): lax.all_to_all(marks, 'tile', split_axis=0, concat_axis=0, tiled=True)]
    all_to_all x1, starting transfers between devices: 8.83 us -> 15.4 us  [body(): lax.all_to_all(payload.reshape(tiles * groups, SLOTS, quarter, cols), ('t...]
    unnamed x23 -> x39, local copies, waits for them, and re-layouts: 3.17 us -> 6.9 us
  transfers between devices with their start and end apart: 17 -> 29, of which waited for: 15 -> 15; matrix products, arithmetic and copies ran while one was open for 4% -> 6% of each run, Pallas kernels for 0% -> 0%
where the time goes in v2:
time: 241 us; the launch traced here: 242 us
  waiting for transfers between devices  120 us (50%)
  starting transfers between devices  62.5 us (26%)
  Pallas kernels  21.9 us (9%)
  between operations  14.5 us (6%)
  local copies, waits for them, and re-layouts  12.5 us (5%)
  other arithmetic  5.05 us (2%)
  matrix products  4.97 us (2%)
    ppermute x27, waiting for transfers between devices, swap(): return lax.ppermute(v, axis, [(d, d ^ mask) for d in range(size)])  120 us
    ppermute x27, starting transfers between devices, swap(): return lax.ppermute(v, axis, [(d, d ^ mask) for d in range(size)])  47.1 us
    pallas_call x1, Pallas kernels, body(): pl.pallas_call(attend_kernel, grid_spec=pltpu.PrefetchScalarGridSpec(num_...  18.9 us
    all_to_all x1, starting transfers between devices, body(): lax.all_to_all(payload.reshape(tiles * groups, SLOTS, quarter, cols), ('t...  15.4 us
    unnamed x39, local copies, waits for them, and re-layouts  6.9 us
  transfers between devices with their start and end apart: 29, of which 15 were waited for; matrix products, arithmetic and copies ran while one was open for 6% of the time, Pallas kernels for 0%

profile of v2, /device:TPU:32, one launch (start us, length us, event | category | flops | bytes accessed | tf_op | source)
XLA Modules:
  0.0 241.7 jit_solution(307003997998392564)
XLA Ops:
  7.2 1.6 copy-done.3
  8.8 0.7 copy-done.7
  9.4 1.7 route.1
  11.2 2.0 copy-done
  13.3 15.4 %all-to-all-start = ((bf16[256,2,32,128]{3,2,1,0:T(8,128)(2,1)}), bf16[256,2,32,128]{3,2,1,0:T(8,128)(2,1)}, u32[]{:S(2)}, u32[]{:S(2)}) async-start(bf16[256,2,32,128]{3,2,1,0:T(8,128)(2,1)} %bitcast.94), calls=%async_computation | async-start | bytes 8388608 | tf_op jit(solution)/shard_map/all_to_all | solution.py:190
  28.7 2.8 %collective-permute-start.8 = (f32[2]{0:T(128)S(1)}, f32[2]{0:T(128)S(1)}, u32[]{:S(2)}, u32[]{:S(2)}) collective-permute-start(f32[2]{0:T(128)S(1)} %copy-done.15), channel_id=1, source_target_pairs={{0,3},{1,2},{2,1},{3,0},{4,7},{5,6},{6,5},{7,4},{8,11},{9,10},{10,... | collective-permute-start | bytes 32 | tf_op jit(solution)/shard_map/ppermute | solution.py:170
  31.5 0.8 collective-permute-start.7
  32.3 0.5 collective-permute-start.6
  33.4 5.6 %collective-permute-start = (bf16[1,64,64]{2,1,0:T(8,128)(2,1)S(1)}, bf16[1,64,64]{2,1,0:T(8,128)(2,1)S(1)}, u32[]{:S(2)}, u32[]{:S(2)}) collective-permute-start(bf16[1,64,64]{2,1,0:T(8,128)(2,1)S(1)} %get-tuple-element.5), channel_id=1, source_target_pairs={{0,32},{4,36},{8,40},{12,44},{16,48},{20,52},{24,56},{28,60},{32,0... | collective-permute-start | bytes 24584 | tf_op jit(solution)/shard_map/ppermute | solution.py:170
  39.2 0.9 pad_maximum_fusion
  40.9 82.3 %collective-permute-done = bf16[1,64,64]{2,1,0:T(8,128)(2,1)S(1)} collective-permute-done((bf16[1,64,64]{2,1,0:T(8,128)(2,1)S(1)}, bf16[1,64,64]{2,1,0:T(8,128)(2,1)S(1)}, u32[]{:S(2)}, u32[]{:S(2)}) %collective-permute-start) | collective-permute-done | bytes 8224 | tf_op jit(solution)/shard_map/ppermute | solution.py:170
  123.3 4.9 %collective-permute-done.1 = bf16[2,64,64]{2,1,0:T(8,128)(2,1)S(1)} collective-permute-done((bf16[2,64,64]{2,1,0:T(8,128)(2,1)S(1)}, bf16[2,64,64]{2,1,0:T(8,128)(2,1)S(1)}, u32[]{:S(2)}, u32[]{:S(2)}) %collective-permute-start.1) | collective-permute-done | bytes 16416 | tf_op jit(solution)/shard_map/ppermute | solution.py:170
  128.1 1.2 collective-permute-start.2
  129.4 3.1 %collective-permute-done.2 = bf16[4,64,64]{2,1,0:T(8,128)(2,1)S(1)} collective-permute-done((bf16[4,64,64]{2,1,0:T(8,128)(2,1)S(1)}, bf16[4,64,64]{2,1,0:T(8,128)(2,1)S(1)}, u32[]{:S(2)}, u32[]{:S(2)}) %collective-permute-start.2) | collective-permute-done | bytes 32800 | tf_op jit(solution)/shard_map/ppermute | solution.py:170
  132.5 3.2 %collective-permute-start.3 = (bf16[8,64,64]{2,1,0:T(8,128)(2,1)S(1)}, bf16[8,64,64]{2,1,0:T(8,128)(2,1)S(1)}, u32[]{:S(2)}, u32[]{:S(2)}) collective-permute-start(bf16[8,64,64]{2,1,0:T(8,128)(2,1)S(1)} %pad_maximum_fusion.2), channel_id=1, source_target_pairs={{0,128},{4,132},{8,136},{12,140},{16,144},{20,148},{24,152},{28,15... | collective-permute-start | bytes 196616 | tf_op jit(solution)/shard_map/ppermute | solution.py:170
  135.8 3.4 %collective-permute-done.3 = bf16[8,64,64]{2,1,0:T(8,128)(2,1)S(1)} collective-permute-done((bf16[8,64,64]{2,1,0:T(8,128)(2,1)S(1)}, bf16[8,64,64]{2,1,0:T(8,128)(2,1)S(1)}, u32[]{:S(2)}, u32[]{:S(2)}) %collective-permute-start.3) | collective-permute-done | bytes 65568 | tf_op jit(solution)/shard_map/ppermute | solution.py:170
  139.3 1.6 collective-permute-start.4
  140.8 4.9 %collective-permute-done.4 = bf16[16,64,64]{2,1,0:T(8,128)(2,1)S(1)} collective-permute-done((bf16[16,64,64]{2,1,0:T(8,128)(2,1)S(1)}, bf16[16,64,64]{2,1,0:T(8,128)(2,1)S(1)}, u32[]{:S(2)}, u32[]{:S(2)}) %collective-permute-start.4) | collective-permute-done | bytes 131104 | tf_op jit(solution)/shard_map/ppermute | solution.py:170
  146.2 0.6 gather_fusion
  146.9 1.1 collective-permute-done.5
  148.1 1.5 compare_reduce_fusion
  151.1 1.7 slice_bitcast_fusion
  154.4 3.3 %multiply_convert_fusion.qw = bf16[8,512,512]{2,1,0:T(8,128)(2,1)} fusion(bf16[512,8,64]{0,2,1:T(8,128)(2,1)S(1)} %bitcast.101, bf16[512,8,64]{0,2,1:T(8,128)(2,1)S(1)} %bitcast.103), kind=kOutput, calls=%fused_computation.2 | convolution fusion | flops 272629760 | bytes 5242880 | tf_op jit(solution)/shard_map/lhd,khd->hlk/dot_general | solution.py:246
  157.7 0.6 broadcast_in_dim.89.own
  158.3 2.2 copy-done.1
  160.5 18.9 %attend.1 = bf16[512,640]{1,0:T(8,128)(2,1)S(1)} custom-call(s32[16]{0:T(128)S(1)} %get-tuple-element.2.counts, s32[16,128]{1,0:T(8,128)S(1)} %select_reduce_fusion.lists, s32[1]{0:T(128)} %bitcast.7.first, bf16[64,4,2,32,128]{4,3,2,1,0:T(8,128)(2,1)} %bitcast.11.x, f32[128,128]{1,0:T(8,128)S(1)} %copy.90.bias, bf16[8,512,512]{2,1,0:T(8,128)(2,1)S(1)} %copy-done.1, ...), custom_call_target="tpu_custom_call" | custom-call | tf_op jit(solution)/shard_map/attend/pallas_call | solution.py:257
  179.5 1.8 collective-permute-start.9
  181.3 2.7 %collective-permute-start.10 = (bf16[128,640]{1,0:T(8,128)(2,1)S(1)}, bf16[128,640]{1,0:T(8,128)(2,1)S(1)}, u32[]{:S(2)}, u32[]{:S(2)}) collective-permute-start(bf16[128,640]{1,0:T(8,128)(2,1)S(1)} %get-tuple-element.11), channel_id=1, source_target_pairs={{0,2},{1,3},{2,0},{3,1},{4,6},{5,7},{6,4},{7,5},{8,10},{9,11},{10,... | collective-permute-start | bytes 491528 | tf_op jit(solution)/shard_map/ppermute | solution.py:170
  184.5 0.5 collective-permute-done.9.r1
  185.0 6.0 %collective-permute-done.10.r2 = bf16[128,640]{1,0:T(8,128)(2,1)S(1)} collective-permute-done((bf16[128,640]{1,0:T(8,128)(2,1)S(1)}, bf16[128,640]{1,0:T(8,128)(2,1)S(1)}, u32[]{:S(2)}, u32[]{:S(2)}) %collective-permute-start.10) | collective-permute-done | bytes 163872 | tf_op jit(solution)/shard_map/ppermute | solution.py:170
  191.0 3.6 %collective-permute-done.11.r3 = bf16[128,640]{1,0:T(8,128)(2,1)S(1)} collective-permute-done((bf16[128,640]{1,0:T(8,128)(2,1)S(1)}, bf16[128,640]{1,0:T(8,128)(2,1)S(1)}, u32[]{:S(2)}, u32[]{:S(2)}) %collective-permute-start.11) | collective-permute-done | bytes 163872 | tf_op jit(solution)/shard_map/ppermute | solution.py:170
  194.6 1.3 finish.1
  196.0 2.1 collective-permute-start.16
  198.1 2.6 %collective-permute-start.17 = (f32[128,128]{1,0:T(8,128)S(1)}, f32[128,128]{1,0:T(8,128)S(1)}, u32[]{:S(2)}, u32[]{:S(2)}) collective-permute-start(f32[128,128]{1,0:T(8,128)S(1)} %get-tuple-element.14), channel_id=1, source_target_pairs={{0,3},{1,2},{2,1},{3,0},{4,7},{5,6},{6,5},{7,4},{8,11},{9,10},{10,... | collective-permute-start | bytes 196616 | tf_op jit(solution)/shard_map/ppermute | solution.py:170
  200.9 1.0 collective-permute-done.16
  202.0 1.6 collective-permute-done.17
  203.9 1.9 collective-permute-start.18
  205.9 2.6 %collective-permute-start.14 = (f32[128,128]{1,0:T(8,128)S(1)}, f32[128,128]{1,0:T(8,128)S(1)}, u32[]{:S(2)}, u32[]{:S(2)}) collective-permute-start(f32[128,128]{1,0:T(8,128)S(1)} %get-tuple-element.15), channel_id=1, source_target_pairs={{0,3},{1,2},{2,1},{3,0},{4,7},{5,6},{6,5},{7,4},{8,11},{9,10},{10,... | collective-permute-start | bytes 196616 | tf_op jit(solution)/shard_map/ppermute | solution.py:170
  208.5 1.5 collective-permute-start.12
  210.2 2.5 %collective-permute-start.23 = (f32[128,128]{1,0:T(8,128)S(1)}, f32[128,128]{1,0:T(8,128)S(1)}, u32[]{:S(2)}, u32[]{:S(2)}) collective-permute-start(f32[128,128]{1,0:T(8,128)S(1)} %add_add_fusion.1), channel_id=1, source_target_pairs={{0,48},{4,52},{8,56},{12,60},{16,32},{20,36},{24,40},{28,44},{32,1... | collective-permute-start | bytes 196616 | tf_op jit(solution)/shard_map/ppermute | solution.py:170
  212.6 4.0 %collective-permute-start.21 = (f32[128,128]{1,0:T(8,128)S(1)}, f32[128,128]{1,0:T(8,128)S(1)}, u32[]{:S(2)}, u32[]{:S(2)}) collective-permute-start(f32[128,128]{1,0:T(8,128)S(1)} %add_add_fusion.1), channel_id=1, source_target_pairs={{0,16},{4,20},{8,24},{12,28},{16,0},{20,4},{24,8},{28,12},{32,48},... | collective-permute-start | bytes 196616 | tf_op jit(solution)/shard_map/ppermute | solution.py:170
  216.7 0.6 gather_fusion.1
  217.2 3.0 %collective-permute-done.22 = f32[128,128]{1,0:T(8,128)S(1)} collective-permute-done((f32[128,128]{1,0:T(8,128)S(1)}, f32[128,128]{1,0:T(8,128)S(1)}, u32[]{:S(2)}, u32[]{:S(2)}) %collective-permute-start.22) | collective-permute-done | bytes 65568 | tf_op jit(solution)/shard_map/ppermute | solution.py:170
  220.3 8.4 %collective-permute-start.25 = (f32[128,128]{1,0:T(8,128)S(1)}, f32[128,128]{1,0:T(8,128)S(1)}, u32[]{:S(2)}, u32[]{:S(2)}) collective-permute-start(f32[128,128]{1,0:T(8,128)S(1)} %add_add_fusion), channel_id=1, source_target_pairs={{0,128},{4,132},{8,136},{12,140},{16,144},{20,148},{24,152},{28,15... | collective-permute-start | bytes 196616 | tf_op jit(solution)/shard_map/ppermute | solution.py:170
  228.8 0.8 bitcast_select_fusion
  229.6 1.5 collective-permute-done.25
  231.1 3.1 %collective-permute-done.26 = f32[128,128]{1,0:T(8,128)S(1)} collective-permute-done((f32[128,128]{1,0:T(8,128)S(1)}, f32[128,128]{1,0:T(8,128)S(1)}, u32[]{:S(2)}, u32[]{:S(2)}) %collective-permute-start.26) | collective-permute-done | bytes 65568 | tf_op jit(solution)/shard_map/ppermute | solution.py:170
  234.2 0.7 add_multiply_fusion
  (116 shorter events, 7.0 us)
Async XLA Ops:
  7.2 1.6 copy-start.3
  8.8 0.7 copy-start.7
  11.2 2.0 copy-start
  13.2 15.5 %copy-start.15 = (f32[2]{0:T(128)S(1)}, f32[2]{0:T(128)}, u32[]{:S(2)}) copy-start(f32[2]{0:T(128)} %param.21) | copy-start | bytes 28
  13.2 19.7 %copy-start.8 = (s32[64,1]{0,1:T(1,128)S(1)}, s32[64,1]{0,1:T(1,128)}, u32[]{:S(2)}) copy-start(s32[64,1]{0,1:T(1,128)} %param.15) | copy-start | bytes 772
  13.2 19.8 %copy-start.14 = (s32[64,16]{0,1:T(8,128)S(1)}, s32[64,16]{0,1:T(8,128)}, u32[]{:S(2)}) copy-start(s32[64,16]{0,1:T(8,128)} %param.16) | copy-start | bytes 12292
  13.2 19.9 %copy-start.13 = (s32[8192]{0:T(1024)S(1)}, s32[8192]{0:T(1024)}, u32[]{:S(2)}) copy-start(s32[8192]{0:T(1024)} %param.14) | copy-start | bytes 98308
  13.2 25.8 %copy-start.9 = (bf16[128,512]{1,0:T(8,128)(2,1)S(1)}, bf16[128,512]{1,0:T(8,128)(2,1)}, u32[]{:S(2)}) copy-start(bf16[128,512]{1,0:T(8,128)(2,1)} %param.22) | copy-start | bytes 393220
  13.2 25.9 %copy-start.10 = (bf16[512,128]{1,0:T(8,128)(2,1)S(1)}, bf16[512,128]{1,0:T(8,128)(2,1)}, u32[]{:S(2)}) copy-start(bf16[512,128]{1,0:T(8,128)(2,1)} %param.20) | copy-start | bytes 393220
  13.2 25.9 %copy-start.11 = (bf16[512,128]{1,0:T(8,128)(2,1)S(1)}, bf16[512,128]{1,0:T(8,128)(2,1)}, u32[]{:S(2)}) copy-start(bf16[512,128]{1,0:T(8,128)(2,1)} %param.19) | copy-start | bytes 393220
  13.2 25.9 %copy-start.12 = (bf16[512,128]{1,0:T(8,128)(2,1)S(1)}, bf16[512,128]{1,0:T(8,128)(2,1)}, u32[]{:S(2)}) copy-start(bf16[512,128]{1,0:T(8,128)(2,1)} %param.18) | copy-start | bytes 393220
  13.3 144.5 %all-to-all-start = ((bf16[256,2,32,128]{3,2,1,0:T(8,128)(2,1)}), bf16[256,2,32,128]{3,2,1,0:T(8,128)(2,1)}, u32[]{:S(2)}, u32[]{:S(2)}) async-start(bf16[256,2,32,128]{3,2,1,0:T(8,128)(2,1)} %bitcast.94), calls=%async_computation | async-start | bytes 8388608 | tf_op jit(solution)/shard_map/all_to_all | solution.py:190
  28.7 122.4 %all-gather.3.cloned.1.call-start = ((), (), s32[]{:S(2)}) async-start(), calls=%async_computation.1 | async-start | bytes 2621440 | tf_op jit(solution)/shard_map/all_gather | solution.py:227
  28.7 117.4 %collective-permute-start.8 = (f32[2]{0:T(128)S(1)}, f32[2]{0:T(128)S(1)}, u32[]{:S(2)}, u32[]{:S(2)}) collective-permute-start(f32[2]{0:T(128)S(1)} %copy-done.15), channel_id=1, source_target_pairs={{0,3},{1,2},{2,1},{3,0},{4,7},{5,6},{6,5},{7,4},{8,11},{9,10},{10,... | collective-permute-start | bytes 32 | tf_op jit(solution)/shard_map/ppermute | solution.py:170
  31.5 114.6 %collective-permute-start.7 = (f32[2]{0:T(128)S(1)}, f32[2]{0:T(128)S(1)}, u32[]{:S(2)}, u32[]{:S(2)}) collective-permute-start(f32[2]{0:T(128)S(1)} %copy-done.15), channel_id=1, source_target_pairs={{0,2},{1,3},{2,0},{3,1},{4,6},{5,7},{6,4},{7,5},{8,10},{9,11},{10,... | collective-permute-start | bytes 32 | tf_op jit(solution)/shard_map/ppermute | solution.py:170
  32.3 113.8 %collective-permute-start.6 = (f32[2]{0:T(128)S(1)}, f32[2]{0:T(128)S(1)}, u32[]{:S(2)}, u32[]{:S(2)}) collective-permute-start(f32[2]{0:T(128)S(1)} %copy-done.15), channel_id=1, source_target_pairs={{0,1},{1,0},{2,3},{3,2},{4,5},{5,4},{6,7},{7,6},{8,9},{9,8},{10,11... | collective-permute-start | bytes 32 | tf_op jit(solution)/shard_map/ppermute | solution.py:170
  33.4 89.7 %collective-permute-start = (bf16[1,64,64]{2,1,0:T(8,128)(2,1)S(1)}, bf16[1,64,64]{2,1,0:T(8,128)(2,1)S(1)}, u32[]{:S(2)}, u32[]{:S(2)}) collective-permute-start(bf16[1,64,64]{2,1,0:T(8,128)(2,1)S(1)} %get-tuple-element.5), channel_id=1, source_target_pairs={{0,32},{4,36},{8,40},{12,44},{16,48},{20,52},{24,56},{28,60},{32,0... | collective-permute-start | bytes 24584 | tf_op jit(solution)/shard_map/ppermute | solution.py:170
  123.1 5.0 %collective-permute-start.1 = (bf16[2,64,64]{2,1,0:T(8,128)(2,1)S(1)}, bf16[2,64,64]{2,1,0:T(8,128)(2,1)S(1)}, u32[]{:S(2)}, u32[]{:S(2)}) collective-permute-start(bf16[2,64,64]{2,1,0:T(8,128)(2,1)S(1)} %pad_maximum_fusion.4), channel_id=1, source_target_pairs={{0,16},{4,20},{8,24},{12,28},{16,0},{20,4},{24,8},{28,12},{32,48},... | collective-permute-start | bytes 49160 | tf_op jit(solution)/shard_map/ppermute | solution.py:170
  128.1 4.4 %collective-permute-start.2 = (bf16[4,64,64]{2,1,0:T(8,128)(2,1)S(1)}, bf16[4,64,64]{2,1,0:T(8,128)(2,1)S(1)}, u32[]{:S(2)}, u32[]{:S(2)}) collective-permute-start(bf16[4,64,64]{2,1,0:T(8,128)(2,1)S(1)} %pad_maximum_fusion.3), channel_id=1, source_target_pairs={{0,8},{4,12},{8,0},{12,4},{16,24},{20,28},{24,16},{28,20},{32,40},... | collective-permute-start | bytes 98312 | tf_op jit(solution)/shard_map/ppermute | solution.py:170
  132.5 6.6 %collective-permute-start.3 = (bf16[8,64,64]{2,1,0:T(8,128)(2,1)S(1)}, bf16[8,64,64]{2,1,0:T(8,128)(2,1)S(1)}, u32[]{:S(2)}, u32[]{:S(2)}) collective-permute-start(bf16[8,64,64]{2,1,0:T(8,128)(2,1)S(1)} %pad_maximum_fusion.2), channel_id=1, source_target_pairs={{0,128},{4,132},{8,136},{12,140},{16,144},{20,148},{24,152},{28,15... | collective-permute-start | bytes 196616 | tf_op jit(solution)/shard_map/ppermute | solution.py:170
  139.3 6.5 %collective-permute-start.4 = (bf16[16,64,64]{2,1,0:T(8,128)(2,1)S(1)}, bf16[16,64,64]{2,1,0:T(8,128)(2,1)S(1)}, u32[]{:S(2)}, u32[]{:S(2)}) collective-permute-start(bf16[16,64,64]{2,1,0:T(8,128)(2,1)S(1)} %get-tuple-element.23), channel_id=1, source_target_pairs={{0,64},{4,68},{8,72},{12,76},{16,80},{20,84},{24,88},{28,92},{32,9... | collective-permute-start | bytes 393224 | tf_op jit(solution)/shard_map/ppermute | solution.py:170
  145.9 2.2 collective-permute-start.5
  150.1 3.3 %copy-start.2 = (bf16[512,512]{1,0:T(8,128)(2,1)S(1)}, bf16[512,512]{1,0:T(8,128)(2,1)}, u32[]{:S(2)}) copy-start(bf16[512,512]{1,0:T(8,128)(2,1)} %lat.3) | copy-start | bytes 1572868
  158.3 2.2 copy-start.1
  160.5 34.1 %copy-start.4 = (bf16[512,128]{1,0:T(8,128)(2,1)S(1)}, bf16[512,128]{1,0:T(8,128)(2,1)}, u32[]{:S(2)}) copy-start(bf16[512,128]{1,0:T(8,128)(2,1)} %w_inc.1) | copy-start | bytes 393220
  160.5 34.1 %copy-start.5 = (bf16[512,128]{1,0:T(8,128)(2,1)S(1)}, bf16[512,128]{1,0:T(8,128)(2,1)}, u32[]{:S(2)}) copy-start(bf16[512,128]{1,0:T(8,128)(2,1)} %target.1) | copy-start | bytes 393220
  160.5 34.1 %copy-start.6 = (f32[512]{0:T(512)S(1)}, f32[512]{0:T(512)}, u32[]{:S(2)}) copy-start(f32[512]{0:T(512)} %param.23) | copy-start | bytes 6148
  179.5 5.5 %collective-permute-start.9 = (bf16[128,640]{1,0:T(8,128)(2,1)S(1)}, bf16[128,640]{1,0:T(8,128)(2,1)S(1)}, u32[]{:S(2)}, u32[]{:S(2)}) collective-permute-start(bf16[128,640]{1,0:T(8,128)(2,1)S(1)} %get-tuple-element.12), channel_id=1, source_target_pairs={{0,1},{1,0},{2,3},{3,2},{4,5},{5,4},{6,7},{7,6},{8,9},{9,8},{10,11... | collective-permute-start | bytes 491528 | tf_op jit(solution)/shard_map/ppermute | solution.py:170
  181.3 9.7 %collective-permute-start.10 = (bf16[128,640]{1,0:T(8,128)(2,1)S(1)}, bf16[128,640]{1,0:T(8,128)(2,1)S(1)}, u32[]{:S(2)}, u32[]{:S(2)}) collective-permute-start(bf16[128,640]{1,0:T(8,128)(2,1)S(1)} %get-tuple-element.11), channel_id=1, source_target_pairs={{0,2},{1,3},{2,0},{3,1},{4,6},{5,7},{6,4},{7,5},{8,10},{9,11},{10,... | collective-permute-start | bytes 491528 | tf_op jit(solution)/shard_map/ppermute | solution.py:170
  184.0 10.6 %collective-permute-start.11 = (bf16[128,640]{1,0:T(8,128)(2,1)S(1)}, bf16[128,640]{1,0:T(8,128)(2,1)S(1)}, u32[]{:S(2)}, u32[]{:S(2)}) collective-permute-start(bf16[128,640]{1,0:T(8,128)(2,1)S(1)} %get-tuple-element.10), channel_id=1, source_target_pairs={{0,3},{1,2},{2,1},{3,0},{4,7},{5,6},{6,5},{7,4},{8,11},{9,10},{10,... | collective-permute-start | bytes 491528 | tf_op jit(solution)/shard_map/ppermute | solution.py:170
  195.9 5.0 %collective-permute-start.15 = (f32[128,128]{1,0:T(8,128)S(1)}, f32[128,128]{1,0:T(8,128)S(1)}, u32[]{:S(2)}, u32[]{:S(2)}) collective-permute-start(f32[128,128]{1,0:T(8,128)S(1)} %get-tuple-element.17), channel_id=1, source_target_pairs={{0,1},{1,0},{2,3},{3,2},{4,5},{5,4},{6,7},{7,6},{8,9},{9,8},{10,11... | collective-permute-start | bytes 196616 | tf_op jit(solution)/shard_map/ppermute | solution.py:170
  196.0 5.9 %collective-permute-start.16 = (f32[128,128]{1,0:T(8,128)S(1)}, f32[128,128]{1,0:T(8,128)S(1)}, u32[]{:S(2)}, u32[]{:S(2)}) collective-permute-start(f32[128,128]{1,0:T(8,128)S(1)} %get-tuple-element.16), channel_id=1, source_target_pairs={{0,2},{1,3},{2,0},{3,1},{4,6},{5,7},{6,4},{7,5},{8,10},{9,11},{10,... | collective-permute-start | bytes 196616 | tf_op jit(solution)/shard_map/ppermute | solution.py:170
  198.1 5.5 %collective-permute-start.17 = (f32[128,128]{1,0:T(8,128)S(1)}, f32[128,128]{1,0:T(8,128)S(1)}, u32[]{:S(2)}, u32[]{:S(2)}) collective-permute-start(f32[128,128]{1,0:T(8,128)S(1)} %get-tuple-element.14), channel_id=1, source_target_pairs={{0,3},{1,2},{2,1},{3,0},{4,7},{5,6},{6,5},{7,4},{8,11},{9,10},{10,... | collective-permute-start | bytes 196616 | tf_op jit(solution)/shard_map/ppermute | solution.py:170
  203.6 4.9 %collective-permute-start.19 = (f32[128,128]{1,0:T(8,128)S(1)}, f32[128,128]{1,0:T(8,128)S(1)}, u32[]{:S(2)}, u32[]{:S(2)}) collective-permute-start(f32[128,128]{1,0:T(8,128)S(1)} %fusion.6), channel_id=1, source_target_pairs={{0,8},{4,12},{8,0},{12,4},{16,24},{20,28},{24,16},{28,20},{32,40},... | collective-permute-start | bytes 196616 | tf_op jit(solution)/shard_map/ppermute | solution.py:170
  203.7 6.3 %collective-permute-start.20 = (f32[128,128]{1,0:T(8,128)S(1)}, f32[128,128]{1,0:T(8,128)S(1)}, u32[]{:S(2)}, u32[]{:S(2)}) collective-permute-start(f32[128,128]{1,0:T(8,128)S(1)} %fusion.6), channel_id=1, source_target_pairs={{0,12},{4,8},{8,4},{12,0},{16,28},{20,24},{24,20},{28,16},{32,44},... | collective-permute-start | bytes 196616 | tf_op jit(solution)/shard_map/ppermute | solution.py:170
  203.9 6.1 %collective-permute-start.18 = (f32[128,128]{1,0:T(8,128)S(1)}, f32[128,128]{1,0:T(8,128)S(1)}, u32[]{:S(2)}, u32[]{:S(2)}) collective-permute-start(f32[128,128]{1,0:T(8,128)S(1)} %fusion.6), channel_id=1, source_target_pairs={{0,4},{4,0},{8,12},{12,8},{16,20},{20,16},{24,28},{28,24},{32,36},... | collective-permute-start | bytes 196616 | tf_op jit(solution)/shard_map/ppermute | solution.py:170
  205.9 6.7 %collective-permute-start.14 = (f32[128,128]{1,0:T(8,128)S(1)}, f32[128,128]{1,0:T(8,128)S(1)}, u32[]{:S(2)}, u32[]{:S(2)}) collective-permute-start(f32[128,128]{1,0:T(8,128)S(1)} %get-tuple-element.15), channel_id=1, source_target_pairs={{0,3},{1,2},{2,1},{3,0},{4,7},{5,6},{6,5},{7,4},{8,11},{9,10},{10,... | collective-permute-start | bytes 196616 | tf_op jit(solution)/shard_map/ppermute | solution.py:170
  208.5 8.1 %collective-permute-start.13 = (f32[128,128]{1,0:T(8,128)S(1)}, f32[128,128]{1,0:T(8,128)S(1)}, u32[]{:S(2)}, u32[]{:S(2)}) collective-permute-start(f32[128,128]{1,0:T(8,128)S(1)} %get-tuple-element.15), channel_id=1, source_target_pairs={{0,2},{1,3},{2,0},{3,1},{4,6},{5,7},{6,4},{7,5},{8,10},{9,11},{10,... | collective-permute-start | bytes 196616 | tf_op jit(solution)/shard_map/ppermute | solution.py:170
  208.5 8.1 %collective-permute-start.12 = (f32[128,128]{1,0:T(8,128)S(1)}, f32[128,128]{1,0:T(8,128)S(1)}, u32[]{:S(2)}, u32[]{:S(2)}) collective-permute-start(f32[128,128]{1,0:T(8,128)S(1)} %get-tuple-element.15), channel_id=1, source_target_pairs={{0,1},{1,0},{2,3},{3,2},{4,5},{5,4},{6,7},{7,6},{8,9},{9,8},{10,11... | collective-permute-start | bytes 196616 | tf_op jit(solution)/shard_map/ppermute | solution.py:170
  210.1 10.2 %collective-permute-start.22 = (f32[128,128]{1,0:T(8,128)S(1)}, f32[128,128]{1,0:T(8,128)S(1)}, u32[]{:S(2)}, u32[]{:S(2)}) collective-permute-start(f32[128,128]{1,0:T(8,128)S(1)} %add_add_fusion.1), channel_id=1, source_target_pairs={{0,32},{4,36},{8,40},{12,44},{16,48},{20,52},{24,56},{28,60},{32,0... | collective-permute-start | bytes 196616 | tf_op jit(solution)/shard_map/ppermute | solution.py:170
  210.2 10.1 %collective-permute-start.23 = (f32[128,128]{1,0:T(8,128)S(1)}, f32[128,128]{1,0:T(8,128)S(1)}, u32[]{:S(2)}, u32[]{:S(2)}) collective-permute-start(f32[128,128]{1,0:T(8,128)S(1)} %add_add_fusion.1), channel_id=1, source_target_pairs={{0,48},{4,52},{8,56},{12,60},{16,32},{20,36},{24,40},{28,44},{32,1... | collective-permute-start | bytes 196616 | tf_op jit(solution)/shard_map/ppermute | solution.py:170
  212.6 7.6 %collective-permute-start.21 = (f32[128,128]{1,0:T(8,128)S(1)}, f32[128,128]{1,0:T(8,128)S(1)}, u32[]{:S(2)}, u32[]{:S(2)}) collective-permute-start(f32[128,128]{1,0:T(8,128)S(1)} %add_add_fusion.1), channel_id=1, source_target_pairs={{0,16},{4,20},{8,24},{12,28},{16,0},{20,4},{24,8},{28,12},{32,48},... | collective-permute-start | bytes 196616 | tf_op jit(solution)/shard_map/ppermute | solution.py:170
  220.3 10.8 %collective-permute-start.25 = (f32[128,128]{1,0:T(8,128)S(1)}, f32[128,128]{1,0:T(8,128)S(1)}, u32[]{:S(2)}, u32[]{:S(2)}) collective-permute-start(f32[128,128]{1,0:T(8,128)S(1)} %add_add_fusion), channel_id=1, source_target_pairs={{0,128},{4,132},{8,136},{12,140},{16,144},{20,148},{24,152},{28,15... | collective-permute-start | bytes 196616 | tf_op jit(solution)/shard_map/ppermute | solution.py:170
  228.7 5.5 %collective-permute-start.26 = (f32[128,128]{1,0:T(8,128)S(1)}, f32[128,128]{1,0:T(8,128)S(1)}, u32[]{:S(2)}, u32[]{:S(2)}) collective-permute-start(f32[128,128]{1,0:T(8,128)S(1)} %add_add_fusion), channel_id=1, source_target_pairs={{0,192},{4,196},{8,200},{12,204},{16,208},{20,212},{24,216},{28,22... | collective-permute-start | bytes 196616 | tf_op jit(solution)/shard_map/ppermute | solution.py:170
  228.7 5.5 %collective-permute-start.24 = (f32[128,128]{1,0:T(8,128)S(1)}, f32[128,128]{1,0:T(8,128)S(1)}, u32[]{:S(2)}, u32[]{:S(2)}) collective-permute-start(f32[128,128]{1,0:T(8,128)S(1)} %add_add_fusion), channel_id=1, source_target_pairs={{0,64},{4,68},{8,72},{12,76},{16,80},{20,84},{24,88},{28,92},{32,9... | collective-permute-start | bytes 196616 | tf_op jit(solution)/shard_map/ppermute | solution.py:170
Sparse Core Ops, SparseCore 0:
  40.2 44.2 all-gather.2

commit v3 on v2

v3 whole, which is shorter than its diff:
```python
import functools
import math

import jax
import jax.numpy as jnp
from jax import lax
from jax.experimental import pallas as pl
from jax.experimental.pallas import tpu as pltpu
from jax.sharding import PartitionSpec as P

BF = jnp.bfloat16
F32 = jnp.float32
NEG = -1e30
SLOTS = 2
CHUNK = 4


def route_kernel(owner, alive, obs, row_marks, pattern, first, second, marks, slots, info):
    tiles = first.shape[0]
    blocks, parts, quarter = obs.shape[:3]
    lane = lax.broadcasted_iota(jnp.int32, (blocks, 128), 1)
    rows = row_marks[...].astype(F32)
    spot = lax.broadcasted_iota(jnp.int32, (pattern.shape[1], 128), 1)
    line = lax.broadcasted_iota(jnp.int32, (pattern.shape[1], 128), 0)
    shift = (spot == line + quarter).astype(F32).astype(BF)
    groups = jnp.dot(pattern[...].astype(F32).astype(BF), shift, preferred_element_type=F32)
    for j in range(parts):
        turned = rows if j == 0 else pltpu.roll(rows, 128 - j * quarter, 1)
        info[j, :blocks] = jnp.where(lane < quarter, turned, groups)
        info[j, blocks:] = jnp.zeros((8, 128), F32)

    def clear(t, carry):
        marks[t] = 0
        slots[t] = blocks
        slots[tiles + t] = blocks
        return carry

    lax.fori_loop(0, tiles, clear, 0)

    def place(b, carry):
        t = owner[b]

        @pl.when(alive[b] > 0)
        def _():
            k = jnp.minimum(marks[t], SLOTS - 1)
            marks[t] = k + 1
            slots[k * tiles + t] = b

        return carry

    lax.fori_loop(0, blocks, place, 0)
    line8 = lax.broadcasted_iota(jnp.int32, (8, 128), 0)

    def fill(t, carry):
        b0 = slots[t]
        b1 = slots[tiles + t]
        for j in range(parts):
            one = info[j, pl.ds(b0, 1), :]
            two = info[j, pl.ds(b1, 1), :]
            pair = jnp.where(line8 == 0, one, jnp.where(line8 == 1, two, 0.0))
            first[t, j, quarter:quarter + 8, :] = pair.astype(BF)

        @pl.when(b0 < blocks)
        def _():
            first[t, :, :quarter, :] = obs[b0]

        @pl.when(b1 < blocks)
        def _():
            second[t] = obs[b1]

        return carry

    lax.fori_loop(0, tiles, fill, 0)


def lists_kernel(arrived, lists, bias):
    tiles = arrived.shape[0]
    quarter = arrived.shape[2] - 8
    subs = lists.shape[1]
    found = arrived[:, 0, quarter:quarter + 8, :].astype(F32)
    ahead = (
        lax.broadcasted_iota(jnp.int32, (tiles, tiles), 0)
        < lax.broadcasted_iota(jnp.int32, (tiles, tiles), 1)
    ).astype(F32).astype(BF)
    pick_group = (
        lax.broadcasted_iota(jnp.int32, (subs, 128), 1)
        == lax.broadcasted_iota(jnp.int32, (subs, 128), 0) + quarter
    ).astype(F32).astype(BF)
    up = lax.broadcasted_iota(jnp.int32, (128, 128), 0)
    along = lax.broadcasted_iota(jnp.int32, (128, 128), 1)
    widen = ((up < quarter) & (up == along % quarter)).astype(F32).astype(BF)
    turn = lax.broadcasted_iota(jnp.int32, (subs, 128, tiles), 1).astype(F32)
    name = lax.broadcasted_iota(jnp.int32, (subs, 128, tiles), 2).astype(F32)
    last = lax.broadcasted_iota(jnp.int32, (subs, 128), 1) == 127
    for k in range(SLOTS):
        mine = found[:, k, :].astype(BF)
        live = lax.dot_general(
            pick_group, mine, (((1,), (1,)), ((), ())), preferred_element_type=F32
        )
        place = jnp.dot(live.astype(BF), ahead, preferred_element_type=F32)
        hit = (place[:, None, :] == turn) & (live[:, None, :] > 0.5)
        order = jnp.sum(jnp.where(hit, name, 0.0), axis=2)
        count = jnp.sum(live, axis=1, keepdims=True)
        lists[k] = jnp.where(last, count, order).astype(jnp.int32)
        rows = jnp.dot(mine, widen, preferred_element_type=F32)
        bias[k] = (rows - 1.0) * (-NEG)


def split3(v):
    hi = v.astype(BF).astype(F32)
    mid = (v - hi).astype(BF).astype(F32)
    return hi, mid, v - hi - mid


def attend_kernel(final, lists, x, bias, qw, begun, given, wv, *rest):
    if final:
        out, xbuf, acc, top, den = rest
    else:
        out, states, xbuf, acc, top, den = rest
    g = pl.program_id(0)
    heads, sub, width = qw.shape
    rows = heads * sub
    quarter = 32
    parts = x.shape[1]
    cols = x.shape[3]
    n = lists[g, 127]
    lane = lax.broadcasted_iota(jnp.int32, (sub, 128), 1)
    start = begun[...]
    tops = [jnp.broadcast_to(start[:, h:h + 1], (sub, 128)) for h in range(heads)]
    dens = [
        jnp.broadcast_to(start[:, heads + h:heads + h + 1], (sub, 128)) for h in range(heads)
    ]

    def store(numer, tops, dens):
        stats = jnp.zeros((sub, 128), F32)
        if final:
            for h in range(heads):
                for q, part in enumerate(split3(tops[h]) + split3(dens[h])):
                    stats = jnp.where(lane == q * heads + h, part, stats)
            out[:, :width] = numer.astype(BF)
            out[:, width:] = stats.astype(BF)
        else:
            for h in range(heads):
                stats = jnp.where(lane == h, tops[h], stats)
                stats = jnp.where(lane == heads + h, dens[h], stats)
            out[...] = numer
            states[...] = stats

    @pl.when(n == 0)
    def _():
        store(given[...], tops, dens)

    @pl.when(n > 0)
    def _():
        queries = qw[...].reshape(rows, width)
        for h in range(heads):
            top[h * sub:(h + 1) * sub, :] = tops[h]
            den[h * sub:(h + 1) * sub, :] = dens[h]
        acc[...] = jnp.zeros_like(acc)
        lane_slot = lax.broadcasted_iota(jnp.int32, (1, CHUNK * quarter), 1) // quarter

        def step(c, carry):
            shade = jnp.full((1, CHUNK * quarter), NEG, F32)
            for u in range(CHUNK):
                place = c * CHUNK + u
                s = lists[g, jnp.minimum(place, n - 1)]
                for i in range(parts):
                    xbuf[u * quarter:(u + 1) * quarter, i * cols:(i + 1) * cols] = x[
                        s, i, :quarter, :
                    ]
                live = (lane_slot == u) & (place < n)
                shade = jnp.where(live, bias[pl.ds(s, 1), :], shade)
            rows_x = xbuf[...]
            scores = lax.dot_general(
                queries, rows_x, (((1,), (1,)), ((), ())), preferred_element_type=F32
            ) + shade
            old = top[...]
            new = jnp.maximum(old, jnp.max(scores, axis=1, keepdims=True))
            weights = jnp.exp(scores - new)
            shrink = jnp.exp(old - new)
            top[...] = new
            den[...] = den[...] * shrink + jnp.sum(weights, axis=1, keepdims=True)
            more = jnp.dot(weights.astype(BF), rows_x, preferred_element_type=F32)
            acc[...] = acc[...] * jnp.concatenate([shrink] * (width // 128), axis=1) + more
            return carry

        lax.fori_loop(0, (n + CHUNK - 1) // CHUNK, step, 0)
        mixed = jnp.dot(acc[...].astype(BF), wv[...], preferred_element_type=F32)
        mixed = mixed.reshape(heads, sub, width)
        head_of = lax.broadcasted_iota(jnp.int32, (sub, width), 1) // (width // heads)
        before = given[...]
        numer = jnp.zeros((sub, width), F32)
        ends = [top[h * sub:(h + 1) * sub, :] for h in range(heads)]
        sums = [den[h * sub:(h + 1) * sub, :] for h in range(heads)]
        for h in range(heads):
            shrink = jnp.concatenate([jnp.exp(tops[h] - ends[h])] * (width // 128), axis=1)
            numer = jnp.where(head_of == h, before * shrink + mixed[h], numer)
        store(numer, ends, sums)


def finish_kernel(place, r0, r1, r2, r3, lat, w_out, gain, w_inc, target, out):
    width = lat.shape[1]
    heads = 8
    tops, dens, nums = [], [], []
    line = lax.broadcasted_iota(jnp.int32, (128, 2 * width), 0)
    col = lax.broadcasted_iota(jnp.int32, (128, 2 * width), 1)
    kind = line // heads
    match = (line % heads == (col % width) // (width // heads)) & (
        kind // 3 == col // width
    ) & (kind < 6)
    spread = match.astype(F32).astype(BF)
    for r in (r0, r1, r2, r3):
        wide = jnp.dot(r[:, width:], spread, preferred_element_type=F32)
        tops.append(wide[:, :width])
        dens.append(wide[:, width:])
        nums.append(r[:, :width].astype(F32))
    best = jnp.maximum(jnp.maximum(tops[0], tops[1]), jnp.maximum(tops[2], tops[3]))
    scale = [jnp.exp(v - best) for v in tops]
    numer = sum(a * b for a, b in zip(scale, nums))
    denom = sum(a * b for a, b in zip(scale, dens))
    attended = (numer / denom).astype(BF)
    updated = lat[...].astype(F32) + jnp.dot(attended, w_out[...], preferred_element_type=F32)
    power = jnp.mean(updated * updated, axis=1, keepdims=True)
    normed = (updated * lax.rsqrt(power + 1e-6) * gain[...]).astype(BF)
    predicted = jnp.dot(normed, w_inc[...], preferred_element_type=F32)
    residual = predicted - target[...].astype(F32)
    high = residual.astype(BF)
    low = (residual - high.astype(F32)).astype(BF)
    dims = (((0,), (0,)), ((), ()))
    grad = lax.dot_general(normed, high, dims, preferred_element_type=F32)
    grad = grad + lax.dot_general(normed, low, dims, preferred_element_type=F32)
    rows = predicted.shape[0]
    for d in range(4):
        out[d, :128, :] = grad[d * 128:(d + 1) * 128]
        out[d, 128:128 + rows, :] = predicted


def body(
    obs_feat,
    row_valid,
    block_owner,
    block_pattern,
    latent,
    w_query,
    w_key,
    w_value,
    self_bias,
    w_out,
    norm_gain,
    w_inc,
    target,
):
    tiles = lax.axis_size("tile")
    groups = lax.axis_size("head")
    me = lax.axis_index("head")
    blocks = block_owner.shape[0]
    block_rows = obs_feat.shape[0] // blocks
    quarter = block_rows // groups
    cols = obs_feat.shape[1]
    lat_rows, width = latent.shape
    subs = block_pattern.shape[1]
    sub = lat_rows // subs
    local_heads = self_bias.shape[0]
    heads = local_heads * groups
    head_size = width // heads
    share = lat_rows // groups

    def swap(v, axis, mask, size):
        return lax.ppermute(v, axis, [(d, d ^ mask) for d in range(size)])

    def pick(v, which):
        return lax.dynamic_index_in_dim(v, which, 0, keepdims=False)

    tile = lax.axis_index("tile")
    whole = lambda *shape: pl.BlockSpec(shape, lambda g, *_: (0,) * len(shape))
    depth = quarter + 8
    first, second = pl.pallas_call(
        route_kernel,
        grid_spec=pltpu.PrefetchScalarGridSpec(
            num_scalar_prefetch=2,
            grid=(1,),
            in_specs=[
                whole(blocks, groups, quarter, cols),
                whole(blocks, block_rows),
                whole(blocks, subs),
            ],
            out_specs=[
                whole(tiles, groups, depth, cols),
                whole(tiles, groups, quarter, cols),
            ],
            scratch_shapes=[
                pltpu.SMEM((tiles,), jnp.int32),
                pltpu.SMEM((SLOTS * tiles,), jnp.int32),
                pltpu.VMEM((groups, blocks + 8, 128), F32),
            ],
        ),
        out_shape=[
            jax.ShapeDtypeStruct((tiles, groups, depth, cols), BF),
            jax.ShapeDtypeStruct((tiles, groups, quarter, cols), BF),
        ],
        compiler_params=pltpu.CompilerParams(vmem_limit_bytes=32 * 1024 * 1024),
        name="route",
    )(
        block_owner[:, 0],
        jnp.max(block_pattern, axis=1),
        obs_feat.reshape(blocks, groups, quarter, cols),
        row_valid.reshape(blocks, block_rows),
        block_pattern,
    )

    def exchange(v):
        flat = v.reshape((tiles * groups,) + v.shape[2:])
        flat = lax.all_to_all(flat, ("tile", "head"), split_axis=0, concat_axis=0, tiled=True)
        return flat.reshape(v.shape)

    first = exchange(first)
    second = exchange(second)

    lists, bias = pl.pallas_call(
        lists_kernel,
        grid=(1,),
        in_specs=[pl.BlockSpec((tiles, 1, depth, cols), lambda g: (0, 0, 0, 0))],
        out_specs=[whole(SLOTS, subs, 128), whole(SLOTS, tiles, 128)],
        out_shape=[
            jax.ShapeDtypeStruct((SLOTS, subs, 128), jnp.int32),
            jax.ShapeDtypeStruct((SLOTS, tiles, 128), F32),
        ],
        name="lists",
    )(first)

    stacked = lax.all_gather(
        jnp.concatenate([w_query, w_key, w_value, w_out.T], axis=1), "head", axis=0
    )
    wq, wk, wv, wo = [
        stacked[:, :, a * 128:(a + 1) * 128].transpose(1, 0, 2).reshape(width, width)
        for a in range(4)
    ]
    wo = wo.T
    by_distance = jnp.stack(
        [self_bias] + [swap(self_bias, "head", d, groups) for d in range(1, groups)]
    )
    turn = jnp.arange(groups, dtype=jnp.int32) ^ me
    bias_all = jnp.take(by_distance, turn, axis=0).reshape(heads)
    queries = jnp.dot(latent, wq, preferred_element_type=F32).astype(BF)
    own_key = jnp.dot(latent, wk, preferred_element_type=F32).astype(BF)
    q3 = queries.reshape(lat_rows, heads, head_size)
    k3 = wk.reshape(width, heads, head_size)
    scale = 1.0 / math.sqrt(head_size)
    qw = (
        jnp.einsum("lhd,khd->hlk", q3, k3, preferred_element_type=F32) * scale
    ).astype(BF)
    own = (
        jnp.sum(
            q3.astype(F32) * own_key.reshape(lat_rows, heads, head_size).astype(F32), axis=-1
        )
        * scale
        + bias_all[None, :]
    )
    keep = (me == 0).astype(F32)
    states = jnp.pad(
        jnp.concatenate([own, jnp.full((lat_rows, heads), keep)], axis=1),
        ((0, 0), (0, 128 - 2 * heads)),
    )
    numer = jnp.dot(latent, wv, preferred_element_type=F32) * keep

    def attend(k, x, numer, states, final):
        if final:
            out_specs = pl.BlockSpec((sub, width + 128), lambda g, *_: (g, 0))
            out_shape = jax.ShapeDtypeStruct((lat_rows, width + 128), BF)
        else:
            out_specs = [
                pl.BlockSpec((sub, width), lambda g, *_: (g, 0)),
                pl.BlockSpec((sub, 128), lambda g, *_: (g, 0)),
            ]
            out_shape = [
                jax.ShapeDtypeStruct((lat_rows, width), F32),
                jax.ShapeDtypeStruct((lat_rows, 128), F32),
            ]
        return pl.pallas_call(
            functools.partial(attend_kernel, final),
            grid_spec=pltpu.PrefetchScalarGridSpec(
                num_scalar_prefetch=1,
                grid=(subs,),
                in_specs=[
                    whole(*x.shape),
                    whole(tiles, 128),
                    pl.BlockSpec((heads, sub, width), lambda g, *_: (0, g, 0)),
                    pl.BlockSpec((sub, 128), lambda g, *_: (g, 0)),
                    pl.BlockSpec((sub, width), lambda g, *_: (g, 0)),
                    whole(width, width),
                ],
                out_specs=out_specs,
                scratch_shapes=[
                    pltpu.VMEM((CHUNK * quarter, width), BF),
                    pltpu.VMEM((heads * sub, width), F32),
                    pltpu.VMEM((heads * sub, 128), F32),
                    pltpu.VMEM((heads * sub, 128), F32),
                ],
            ),
            out_shape=out_shape,
            compiler_params=pltpu.CompilerParams(vmem_limit_bytes=40 * 1024 * 1024),
            name="attend",
        )(lists[k], x, bias[k], qw, states, numer, wv)

    numer, states = attend(0, first, numer, states, False)
    partial = attend(1, second, numer, states, True)

    partial = partial.reshape(groups, share, width + 128)
    received = [pick(partial, me)] + [
        swap(pick(partial, me ^ d), "head", d, groups) for d in range(1, groups)
    ]
    row = lambda *shape: pl.BlockSpec(shape, lambda i, m: (m[0], 0))
    full = lambda *shape: pl.BlockSpec(shape, lambda i, m: (0,) * len(shape))
    packed = pl.pallas_call(
        finish_kernel,
        grid_spec=pltpu.PrefetchScalarGridSpec(
            num_scalar_prefetch=1,
            grid=(1,),
            in_specs=[full(share, width + 128)] * 4
            + [
                row(share, width),
                full(width, width),
                full(1, width),
                full(width, 128),
                row(share, 128),
            ],
            out_specs=full(groups, 128 + share, 128),
        ),
        out_shape=jax.ShapeDtypeStruct((groups, 128 + share, 128), F32),
        compiler_params=pltpu.CompilerParams(vmem_limit_bytes=32 * 1024 * 1024),
        name="finish",
    )(
        me[None].astype(jnp.int32),
        *received,
        latent,
        wo,
        norm_gain[None, :],
        w_inc,
        target,
    )
    grads = [pick(packed, me)[:128]] + [
        swap(pick(packed, me ^ d)[:128], "head", d, groups) for d in range(1, groups)
    ]
    grad = (grads[0] + grads[1]) + (grads[2] + grads[3])
    for low, high in ((1, 2), (4, 8), (16, 32)):
        a, b, c = (swap(grad, "tile", m, tiles) for m in (low, high, low + high))
        grad = (grad + a) + (b + c)
    mine = packed[0, 128:]
    preds = jnp.stack([mine] + [swap(mine, "head", d, groups) for d in range(1, groups)])
    predicted = jnp.take(preds, turn, axis=0).reshape(lat_rows, 128)
    return predicted, grad * (1.0 / math.sqrt(lat_rows * tiles))


def solution(mesh):
    in_specs = (
        P("tile", "head"),
        P("tile"),
        P("tile", None),
        P("tile", None),
        P("tile", None),
        P(None, "head"),
        P(None, "head"),
        P(None, "head"),
        P("head"),
        P("head", None),
        P(),
        P(),
        P("tile", None),
    )
    out_specs = (P("tile", None), P("head", None))
    return jax.shard_map(body, mesh=mesh, in_specs=in_specs, out_specs=out_specs, check_vma=False)
```

time: 241 us -> 231 us (0.959)
  waiting for transfers between devices: 120 us -> 93.3 us
  local copies, waits for them, and re-layouts: 12.5 us -> 25.4 us
  Pallas kernels: 21.9 us -> 31.6 us
  starting transfers between devices: 62.5 us -> 55.6 us
    ppermute x27 -> x21, waiting for transfers between devices: 120 us -> 22 us  [swap(): return lax.ppermute(v, axis, [(d, d ^ mask) for d in range(size)])]
    all_to_all x1 -> x2, waiting for transfers between devices: 0.01 us -> 71.3 us  [exchange(): lax.all_to_all(flat, ('tile', 'head'), split_axis=0, concat_axis=0, tiled...]
    ppermute x27 -> x21, starting transfers between devices: 47.1 us -> 33.1 us  [swap(): return lax.ppermute(v, axis, [(d, d ^ mask) for d in range(size)])]
    unnamed x39 -> x56, local copies, waits for them, and re-layouts: 6.9 us -> 16.5 us
    pallas_call x1 -> x3, Pallas kernels: 18.9 us -> 26.8 us  [the longest x2 24.1 us: attend(): pl.pallas_call(functools.partial(attend_kernel, final), grid_spec=pltpu.P...]
    all_to_all x1 -> x2, starting transfers between devices: 15.4 us -> 22.5 us  [exchange(): lax.all_to_all(flat, ('tile', 'head'), split_axis=0, concat_axis=0, tiled...]
    transpose x4, local copies, waits for them, and re-layouts: 2.38 us -> 5.76 us  [body(): stacked[:, :, a * 128:(a + 1) * 128].transpose(1, 0, 2)]
  transfers between devices with their start and end apart: 29 -> 24, of which waited for: 15 -> 15; matrix products, arithmetic and copies ran while one was open for 6% -> 7% of each run, Pallas kernels for 0% -> 9%
where the time goes in v3:
time: 231 us; the launch traced here: 229 us
  waiting for transfers between devices  93.3 us (40%)
  starting transfers between devices  55.6 us (24%)
  Pallas kernels  31.6 us (14%)
  local copies, waits for them, and re-layouts  25.4 us (11%)
  between operations  14.4 us (6%)
  matrix products  5.69 us (2%)
  other arithmetic  3.29 us (1%)
    all_to_all x2, waiting for transfers between devices, exchange(): lax.all_to_all(flat, ('tile', 'head'), split_axis=0, concat_axis=0, tiled...  71.3 us
    ppermute x21, starting transfers between devices, swap(): return lax.ppermute(v, axis, [(d, d ^ mask) for d in range(size)])  33.1 us
    pallas_call x2, Pallas kernels, attend(): pl.pallas_call(functools.partial(attend_kernel, final), grid_spec=pltpu.P...  24.1 us
    all_to_all x2, starting transfers between devices, exchange(): lax.all_to_all(flat, ('tile', 'head'), split_axis=0, concat_axis=0, tiled...  22.5 us
    ppermute x21, waiting for transfers between devices, swap(): return lax.ppermute(v, axis, [(d, d ^ mask) for d in range(size)])  22 us
    unnamed x56, local copies, waits for them, and re-layouts  16.5 us
    transpose x4, local copies, waits for them, and re-layouts, body(): stacked[:, :, a * 128:(a + 1) * 128].transpose(1, 0, 2)  5.76 us
  transfers between devices with their start and end apart: 24, of which 15 were waited for; matrix products, arithmetic and copies ran while one was open for 7% of the time, Pallas kernels for 9%

profile of v3, /device:TPU:32, one launch (start us, length us, event | category | flops | bytes accessed | tf_op | source)
XLA Modules:
  0.0 229.4 jit_solution(5611631912248435614)
XLA Ops:
  7.2 0.8 copy.54.pattern
  7.9 0.7 reduce_max.9.alive
  8.7 1.6 copy-done.9
  10.3 0.8 copy-done.17
  11.7 3.5 %route.1 = (bf16[64,4,40,128]{3,2,1,0:T(8,128)(2,1)S(1)}, bf16[64,4,32,128]{3,2,1,0:T(8,128)(2,1)S(1)}) custom-call(s32[64]{0:T(128)S(1)} %bitcast.102, s32[64]{0:T(128)S(1)} %reduce_max.9.alive, bf16[64,4,32,128]{3,2,1,0:T(8,128)(2,1)S(1)} %bitcast.97, s32[64,128]{1,0:T(8,128)S(1)} %bitcast.100, s32[64,16]{1,0:T(8,128)S(1)} %copy.54.pattern), custom_call_target="tpu_custom_call" | custom-call | tf_op jit(solution)/shard_map/route/pallas_call | solution.py:277
  15.2 1.6 copy-done.8
  16.8 1.3 copy-done.10
  18.1 14.4 %all-to-all-start = ((bf16[256,40,128]{2,1,0:T(8,128)(2,1)}), bf16[256,40,128]{2,1,0:T(8,128)(2,1)S(1)}, u32[]{:S(2)}, u32[]{:S(2)}) async-start(bf16[256,40,128]{2,1,0:T(8,128)(2,1)} %bitcast.96), calls=%async_computation | async-start | bytes 5242880 | tf_op jit(solution)/shard_map/all_to_all | solution.py:313
  32.7 0.9 pad_maximum_fusion
  33.6 64.6 %all-to-all-done = bf16[256,40,128]{2,1,0:T(8,128)(2,1)S(1)} async-done(((bf16[256,40,128]{2,1,0:T(8,128)(2,1)}), bf16[256,40,128]{2,1,0:T(8,128)(2,1)S(1)}, u32[]{:S(2)}, u32[]{:S(2)}) %all-to-all-start) | async-done | bytes 2621472 | tf_op jit(solution)/shard_map/all_to_all | solution.py:313
  98.2 8.1 %all-to-all-start.1 = ((bf16[256,32,128]{2,1,0:T(8,128)(2,1)}), bf16[256,32,128]{2,1,0:T(8,128)(2,1)}, u32[]{:S(2)}, u32[]{:S(2)}) async-start(bf16[256,32,128]{2,1,0:T(8,128)(2,1)} %bitcast.98), calls=%async_computation.1 | async-start | bytes 4194304 | tf_op jit(solution)/shard_map/all_to_all | solution.py:313
  106.3 2.8 %collective-permute-start.2 = (f32[2]{0:T(128)S(1)}, f32[2]{0:T(128)S(1)}, u32[]{:S(2)}, u32[]{:S(2)}) collective-permute-start(f32[2]{0:T(128)S(1)} %copy-done.26), channel_id=1, source_target_pairs={{0,3},{1,2},{2,1},{3,0},{4,7},{5,6},{6,5},{7,4},{8,11},{9,10},{10,... | collective-permute-start | bytes 32 | tf_op jit(solution)/shard_map/ppermute | solution.py:269
  109.2 0.8 collective-permute-start.1
  111.3 3.0 %collective-permute-done.1 = f32[2]{0:T(128)S(1)} collective-permute-done((f32[2]{0:T(128)S(1)}, f32[2]{0:T(128)S(1)}, u32[]{:S(2)}, u32[]{:S(2)}) %collective-permute-start.1) | collective-permute-done | bytes 40 | tf_op jit(solution)/shard_map/ppermute | solution.py:269
  114.9 3.0 %slice_bitcast_fusion = (bf16[512,4,128]{2,0,1:T(8,128)(2,1)}, bf16[4,64,8,128]{3,2,1,0:T(8,128)(2,1)}, bf16[512,4,128]{2,0,1:T(8,128)(2,1)}, bf16[512,4,128]{2,0,1:T(8,128)(2,1)}) fusion(bf16[4,512,512]{2,1,0:T(8,128)(2,1)} %bitcast.107), kind=kLoop, calls=%fused_computation.10 | loop fusion | bytes 4194304 | tf_op jit(solution)/shard_map/transpose | solution.py:335
  117.9 1.2 copy.56
  119.2 1.3 copy.57
  122.0 1.5 fusion.given
  123.5 3.3 %multiply_convert_fusion.qw = bf16[8,512,512]{2,1,0:T(8,128)(2,1)} fusion(bf16[512,8,64]{0,2,1:T(8,128)(2,1)S(1)} %bitcast.103, bf16[512,8,64]{0,2,1:T(8,128)(2,1)S(1)} %bitcast.105), kind=kOutput, calls=%fused_computation.2 | convolution fusion | flops 272629760 | bytes 5242880 | tf_op jit(solution)/shard_map/lhd,khd->hlk/dot_general | solution.py:350
  126.8 2.7 %lists.1 = (s32[2,16,128]{2,1,0:T(8,128)}, f32[2,64,128]{2,1,0:T(8,128)}) custom-call(bf16[64,4,40,128]{3,2,1,0:T(8,128)(2,1)} %bitcast.91), custom_call_target="tpu_custom_call" | custom-call | tf_op jit(solution)/shard_map/lists/pallas_call | solution.py:319
  129.5 0.7 slice_bitcast_fusion.6
  130.3 0.8 slice_bitcast_fusion.4
  131.0 2.2 copy-done
  133.2 1.2 copy-done.7
  134.5 17.1 %attend.2 = (f32[512,512]{1,0:T(8,128)S(1)}, f32[512,128]{1,0:T(8,128)S(1)}) custom-call(s32[16,128]{1,0:T(8,128)S(1)} %get-tuple-element.29.lists, bf16[64,4,40,128]{3,2,1,0:T(8,128)(2,1)S(1)} %bitcast.92, f32[64,128]{1,0:T(8,128)S(1)} %get-tuple-element.27.bias, bf16[8,512,512]{2,1,0:T(8,128)(2,1)S(1)} %copy-done, f32[512,128]{1,0:T(8,128)S(1)} %pad_select_fusion.begun, ...), custom_call_target="tpu_custom_call" | custom-call | tf_op jit(solution)/shard_map/attend/pallas_call | solution.py:379
  151.5 1.0 copy-done.11
  153.2 6.7 %all-to-all-done.1 = bf16[256,32,128]{2,1,0:T(8,128)(2,1)} async-done(((bf16[256,32,128]{2,1,0:T(8,128)(2,1)}), bf16[256,32,128]{2,1,0:T(8,128)(2,1)}, u32[]{:S(2)}, u32[]{:S(2)}) %all-to-all-start.1) | async-done | bytes 2097184 | tf_op jit(solution)/shard_map/all_to_all | solution.py:313
  159.9 2.2 copy-done.1
  162.1 1.2 copy-done.12
  163.3 0.9 copy-done.14
  164.3 7.0 %attend.3 = bf16[512,640]{1,0:T(8,128)(2,1)S(1)} custom-call(s32[16,128]{1,0:T(8,128)S(1)} %get-tuple-element.30.lists, bf16[64,4,32,128]{3,2,1,0:T(8,128)(2,1)} %bitcast.9.x, f32[64,128]{1,0:T(8,128)S(1)} %get-tuple-element.28.bias, bf16[8,512,512]{2,1,0:T(8,128)(2,1)S(1)} %copy-done.1, f32[512,128]{1,0:T(8,128)S(1)} %copy-done.14, ...), custom_call_target="tpu_custom_call" | custom-call | tf_op jit(solution)/shard_map/attend/pallas_call | solution.py:379
  172.1 1.6 collective-permute-start.4
  173.7 2.5 %collective-permute-start.5 = (bf16[128,640]{1,0:T(8,128)(2,1)S(1)}, bf16[128,640]{1,0:T(8,128)(2,1)S(1)}, u32[]{:S(2)}, u32[]{:S(2)}) collective-permute-start(bf16[128,640]{1,0:T(8,128)(2,1)S(1)} %get-tuple-element.18), channel_id=1, source_target_pairs={{0,3},{1,2},{2,1},{3,0},{4,7},{5,6},{6,5},{7,4},{8,11},{9,10},{10,... | collective-permute-start | bytes 491528 | tf_op jit(solution)/shard_map/ppermute | solution.py:269
  176.4 2.2 collective-permute-done.3.r1
  178.6 1.9 collective-permute-done.4.r2
  180.6 2.1 collective-permute-done.5.r3
  182.7 1.3 finish.1
  184.1 4.3 %collective-permute-start.10 = (f32[128,128]{1,0:T(8,128)S(1)}, f32[128,128]{1,0:T(8,128)S(1)}, u32[]{:S(2)}, u32[]{:S(2)}) collective-permute-start(f32[128,128]{1,0:T(8,128)S(1)} %get-tuple-element.24), channel_id=1, source_target_pairs={{0,2},{1,3},{2,0},{3,1},{4,6},{5,7},{6,4},{7,5},{8,10},{9,11},{10,... | collective-permute-start | bytes 196616 | tf_op jit(solution)/shard_map/ppermute | solution.py:269
  188.8 2.6 %collective-permute-done.10 = f32[128,128]{1,0:T(8,128)S(1)} collective-permute-done((f32[128,128]{1,0:T(8,128)S(1)}, f32[128,128]{1,0:T(8,128)S(1)}, u32[]{:S(2)}, u32[]{:S(2)}) %collective-permute-start.10) | collective-permute-done | bytes 65568 | tf_op jit(solution)/shard_map/ppermute | solution.py:269
  191.4 2.4 %collective-permute-done.11 = f32[128,128]{1,0:T(8,128)S(1)} collective-permute-done((f32[128,128]{1,0:T(8,128)S(1)}, f32[128,128]{1,0:T(8,128)S(1)}, u32[]{:S(2)}, u32[]{:S(2)}) %collective-permute-start.11) | collective-permute-done | bytes 65568 | tf_op jit(solution)/shard_map/ppermute | solution.py:269
  194.0 2.7 %collective-permute-start.14 = (f32[128,128]{1,0:T(8,128)S(1)}, f32[128,128]{1,0:T(8,128)S(1)}, u32[]{:S(2)}, u32[]{:S(2)}) collective-permute-start(f32[128,128]{1,0:T(8,128)S(1)} %fusion.3), channel_id=1, source_target_pairs={{0,12},{4,8},{8,4},{12,0},{16,28},{20,24},{24,20},{28,16},{32,44},... | collective-permute-start | bytes 196616 | tf_op jit(solution)/shard_map/ppermute | solution.py:269
  198.6 2.3 %collective-permute-start.6 = (f32[128,128]{1,0:T(8,128)S(1)}, f32[128,128]{1,0:T(8,128)S(1)}, u32[]{:S(2)}, u32[]{:S(2)}) collective-permute-start(f32[128,128]{1,0:T(8,128)S(1)} %get-tuple-element.23), channel_id=1, source_target_pairs={{0,1},{1,0},{2,3},{3,2},{4,5},{5,4},{6,7},{7,6},{8,9},{9,8},{10,11... | collective-permute-start | bytes 196616 | tf_op jit(solution)/shard_map/ppermute | solution.py:269
  200.9 7.7 %collective-permute-start.16 = (f32[128,128]{1,0:T(8,128)S(1)}, f32[128,128]{1,0:T(8,128)S(1)}, u32[]{:S(2)}, u32[]{:S(2)}) collective-permute-start(f32[128,128]{1,0:T(8,128)S(1)} %add_add_fusion.1), channel_id=1, source_target_pairs={{0,32},{4,36},{8,40},{12,44},{16,48},{20,52},{24,56},{28,60},{32,0... | collective-permute-start | bytes 196616 | tf_op jit(solution)/shard_map/ppermute | solution.py:269
  208.7 1.6 collective-permute-start.17
  211.4 3.9 %collective-permute-done.17 = f32[128,128]{1,0:T(8,128)S(1)} collective-permute-done((f32[128,128]{1,0:T(8,128)S(1)}, f32[128,128]{1,0:T(8,128)S(1)}, u32[]{:S(2)}, u32[]{:S(2)}) %collective-permute-start.17) | collective-permute-done | bytes 65568 | tf_op jit(solution)/shard_map/ppermute | solution.py:269
  216.1 3.0 %collective-permute-start.18 = (f32[128,128]{1,0:T(8,128)S(1)}, f32[128,128]{1,0:T(8,128)S(1)}, u32[]{:S(2)}, u32[]{:S(2)}) collective-permute-start(f32[128,128]{1,0:T(8,128)S(1)} %add_add_fusion), channel_id=1, source_target_pairs={{0,64},{4,68},{8,72},{12,76},{16,80},{20,84},{24,88},{28,92},{32,9... | collective-permute-start | bytes 196616 | tf_op jit(solution)/shard_map/ppermute | solution.py:269
  219.1 0.8 bitcast_select_fusion
  219.9 1.6 collective-permute-done.19
  (96 shorter events, 11.4 us)
Async XLA Ops:
  8.7 1.6 copy-start.9
  15.2 1.6 copy-start.8
  16.8 1.3 copy-start.10
  18.1 14.5 %copy-start.22 = (bf16[128,512]{1,0:T(8,128)(2,1)S(1)}, bf16[128,512]{1,0:T(8,128)(2,1)}, u32[]{:S(2)}) copy-start(bf16[128,512]{1,0:T(8,128)(2,1)} %param.22) | copy-start | bytes 393220
  18.1 14.6 %copy-start.23 = (bf16[512,128]{1,0:T(8,128)(2,1)S(1)}, bf16[512,128]{1,0:T(8,128)(2,1)}, u32[]{:S(2)}) copy-start(bf16[512,128]{1,0:T(8,128)(2,1)} %param.20) | copy-start | bytes 393220
  18.1 14.6 %copy-start.24 = (bf16[512,128]{1,0:T(8,128)(2,1)S(1)}, bf16[512,128]{1,0:T(8,128)(2,1)}, u32[]{:S(2)}) copy-start(bf16[512,128]{1,0:T(8,128)(2,1)} %param.19) | copy-start | bytes 393220
  18.1 14.6 %copy-start.25 = (bf16[512,128]{1,0:T(8,128)(2,1)S(1)}, bf16[512,128]{1,0:T(8,128)(2,1)}, u32[]{:S(2)}) copy-start(bf16[512,128]{1,0:T(8,128)(2,1)} %param.18) | copy-start | bytes 393220
  18.1 80.1 %all-to-all-start = ((bf16[256,40,128]{2,1,0:T(8,128)(2,1)}), bf16[256,40,128]{2,1,0:T(8,128)(2,1)S(1)}, u32[]{:S(2)}, u32[]{:S(2)}) async-start(bf16[256,40,128]{2,1,0:T(8,128)(2,1)} %bitcast.96), calls=%async_computation | async-start | bytes 5242880 | tf_op jit(solution)/shard_map/all_to_all | solution.py:313
  32.5 82.4 %all-gather.3.cloned.1.call-start = ((), (), s32[]{:S(2)}) async-start(), calls=%async_computation.2 | async-start | bytes 2621440 | tf_op jit(solution)/shard_map/all_gather | solution.py:331
  33.6 72.8 %copy-start.26 = (f32[2]{0:T(128)S(1)}, f32[2]{0:T(128)}, u32[]{:S(2)}) copy-start(f32[2]{0:T(128)} %param.21) | copy-start | bytes 28
  98.2 19.8 %copy-start.2 = (bf16[256,40,128]{2,1,0:T(8,128)(2,1)}, bf16[256,40,128]{2,1,0:T(8,128)(2,1)S(1)}, u32[]{:S(2)}) copy-start(bf16[256,40,128]{2,1,0:T(8,128)(2,1)S(1)} %all-to-all-done) | copy-start | bytes 7864324
  98.2 61.7 %all-to-all-start.1 = ((bf16[256,32,128]{2,1,0:T(8,128)(2,1)}), bf16[256,32,128]{2,1,0:T(8,128)(2,1)}, u32[]{:S(2)}, u32[]{:S(2)}) async-start(bf16[256,32,128]{2,1,0:T(8,128)(2,1)} %bitcast.98), calls=%async_computation.1 | async-start | bytes 4194304 | tf_op jit(solution)/shard_map/all_to_all | solution.py:313
  106.3 4.9 %collective-permute-start.2 = (f32[2]{0:T(128)S(1)}, f32[2]{0:T(128)S(1)}, u32[]{:S(2)}, u32[]{:S(2)}) collective-permute-start(f32[2]{0:T(128)S(1)} %copy-done.26), channel_id=1, source_target_pairs={{0,3},{1,2},{2,1},{3,0},{4,7},{5,6},{6,5},{7,4},{8,11},{9,10},{10,... | collective-permute-start | bytes 32 | tf_op jit(solution)/shard_map/ppermute | solution.py:269
  109.2 5.0 %collective-permute-start.1 = (f32[2]{0:T(128)S(1)}, f32[2]{0:T(128)S(1)}, u32[]{:S(2)}, u32[]{:S(2)}) collective-permute-start(f32[2]{0:T(128)S(1)} %copy-done.26), channel_id=1, source_target_pairs={{0,2},{1,3},{2,0},{3,1},{4,6},{5,7},{6,4},{7,5},{8,10},{9,11},{10,... | collective-permute-start | bytes 32 | tf_op jit(solution)/shard_map/ppermute | solution.py:269
  110.0 4.2 %collective-permute-start = (f32[2]{0:T(128)S(1)}, f32[2]{0:T(128)S(1)}, u32[]{:S(2)}, u32[]{:S(2)}) collective-permute-start(f32[2]{0:T(128)S(1)} %copy-done.26), channel_id=1, source_target_pairs={{0,1},{1,0},{2,3},{3,2},{4,5},{5,4},{6,7},{7,6},{8,9},{9,8},{10,11... | collective-permute-start | bytes 32 | tf_op jit(solution)/shard_map/ppermute | solution.py:269
  114.9 5.6 %copy-start.4 = (bf16[512,512]{1,0:T(8,128)(2,1)S(1)}, bf16[512,512]{1,0:T(8,128)(2,1)}, u32[]{:S(2)}) copy-start(bf16[512,512]{1,0:T(8,128)(2,1)} %lat.1) | copy-start | bytes 1572868
  119.2 2.4 %copy-start.20 = (bf16[4,64,8,128]{3,2,1,0:T(8,128)(2,1)S(1)}, bf16[4,64,8,128]{3,2,1,0:T(8,128)(2,1)}, u32[]{:S(2)}) copy-start(bf16[4,64,8,128]{3,2,1,0:T(8,128)(2,1)} %get-tuple-element.15) | copy-start | bytes 1572868
  121.0 1.0 copy-start.5
  126.8 4.3 %copy-start.3 = (bf16[256,40,128]{2,1,0:T(8,128)(2,1)S(1)}, bf16[256,40,128]{2,1,0:T(8,128)(2,1)}, u32[]{:S(2)}) copy-start(bf16[256,40,128]{2,1,0:T(8,128)(2,1)} %copy-done.2) | copy-start | bytes 7864324
  131.0 2.2 copy-start
  133.2 1.2 copy-start.7
  151.5 1.0 copy-start.11
  159.9 2.2 copy-start.1
  162.1 1.2 copy-start.12
  163.3 0.9 copy-start.14
  164.3 11.9 %copy-start.21 = (bf16[512,4,128]{2,0,1:T(8,128)(2,1)S(1)}, bf16[512,4,128]{2,0,1:T(8,128)(2,1)}, u32[]{:S(2)}) copy-start(bf16[512,4,128]{2,0,1:T(8,128)(2,1)} %get-tuple-element.14) | copy-start | bytes 1572868
  164.3 18.4 %copy-start.15 = (bf16[512,128]{1,0:T(8,128)(2,1)S(1)}, bf16[512,128]{1,0:T(8,128)(2,1)}, u32[]{:S(2)}) copy-start(bf16[512,128]{1,0:T(8,128)(2,1)} %w_inc.1) | copy-start | bytes 393220
  164.3 18.4 %copy-start.16 = (bf16[512,128]{1,0:T(8,128)(2,1)S(1)}, bf16[512,128]{1,0:T(8,128)(2,1)}, u32[]{:S(2)}) copy-start(bf16[512,128]{1,0:T(8,128)(2,1)} %target.1) | copy-start | bytes 393220
  164.3 18.4 %copy-start.18 = (f32[512]{0:T(512)S(1)}, f32[512]{0:T(512)}, u32[]{:S(2)}) copy-start(f32[512]{0:T(512)} %param.23) | copy-start | bytes 6148
  171.3 11.4 %copy-start.6 = (bf16[512,512]{1,0:T(8,128)(2,1)S(1)}, bf16[512,512]{1,0:T(8,128)(2,1)}, u32[]{:S(2)}) copy-start(bf16[512,512]{1,0:T(8,128)(2,1)} %lat.1) | copy-start | bytes 1572868
  171.4 7.2 %collective-permute-start.3 = (bf16[128,640]{1,0:T(8,128)(2,1)S(1)}, bf16[128,640]{1,0:T(8,128)(2,1)S(1)}, u32[]{:S(2)}, u32[]{:S(2)}) collective-permute-start(bf16[128,640]{1,0:T(8,128)(2,1)S(1)} %get-tuple-element.20), channel_id=1, source_target_pairs={{0,1},{1,0},{2,3},{3,2},{4,5},{5,4},{6,7},{7,6},{8,9},{9,8},{10,11... | collective-permute-start | bytes 491528 | tf_op jit(solution)/shard_map/ppermute | solution.py:269
  172.1 8.5 %collective-permute-start.4 = (bf16[128,640]{1,0:T(8,128)(2,1)S(1)}, bf16[128,640]{1,0:T(8,128)(2,1)S(1)}, u32[]{:S(2)}, u32[]{:S(2)}) collective-permute-start(bf16[128,640]{1,0:T(8,128)(2,1)S(1)} %get-tuple-element.19), channel_id=1, source_target_pairs={{0,2},{1,3},{2,0},{3,1},{4,6},{5,7},{6,4},{7,5},{8,10},{9,11},{10,... | collective-permute-start | bytes 491528 | tf_op jit(solution)/shard_map/ppermute | solution.py:269
  173.7 9.0 %collective-permute-start.5 = (bf16[128,640]{1,0:T(8,128)(2,1)S(1)}, bf16[128,640]{1,0:T(8,128)(2,1)S(1)}, u32[]{:S(2)}, u32[]{:S(2)}) collective-permute-start(bf16[128,640]{1,0:T(8,128)(2,1)S(1)} %get-tuple-element.18), channel_id=1, source_target_pairs={{0,3},{1,2},{2,1},{3,0},{4,7},{5,6},{6,5},{7,4},{8,11},{9,10},{10,... | collective-permute-start | bytes 491528 | tf_op jit(solution)/shard_map/ppermute | solution.py:269
  184.0 4.8 %collective-permute-start.9 = (f32[128,128]{1,0:T(8,128)S(1)}, f32[128,128]{1,0:T(8,128)S(1)}, u32[]{:S(2)}, u32[]{:S(2)}) collective-permute-start(f32[128,128]{1,0:T(8,128)S(1)} %get-tuple-element.25), channel_id=1, source_target_pairs={{0,1},{1,0},{2,3},{3,2},{4,5},{5,4},{6,7},{7,6},{8,9},{9,8},{10,11... | collective-permute-start | bytes 196616 | tf_op jit(solution)/shard_map/ppermute | solution.py:269
  184.1 7.3 %collective-permute-start.10 = (f32[128,128]{1,0:T(8,128)S(1)}, f32[128,128]{1,0:T(8,128)S(1)}, u32[]{:S(2)}, u32[]{:S(2)}) collective-permute-start(f32[128,128]{1,0:T(8,128)S(1)} %get-tuple-element.24), channel_id=1, source_target_pairs={{0,2},{1,3},{2,0},{3,1},{4,6},{5,7},{6,4},{7,5},{8,10},{9,11},{10,... | collective-permute-start | bytes 196616 | tf_op jit(solution)/shard_map/ppermute | solution.py:269
  188.4 5.5 %collective-permute-start.11 = (f32[128,128]{1,0:T(8,128)S(1)}, f32[128,128]{1,0:T(8,128)S(1)}, u32[]{:S(2)}, u32[]{:S(2)}) collective-permute-start(f32[128,128]{1,0:T(8,128)S(1)} %get-tuple-element.22), channel_id=1, source_target_pairs={{0,3},{1,2},{2,1},{3,0},{4,7},{5,6},{6,5},{7,4},{8,11},{9,10},{10,... | collective-permute-start | bytes 196616 | tf_op jit(solution)/shard_map/ppermute | solution.py:269
  193.9 4.7 %collective-permute-start.13 = (f32[128,128]{1,0:T(8,128)S(1)}, f32[128,128]{1,0:T(8,128)S(1)}, u32[]{:S(2)}, u32[]{:S(2)}) collective-permute-start(f32[128,128]{1,0:T(8,128)S(1)} %fusion.3), channel_id=1, source_target_pairs={{0,8},{4,12},{8,0},{12,4},{16,24},{20,28},{24,16},{28,20},{32,40},... | collective-permute-start | bytes 196616 | tf_op jit(solution)/shard_map/ppermute | solution.py:269
  194.0 6.9 %collective-permute-start.14 = (f32[128,128]{1,0:T(8,128)S(1)}, f32[128,128]{1,0:T(8,128)S(1)}, u32[]{:S(2)}, u32[]{:S(2)}) collective-permute-start(f32[128,128]{1,0:T(8,128)S(1)} %fusion.3), channel_id=1, source_target_pairs={{0,12},{4,8},{8,4},{12,0},{16,28},{20,24},{24,20},{28,16},{32,44},... | collective-permute-start | bytes 196616 | tf_op jit(solution)/shard_map/ppermute | solution.py:269
  196.7 4.2 %collective-permute-start.12 = (f32[128,128]{1,0:T(8,128)S(1)}, f32[128,128]{1,0:T(8,128)S(1)}, u32[]{:S(2)}, u32[]{:S(2)}) collective-permute-start(f32[128,128]{1,0:T(8,128)S(1)} %fusion.3), channel_id=1, source_target_pairs={{0,4},{4,0},{8,12},{12,8},{16,20},{20,16},{24,28},{28,24},{32,36},... | collective-permute-start | bytes 196616 | tf_op jit(solution)/shard_map/ppermute | solution.py:269
  196.8 13.5 %collective-permute-start.8 = (f32[128,128]{1,0:T(8,128)S(1)}, f32[128,128]{1,0:T(8,128)S(1)}, u32[]{:S(2)}, u32[]{:S(2)}) collective-permute-start(f32[128,128]{1,0:T(8,128)S(1)} %get-tuple-element.23), channel_id=1, source_target_pairs={{0,3},{1,2},{2,1},{3,0},{4,7},{5,6},{6,5},{7,4},{8,11},{9,10},{10,... | collective-permute-start | bytes 196616 | tf_op jit(solution)/shard_map/ppermute | solution.py:269
  197.4 13.0 %collective-permute-start.7 = (f32[128,128]{1,0:T(8,128)S(1)}, f32[128,128]{1,0:T(8,128)S(1)}, u32[]{:S(2)}, u32[]{:S(2)}) collective-permute-start(f32[128,128]{1,0:T(8,128)S(1)} %get-tuple-element.23), channel_id=1, source_target_pairs={{0,2},{1,3},{2,0},{3,1},{4,6},{5,7},{6,4},{7,5},{8,10},{9,11},{10,... | collective-permute-start | bytes 196616 | tf_op jit(solution)/shard_map/ppermute | solution.py:269
  198.6 11.7 %collective-permute-start.6 = (f32[128,128]{1,0:T(8,128)S(1)}, f32[128,128]{1,0:T(8,128)S(1)}, u32[]{:S(2)}, u32[]{:S(2)}) collective-permute-start(f32[128,128]{1,0:T(8,128)S(1)} %get-tuple-element.23), channel_id=1, source_target_pairs={{0,1},{1,0},{2,3},{3,2},{4,5},{5,4},{6,7},{7,6},{8,9},{9,8},{10,11... | collective-permute-start | bytes 196616 | tf_op jit(solution)/shard_map/ppermute | solution.py:269
  200.9 10.4 %collective-permute-start.16 = (f32[128,128]{1,0:T(8,128)S(1)}, f32[128,128]{1,0:T(8,128)S(1)}, u32[]{:S(2)}, u32[]{:S(2)}) collective-permute-start(f32[128,128]{1,0:T(8,128)S(1)} %add_add_fusion.1), channel_id=1, source_target_pairs={{0,32},{4,36},{8,40},{12,44},{16,48},{20,52},{24,56},{28,60},{32,0... | collective-permute-start | bytes 196616 | tf_op jit(solution)/shard_map/ppermute | solution.py:269
  208.7 6.6 %collective-permute-start.17 = (f32[128,128]{1,0:T(8,128)S(1)}, f32[128,128]{1,0:T(8,128)S(1)}, u32[]{:S(2)}, u32[]{:S(2)}) collective-permute-start(f32[128,128]{1,0:T(8,128)S(1)} %add_add_fusion.1), channel_id=1, source_target_pairs={{0,48},{4,52},{8,56},{12,60},{16,32},{20,36},{24,40},{28,44},{32,1... | collective-permute-start | bytes 196616 | tf_op jit(solution)/shard_map/ppermute | solution.py:269
  210.3 5.2 %collective-permute-start.15 = (f32[128,128]{1,0:T(8,128)S(1)}, f32[128,128]{1,0:T(8,128)S(1)}, u32[]{:S(2)}, u32[]{:S(2)}) collective-permute-start(f32[128,128]{1,0:T(8,128)S(1)} %add_add_fusion.1), channel_id=1, source_target_pairs={{0,16},{4,20},{8,24},{12,28},{16,0},{20,4},{24,8},{28,12},{32,48},... | collective-permute-start | bytes 196616 | tf_op jit(solution)/shard_map/ppermute | solution.py:269
  215.5 6.0 %collective-permute-start.19 = (f32[128,128]{1,0:T(8,128)S(1)}, f32[128,128]{1,0:T(8,128)S(1)}, u32[]{:S(2)}, u32[]{:S(2)}) collective-permute-start(f32[128,128]{1,0:T(8,128)S(1)} %add_add_fusion), channel_id=1, source_target_pairs={{0,128},{4,132},{8,136},{12,140},{16,144},{20,148},{24,152},{28,15... | collective-permute-start | bytes 196616 | tf_op jit(solution)/shard_map/ppermute | solution.py:269
  215.7 6.2 %collective-permute-start.20 = (f32[128,128]{1,0:T(8,128)S(1)}, f32[128,128]{1,0:T(8,128)S(1)}, u32[]{:S(2)}, u32[]{:S(2)}) collective-permute-start(f32[128,128]{1,0:T(8,128)S(1)} %add_add_fusion), channel_id=1, source_target_pairs={{0,192},{4,196},{8,200},{12,204},{16,208},{20,212},{24,216},{28,22... | collective-permute-start | bytes 196616 | tf_op jit(solution)/shard_map/ppermute | solution.py:269
  216.1 5.8 %collective-permute-start.18 = (f32[128,128]{1,0:T(8,128)S(1)}, f32[128,128]{1,0:T(8,128)S(1)}, u32[]{:S(2)}, u32[]{:S(2)}) collective-permute-start(f32[128,128]{1,0:T(8,128)S(1)} %add_add_fusion), channel_id=1, source_target_pairs={{0,64},{4,68},{8,72},{12,76},{16,80},{20,84},{24,88},{28,92},{32,9... | collective-permute-start | bytes 196616 | tf_op jit(solution)/shard_map/ppermute | solution.py:269
  (3 other events, 2.1 us)
Sparse Core Ops, SparseCore 0:
  35.1 48.6 all-gather.2

commit v4 on v3

--- a/solution.py
+++ b/solution.py
@@ -13,24 +13,25 @@
 NEG = -1e30
 SLOTS = 2
 CHUNK = 4
-
-
-def route_kernel(owner, alive, obs, row_marks, pattern, first, second, marks, slots, info):
-    tiles = first.shape[0]
-    blocks, parts, quarter = obs.shape[:3]
+MARK_ROWS = 2
+
+
+def marks_kernel(owner, alive, row_marks, pattern, marks, slots, info, taken):
+    tiles = marks.shape[0]
+    blocks = row_marks.shape[0]
+    quarter = 32
+    j = owner[blocks]
+    turned = pltpu.roll(row_marks[...].astype(F32), (128 - j * quarter) % 128, 1)
     lane = lax.broadcasted_iota(jnp.int32, (blocks, 128), 1)
-    rows = row_marks[...].astype(F32)
     spot = lax.broadcasted_iota(jnp.int32, (pattern.shape[1], 128), 1)
     line = lax.broadcasted_iota(jnp.int32, (pattern.shape[1], 128), 0)
     shift = (spot == line + quarter).astype(F32).astype(BF)
     groups = jnp.dot(pattern[...].astype(F32).astype(BF), shift, preferred_element_type=F32)
-    for j in range(parts):
-        turned = rows if j == 0 else pltpu.roll(rows, 128 - j * quarter, 1)
-        info[j, :blocks] = jnp.where(lane < quarter, turned, groups)
-        info[j, blocks:] = jnp.zeros((8, 128), F32)
+    info[...] = jnp.where(lane < quarter, turned, groups)
+    marks[...] = jnp.zeros_like(marks)
 
     def clear(t, carry):
-        marks[t] = 0
+        taken[t] = 0
         slots[t] = blocks
         slots[tiles + t] = blocks
         return carry
@@ -42,45 +43,42 @@
 
         @pl.when(alive[b] > 0)
         def _():
-            k = jnp.minimum(marks[t], SLOTS - 1)
-            marks[t] = k + 1
+            k = jnp.minimum(taken[t], SLOTS - 1)
+            taken[t] = k + 1
             slots[k * tiles + t] = b
+            marks[t, pl.ds(k, 1), :] = info[pl.ds(b, 1), :]
 
         return carry
 
     lax.fori_loop(0, blocks, place, 0)
-    line8 = lax.broadcasted_iota(jnp.int32, (8, 128), 0)
+
+
+def pack_kernel(slots, obs, payload):
+    tiles = payload.shape[0]
+    blocks = obs.shape[0]
 
     def fill(t, carry):
-        b0 = slots[t]
-        b1 = slots[tiles + t]
-        for j in range(parts):
-            one = info[j, pl.ds(b0, 1), :]
-            two = info[j, pl.ds(b1, 1), :]
-            pair = jnp.where(line8 == 0, one, jnp.where(line8 == 1, two, 0.0))
-            first[t, j, quarter:quarter + 8, :] = pair.astype(BF)
-
-        @pl.when(b0 < blocks)
-        def _():
-            first[t, :, :quarter, :] = obs[b0]
-
-        @pl.when(b1 < blocks)
-        def _():
-            second[t] = obs[b1]
+        for k in range(SLOTS):
+            b = slots[k * tiles + t]
+
+            @pl.when(b < blocks)
+            def _():
+                payload[t, :, k] = obs[b]
 
         return carry
 
     lax.fori_loop(0, tiles, fill, 0)
 
 
-def lists_kernel(arrived, lists, bias):
-    tiles = arrived.shape[0]
-    quarter = arrived.shape[2] - 8
-    subs = lists.shape[1]
-    found = arrived[:, 0, quarter:quarter + 8, :].astype(F32)
+def lists_kernel(found, lists, bias):
+    tiles = found.shape[0]
+    slots = SLOTS * tiles
+    quarter = 32
+    subs = lists.shape[0]
+    mine = jnp.concatenate([found[:, k, :] for k in range(SLOTS)], axis=0).astype(BF)
     ahead = (
-        lax.broadcasted_iota(jnp.int32, (tiles, tiles), 0)
-        < lax.broadcasted_iota(jnp.int32, (tiles, tiles), 1)
+        lax.broadcasted_iota(jnp.int32, (slots, slots), 0)
+        < lax.broadcasted_iota(jnp.int32, (slots, slots), 1)
     ).astype(F32).astype(BF)
     pick_group = (
         lax.broadcasted_iota(jnp.int32, (subs, 128), 1)
@@ -89,21 +87,19 @@
     up = lax.broadcasted_iota(jnp.int32, (128, 128), 0)
     along = lax.broadcasted_iota(jnp.int32, (128, 128), 1)
     widen = ((up < quarter) & (up == along % quarter)).astype(F32).astype(BF)
-    turn = lax.broadcasted_iota(jnp.int32, (subs, 128, tiles), 1).astype(F32)
-    name = lax.broadcasted_iota(jnp.int32, (subs, 128, tiles), 2).astype(F32)
-    last = lax.broadcasted_iota(jnp.int32, (subs, 128), 1) == 127
-    for k in range(SLOTS):
-        mine = found[:, k, :].astype(BF)
-        live = lax.dot_general(
-            pick_group, mine, (((1,), (1,)), ((), ())), preferred_element_type=F32
-        )
-        place = jnp.dot(live.astype(BF), ahead, preferred_element_type=F32)
-        hit = (place[:, None, :] == turn) & (live[:, None, :] > 0.5)
-        order = jnp.sum(jnp.where(hit, name, 0.0), axis=2)
-        count = jnp.sum(live, axis=1, keepdims=True)
-        lists[k] = jnp.where(last, count, order).astype(jnp.int32)
-        rows = jnp.dot(mine, widen, preferred_element_type=F32)
-        bias[k] = (rows - 1.0) * (-NEG)
+    live = lax.dot_general(
+        pick_group, mine, (((1,), (1,)), ((), ())), preferred_element_type=F32
+    )
+    place = jnp.dot(live.astype(BF), ahead, preferred_element_type=F32)
+    turn = lax.broadcasted_iota(jnp.int32, (subs, slots, slots), 1).astype(F32)
+    name = lax.broadcasted_iota(jnp.int32, (subs, slots, slots), 2).astype(F32)
+    hit = (place[:, None, :] == turn) & (live[:, None, :] > 0.5)
+    order = jnp.sum(jnp.where(hit, name, 0.0), axis=2)
+    count = jnp.sum(live, axis=1, keepdims=True)
+    lists[:, :128] = order.astype(jnp.int32)
+    lists[:, 128:] = jnp.broadcast_to(count, (subs, 128)).astype(jnp.int32)
+    rows = jnp.dot(mine, widen, preferred_element_type=F32)
+    bias[...] = (rows - 1.0) * (-NEG)
 
 
 def split3(v):
@@ -122,8 +118,9 @@
     rows = heads * sub
     quarter = 32
     parts = x.shape[1]
-    cols = x.shape[3]
-    n = lists[g, 127]
+    cols = x.shape[4]
+    n = lists[g, 128]
+    tiles = x.shape[0]
     lane = lax.broadcasted_iota(jnp.int32, (sub, 128), 1)
     start = begun[...]
     tops = [jnp.broadcast_to(start[:, h:h + 1], (sub, 128)) for h in range(heads)]
@@ -166,7 +163,7 @@
                 s = lists[g, jnp.minimum(place, n - 1)]
                 for i in range(parts):
                     xbuf[u * quarter:(u + 1) * quarter, i * cols:(i + 1) * cols] = x[
-                        s, i, :quarter, :
+                        s % tiles, i, s // tiles
                     ]
                 live = (lane_slot == u) & (place < n)
                 shade = jnp.where(live, bias[pl.ds(s, 1), :], shade)
@@ -273,60 +270,61 @@
 
     tile = lax.axis_index("tile")
     whole = lambda *shape: pl.BlockSpec(shape, lambda g, *_: (0,) * len(shape))
-    depth = quarter + 8
-    first, second = pl.pallas_call(
-        route_kernel,
+    owners = jnp.concatenate([block_owner[:, 0], me[None].astype(jnp.int32)])
+    alive = jnp.max(block_pattern, axis=1)
+    marks, taken = pl.pallas_call(
+        marks_kernel,
         grid_spec=pltpu.PrefetchScalarGridSpec(
             num_scalar_prefetch=2,
             grid=(1,),
-            in_specs=[
-                whole(blocks, groups, quarter, cols),
-                whole(blocks, block_rows),
-                whole(blocks, subs),
-            ],
+            in_specs=[whole(blocks, block_rows), whole(blocks, subs)],
             out_specs=[
-                whole(tiles, groups, depth, cols),
-                whole(tiles, groups, quarter, cols),
+                whole(tiles, MARK_ROWS, 128),
+                pl.BlockSpec(memory_space=pltpu.SMEM),
             ],
             scratch_shapes=[
+                pltpu.VMEM((blocks, 128), F32),
                 pltpu.SMEM((tiles,), jnp.int32),
-                pltpu.SMEM((SLOTS * tiles,), jnp.int32),
-                pltpu.VMEM((groups, blocks + 8, 128), F32),
             ],
         ),
         out_shape=[
-            jax.ShapeDtypeStruct((tiles, groups, depth, cols), BF),
-            jax.ShapeDtypeStruct((tiles, groups, quarter, cols), BF),
+            jax.ShapeDtypeStruct((tiles, MARK_ROWS, 128), F32),
+            jax.ShapeDtypeStruct((SLOTS * tiles,), jnp.int32),
         ],
+        name="marks",
+    )(owners, alive, row_valid.reshape(blocks, block_rows), block_pattern)
+    marks = lax.all_to_all(marks, "tile", split_axis=0, concat_axis=0, tiled=True)
+    payload = pl.pallas_call(
+        pack_kernel,
+        grid_spec=pltpu.PrefetchScalarGridSpec(
+            num_scalar_prefetch=1,
+            grid=(1,),
+            in_specs=[whole(blocks, groups, quarter, cols)],
+            out_specs=whole(tiles, groups, SLOTS, quarter, cols),
+        ),
+        out_shape=jax.ShapeDtypeStruct((tiles, groups, SLOTS, quarter, cols), BF),
         compiler_params=pltpu.CompilerParams(vmem_limit_bytes=32 * 1024 * 1024),
-        name="route",
-    )(
-        block_owner[:, 0],
-        jnp.max(block_pattern, axis=1),
-        obs_feat.reshape(blocks, groups, quarter, cols),
-        row_valid.reshape(blocks, block_rows),
-        block_pattern,
-    )
-
-    def exchange(v):
-        flat = v.reshape((tiles * groups,) + v.shape[2:])
-        flat = lax.all_to_all(flat, ("tile", "head"), split_axis=0, concat_axis=0, tiled=True)
-        return flat.reshape(v.shape)
-
-    first = exchange(first)
-    second = exchange(second)
+        name="pack",
+    )(taken, obs_feat.reshape(blocks, groups, quarter, cols))
+    arrived = lax.all_to_all(
+        payload.reshape(tiles * groups, SLOTS, quarter, cols),
+        ("tile", "head"),
+        split_axis=0,
+        concat_axis=0,
+        tiled=True,
+    ).reshape(tiles, groups, SLOTS, quarter, cols)
 
     lists, bias = pl.pallas_call(
         lists_kernel,
         grid=(1,),
-        in_specs=[pl.BlockSpec((tiles, 1, depth, cols), lambda g: (0, 0, 0, 0))],
-        out_specs=[whole(SLOTS, subs, 128), whole(SLOTS, tiles, 128)],
+        in_specs=[whole(tiles, MARK_ROWS, 128)],
+        out_specs=[whole(subs, 256), whole(SLOTS * tiles, 128)],
         out_shape=[
-            jax.ShapeDtypeStruct((SLOTS, subs, 128), jnp.int32),
-            jax.ShapeDtypeStruct((SLOTS, tiles, 128), F32),
+            jax.ShapeDtypeStruct((subs, 256), jnp.int32),
+            jax.ShapeDtypeStruct((SLOTS * tiles, 128), F32),
         ],
         name="lists",
-    )(first)
+    )(marks)
 
     stacked = lax.all_gather(
         jnp.concatenate([w_query, w_key, w_value, w_out.T], axis=1), "head", axis=0
@@ -363,7 +361,7 @@
     )
     numer = jnp.dot(latent, wv, preferred_element_type=F32) * keep
 
-    def attend(k, x, numer, states, final):
+    def attend(x, numer, states, final):
         if final:
             out_specs = pl.BlockSpec((sub, width + 128), lambda g, *_: (g, 0))
             out_shape = jax.ShapeDtypeStruct((lat_rows, width + 128), BF)
@@ -383,7 +381,7 @@
                 grid=(subs,),
                 in_specs=[
                     whole(*x.shape),
-                    whole(tiles, 128),
+                    whole(SLOTS * tiles, 128),
                     pl.BlockSpec((heads, sub, width), lambda g, *_: (0, g, 0)),
                     pl.BlockSpec((sub, 128), lambda g, *_: (g, 0)),
                     pl.BlockSpec((sub, width), lambda g, *_: (g, 0)),
@@ -400,10 +398,9 @@
             out_shape=out_shape,
             compiler_params=pltpu.CompilerParams(vmem_limit_bytes=40 * 1024 * 1024),
             name="attend",
-        )(lists[k], x, bias[k], qw, states, numer, wv)
-
-    numer, states = attend(0, first, numer, states, False)
-    partial = attend(1, second, numer, states, True)
+        )(lists, x, bias, qw, states, numer, wv)
+
+    partial = attend(arrived, numer, states, True)
 
     partial = partial.reshape(groups, share, width + 128)
     received = [pick(partial, me)] + [

time: 231 us -> 227 us (0.983)
  local copies, waits for them, and re-layouts: 25.4 us -> 13.7 us
  waiting for transfers between devices: 93.3 us -> 102 us
  Pallas kernels: 31.6 us -> 28.6 us
    all_gather x1, waiting for transfers between devices: 0.01 us -> 39.4 us  [body(): lax.all_gather(jnp.concatenate([w_query, w_key, w_value, w_out.T], axis=1...]
    all_to_all x2, waiting for transfers between devices: 71.3 us -> 41.2 us  [the longest x1 38.4 us: body(): lax.all_to_all(payload.reshape(tiles * groups, SLOTS, quarter, cols), ('t...]
    unnamed x56 -> x40, local copies, waits for them, and re-layouts: 16.5 us -> 8.94 us
    pallas_call x2 -> x1, Pallas kernels: 24.1 us -> 19.6 us  [attend(): pl.pallas_call(functools.partial(attend_kernel, final), grid_spec=pltpu.P...]
    transpose x4, local copies, waits for them, and re-layouts: 5.76 us -> 3.18 us  [body(): stacked[:, :, a * 128:(a + 1) * 128].transpose(1, 0, 2)]
    pallas_call x2 -> x3, Pallas kernels: 6.26 us -> 7.67 us  [the longest x1 3.6 us: body(): pl.pallas_call(marks_kernel, grid_spec=pltpu.PrefetchScalarGridSpec(num_s...]
  transfers between devices with their start and end apart: 24 -> 24, of which waited for: 15 -> 16; matrix products, arithmetic and copies ran while one was open for 7% -> 5% of each run, Pallas kernels for 9% -> 2%
where the time goes in v4:
time: 227 us; the launch traced here: 224 us
  waiting for transfers between devices  102 us (45%)
  starting transfers between devices  55.2 us (24%)
  Pallas kernels  28.6 us (13%)
  between operations  14.4 us (6%)
  local copies, waits for them, and re-layouts  13.7 us (6%)
  other arithmetic  5.05 us (2%)
  matrix products  4.72 us (2%)
    all_gather x1, waiting for transfers between devices, body(): lax.all_gather(jnp.concatenate([w_query, w_key, w_value, w_out.T], axis=1...  39.4 us
    all_to_all x1, waiting for transfers between devices, body(): lax.all_to_all(payload.reshape(tiles * groups, SLOTS, quarter, cols), ('t...  38.4 us
    ppermute x21, starting transfers between devices, swap(): return lax.ppermute(v, axis, [(d, d ^ mask) for d in range(size)])  32.2 us
    ppermute x21, waiting for transfers between devices, swap(): return lax.ppermute(v, axis, [(d, d ^ mask) for d in range(size)])  21.7 us
    pallas_call x1, Pallas kernels, attend(): pl.pallas_call(functools.partial(attend_kernel, final), grid_spec=pltpu.P...  19.6 us
    all_to_all x1, starting transfers between devices, body(): lax.all_to_all(marks, 'tile', split_axis=0, concat_axis=0, tiled=True)  11.8 us
    all_to_all x1, starting transfers between devices, body(): lax.all_to_all(payload.reshape(tiles * groups, SLOTS, quarter, cols), ('t...  11.2 us
    unnamed x40, local copies, waits for them, and re-layouts  8.94 us
  transfers between devices with their start and end apart: 24, of which 16 were waited for; matrix products, arithmetic and copies ran while one was open for 5% of the time, Pallas kernels for 2%

profile of v4, /device:TPU:32, one launch (start us, length us, event | category | flops | bytes accessed | tf_op | source)
XLA Modules:
  0.0 223.9 jit_solution(2206996350697924598)
XLA Ops:
  7.2 1.4 copy.54.pattern
  8.6 1.3 reduce_max.9.alive
  9.9 1.2 pad_add_fusion.owner
  11.1 3.6 %marks.1 = (f32[64,2,128]{2,1,0:T(2,128)}, s32[128]{0:T(128)}) custom-call(s32[65]{0:T(128)} %pad_add_fusion.owner, s32[64]{0:T(128)} %reduce_max.9.alive, s32[64,128]{1,0:T(8,128)} %bitcast.96, s32[64,16]{1,0:T(8,128)} %copy.54.pattern), custom_call_target="tpu_custom_call" | custom-call | tf_op jit(solution)/shard_map/marks/pallas_call | solution.py:275
  14.7 11.8 %all-to-all-start = ((f32[64,2,128]{2,1,0:T(2,128)}), f32[64,2,128]{2,1,0:T(2,128)S(1)}, u32[]{:S(2)}, u32[]{:S(2)}) async-start(f32[64,2,128]{2,1,0:T(2,128)} %get-tuple-element.6), calls=%async_computation | async-start | bytes 131072 | tf_op jit(solution)/shard_map/all_to_all | solution.py:296
  26.5 1.6 copy-done.3
  28.0 0.6 copy-done.9
  28.6 2.0 pack.1
  30.6 2.0 copy-done.1
  32.6 2.8 %all-to-all-done.found = f32[64,2,128]{2,1,0:T(2,128)S(1)} async-done(((f32[64,2,128]{2,1,0:T(2,128)}), f32[64,2,128]{2,1,0:T(2,128)S(1)}, u32[]{:S(2)}, u32[]{:S(2)}) %all-to-all-start) | async-done | bytes 65568 | tf_op jit(solution)/shard_map/all_to_all | solution.py:296
  35.4 0.6 copy-done.13
  36.0 11.2 %all-to-all-start.1 = ((bf16[256,2,32,128]{3,2,1,0:T(8,128)(2,1)}), bf16[256,2,32,128]{3,2,1,0:T(8,128)(2,1)}, u32[]{:S(2)}, u32[]{:S(2)}) async-start(bf16[256,2,32,128]{3,2,1,0:T(8,128)(2,1)} %bitcast.81), calls=%async_computation.1 | async-start | bytes 8388608 | tf_op jit(solution)/shard_map/all_to_all | solution.py:309
  47.4 0.9 pad_maximum_fusion
  48.3 2.8 %collective-permute-start.2 = (f32[2]{0:T(128)S(1)}, f32[2]{0:T(128)S(1)}, u32[]{:S(2)}, u32[]{:S(2)}) collective-permute-start(f32[2]{0:T(128)S(1)} %copy-done.18), channel_id=1, source_target_pairs={{0,3},{1,2},{2,1},{3,0},{4,7},{5,6},{6,5},{7,4},{8,11},{9,10},{10,... | collective-permute-start | bytes 32 | tf_op jit(solution)/shard_map/ppermute | solution.py:266
  51.1 0.8 collective-permute-start.1
  52.5 3.4 %collective-permute-done.2 = f32[2]{0:T(128)S(1)} collective-permute-done((f32[2]{0:T(128)S(1)}, f32[2]{0:T(128)S(1)}, u32[]{:S(2)}, u32[]{:S(2)}) %collective-permute-start.2) | collective-permute-done | bytes 40 | tf_op jit(solution)/shard_map/ppermute | solution.py:266
  56.9 2.1 lists.1
  59.0 39.4 %all-gather.3.cloned.1.call-done = bf16[2048,512]{1,0:T(8,128)(2,1)} async-done(((bf16[512,512]{1,0:T(8,128)(2,1)}), bf16[2048,512]{1,0:T(8,128)(2,1)}) %all-gather.3.cloned.1.call-update) | async-done | bytes 2097168 | tf_op jit(solution)/shard_map/all_gather | solution.py:329
  98.4 2.5 %slice_bitcast_fusion = (bf16[512,4,128]{2,0,1:T(8,128)(2,1)}, bf16[4,64,8,128]{3,2,1,0:T(8,128)(2,1)S(1)}, bf16[512,4,128]{2,0,1:T(8,128)(2,1)S(1)}, bf16[512,4,128]{2,0,1:T(8,128)(2,1)S(1)}) fusion(bf16[4,512,512]{2,1,0:T(8,128)(2,1)} %bitcast.91), kind=kLoop, calls=%fused_computation.10 | loop fusion | bytes 4194304 | tf_op jit(solution)/shard_map/transpose | solution.py:333
  103.6 3.3 %multiply_convert_fusion.qw = bf16[8,512,512]{2,1,0:T(8,128)(2,1)} fusion(bf16[512,8,64]{0,2,1:T(8,128)(2,1)S(1)} %bitcast.87, bf16[512,8,64]{0,2,1:T(8,128)(2,1)S(1)} %bitcast.89), kind=kOutput, calls=%fused_computation.2 | convolution fusion | flops 272629760 | bytes 5242880 | tf_op jit(solution)/shard_map/lhd,khd->hlk/dot_general | solution.py:348
  106.9 38.4 %all-to-all-done.1 = bf16[256,2,32,128]{3,2,1,0:T(8,128)(2,1)} async-done(((bf16[256,2,32,128]{3,2,1,0:T(8,128)(2,1)}), bf16[256,2,32,128]{3,2,1,0:T(8,128)(2,1)}, u32[]{:S(2)}, u32[]{:S(2)}) %all-to-all-start.1) | async-done | bytes 4194336 | tf_op jit(solution)/shard_map/all_to_all | solution.py:309
  145.3 2.2 copy-done
  147.5 19.6 %attend.1 = bf16[512,640]{1,0:T(8,128)(2,1)S(1)} custom-call(s32[16,256]{1,0:T(8,128)S(1)} %copy-done.7, bf16[64,4,2,32,128]{4,3,2,1,0:T(8,128)(2,1)} %bitcast.6.x, f32[128,128]{1,0:T(8,128)S(1)} %copy-done.6, bf16[8,512,512]{2,1,0:T(8,128)(2,1)S(1)} %copy-done, f32[512,128]{1,0:T(8,128)S(1)} %pad_select_fusion.begun, f32[512,512]{1,0:T(8,128)S(1)} %fusion.given, ...), custom_call_target="tpu_custom_call" | custom-call | tf_op jit(solution)/shard_map/attend/pallas_call | solution.py:377
  167.2 0.7 collective-permute-start.3
  167.9 1.1 collective-permute-start.4
  169.0 3.0 %collective-permute-start.5 = (bf16[128,640]{1,0:T(8,128)(2,1)S(1)}, bf16[128,640]{1,0:T(8,128)(2,1)S(1)}, u32[]{:S(2)}, u32[]{:S(2)}) collective-permute-start(bf16[128,640]{1,0:T(8,128)(2,1)S(1)} %get-tuple-element.14), channel_id=1, source_target_pairs={{0,3},{1,2},{2,1},{3,0},{4,7},{5,6},{6,5},{7,4},{8,11},{9,10},{10,... | collective-permute-start | bytes 491528 | tf_op jit(solution)/shard_map/ppermute | solution.py:266
  172.2 1.2 collective-permute-done.3.r1
  173.4 2.6 %collective-permute-done.4.r2 = bf16[128,640]{1,0:T(8,128)(2,1)S(1)} collective-permute-done((bf16[128,640]{1,0:T(8,128)(2,1)S(1)}, bf16[128,640]{1,0:T(8,128)(2,1)S(1)}, u32[]{:S(2)}, u32[]{:S(2)}) %collective-permute-start.4) | collective-permute-done | bytes 163872 | tf_op jit(solution)/shard_map/ppermute | solution.py:266
  175.9 2.1 collective-permute-done.5.r3
  178.0 1.3 finish.1
  179.6 3.0 %collective-permute-start.10 = (f32[128,128]{1,0:T(8,128)S(1)}, f32[128,128]{1,0:T(8,128)S(1)}, u32[]{:S(2)}, u32[]{:S(2)}) collective-permute-start(f32[128,128]{1,0:T(8,128)S(1)} %get-tuple-element.20), channel_id=1, source_target_pairs={{0,2},{1,3},{2,0},{3,1},{4,6},{5,7},{6,4},{7,5},{8,10},{9,11},{10,... | collective-permute-start | bytes 196616 | tf_op jit(solution)/shard_map/ppermute | solution.py:266
  182.6 1.7 collective-permute-start.11
  184.3 1.2 collective-permute-done.10
  185.6 2.5 %collective-permute-done.11 = f32[128,128]{1,0:T(8,128)S(1)} collective-permute-done((f32[128,128]{1,0:T(8,128)S(1)}, f32[128,128]{1,0:T(8,128)S(1)}, u32[]{:S(2)}, u32[]{:S(2)}) %collective-permute-start.11) | collective-permute-done | bytes 65568 | tf_op jit(solution)/shard_map/ppermute | solution.py:266
  188.1 7.6 %collective-permute-start.13 = (f32[128,128]{1,0:T(8,128)S(1)}, f32[128,128]{1,0:T(8,128)S(1)}, u32[]{:S(2)}, u32[]{:S(2)}) collective-permute-start(f32[128,128]{1,0:T(8,128)S(1)} %fusion.3), channel_id=1, source_target_pairs={{0,8},{4,12},{8,0},{12,4},{16,24},{20,28},{24,16},{28,20},{32,40},... | collective-permute-start | bytes 196616 | tf_op jit(solution)/shard_map/ppermute | solution.py:266
  196.0 0.9 collective-permute-start.8
  197.1 1.7 collective-permute-done.13
  198.8 1.3 collective-permute-start.6
  200.4 2.1 collective-permute-done.8
  202.5 4.3 %collective-permute-start.15 = (f32[128,128]{1,0:T(8,128)S(1)}, f32[128,128]{1,0:T(8,128)S(1)}, u32[]{:S(2)}, u32[]{:S(2)}) collective-permute-start(f32[128,128]{1,0:T(8,128)S(1)} %add_add_fusion.1), channel_id=1, source_target_pairs={{0,16},{4,20},{8,24},{12,28},{16,0},{20,4},{24,8},{28,12},{32,48},... | collective-permute-start | bytes 196616 | tf_op jit(solution)/shard_map/ppermute | solution.py:266
  206.8 0.6 gather_fusion.1
  207.4 1.1 collective-permute-done.16
  208.5 0.7 collective-permute-done.15
  209.2 1.7 collective-permute-start.19
  210.8 1.9 collective-permute-start.18
  212.8 0.8 bitcast_select_fusion
  213.6 2.2 collective-permute-done.19
  216.4 0.6 add_multiply_fusion
  (79 shorter events, 6.2 us)
Async XLA Ops:
  14.7 20.7 %all-to-all-start = ((f32[64,2,128]{2,1,0:T(2,128)}), f32[64,2,128]{2,1,0:T(2,128)S(1)}, u32[]{:S(2)}, u32[]{:S(2)}) async-start(f32[64,2,128]{2,1,0:T(2,128)} %get-tuple-element.6), calls=%async_computation | async-start | bytes 131072 | tf_op jit(solution)/shard_map/all_to_all | solution.py:296
  26.4 1.6 copy-start.3
  28.0 0.6 copy-start.9
  30.6 2.0 copy-start.1
  35.4 0.6 copy-start.13
  35.4 11.9 %copy-start.14 = (bf16[128,512]{1,0:T(8,128)(2,1)S(1)}, bf16[128,512]{1,0:T(8,128)(2,1)}, u32[]{:S(2)}) copy-start(bf16[128,512]{1,0:T(8,128)(2,1)} %param.22) | copy-start | bytes 393220
  35.4 12.0 %copy-start.15 = (bf16[512,128]{1,0:T(8,128)(2,1)S(1)}, bf16[512,128]{1,0:T(8,128)(2,1)}, u32[]{:S(2)}) copy-start(bf16[512,128]{1,0:T(8,128)(2,1)} %param.20) | copy-start | bytes 393220
  35.4 12.0 %copy-start.16 = (bf16[512,128]{1,0:T(8,128)(2,1)S(1)}, bf16[512,128]{1,0:T(8,128)(2,1)}, u32[]{:S(2)}) copy-start(bf16[512,128]{1,0:T(8,128)(2,1)} %param.19) | copy-start | bytes 393220
  35.4 12.0 %copy-start.17 = (bf16[512,128]{1,0:T(8,128)(2,1)S(1)}, bf16[512,128]{1,0:T(8,128)(2,1)}, u32[]{:S(2)}) copy-start(bf16[512,128]{1,0:T(8,128)(2,1)} %param.18) | copy-start | bytes 393220
  35.4 12.9 %copy-start.18 = (f32[2]{0:T(128)S(1)}, f32[2]{0:T(128)}, u32[]{:S(2)}) copy-start(f32[2]{0:T(128)} %param.21) | copy-start | bytes 28
  36.0 109.3 %all-to-all-start.1 = ((bf16[256,2,32,128]{3,2,1,0:T(8,128)(2,1)}), bf16[256,2,32,128]{3,2,1,0:T(8,128)(2,1)}, u32[]{:S(2)}, u32[]{:S(2)}) async-start(bf16[256,2,32,128]{3,2,1,0:T(8,128)(2,1)} %bitcast.81), calls=%async_computation.1 | async-start | bytes 8388608 | tf_op jit(solution)/shard_map/all_to_all | solution.py:309
  47.2 54.2 %copy-start.2 = (bf16[512,512]{1,0:T(8,128)(2,1)S(1)}, bf16[512,512]{1,0:T(8,128)(2,1)}, u32[]{:S(2)}) copy-start(bf16[512,512]{1,0:T(8,128)(2,1)} %lat.1) | copy-start | bytes 1572868
  47.2 51.2 %all-gather.3.cloned.1.call-start = ((), (), s32[]{:S(2)}) async-start(), calls=%async_computation.2 | async-start | bytes 2621440 | tf_op jit(solution)/shard_map/all_gather | solution.py:329
  48.3 7.6 %collective-permute-start.2 = (f32[2]{0:T(128)S(1)}, f32[2]{0:T(128)S(1)}, u32[]{:S(2)}, u32[]{:S(2)}) collective-permute-start(f32[2]{0:T(128)S(1)} %copy-done.18), channel_id=1, source_target_pairs={{0,3},{1,2},{2,1},{3,0},{4,7},{5,6},{6,5},{7,4},{8,11},{9,10},{10,... | collective-permute-start | bytes 32 | tf_op jit(solution)/shard_map/ppermute | solution.py:266
  51.1 5.0 %collective-permute-start.1 = (f32[2]{0:T(128)S(1)}, f32[2]{0:T(128)S(1)}, u32[]{:S(2)}, u32[]{:S(2)}) collective-permute-start(f32[2]{0:T(128)S(1)} %copy-done.18), channel_id=1, source_target_pairs={{0,2},{1,3},{2,0},{3,1},{4,6},{5,7},{6,4},{7,5},{8,10},{9,11},{10,... | collective-permute-start | bytes 32 | tf_op jit(solution)/shard_map/ppermute | solution.py:266
  52.0 4.2 %collective-permute-start = (f32[2]{0:T(128)S(1)}, f32[2]{0:T(128)S(1)}, u32[]{:S(2)}, u32[]{:S(2)}) collective-permute-start(f32[2]{0:T(128)S(1)} %copy-done.18), channel_id=1, source_target_pairs={{0,1},{1,0},{2,3},{3,2},{4,5},{5,4},{6,7},{7,6},{8,9},{9,8},{10,11... | collective-permute-start | bytes 32 | tf_op jit(solution)/shard_map/ppermute | solution.py:266
  101.4 1.1 copy-start.10
  102.5 1.0 copy-start.11
  102.6 42.7 %copy-start.6 = (f32[128,128]{1,0:T(8,128)S(1)}, f32[128,128]{1,0:T(8,128)}, u32[]{:S(2)}) copy-start(f32[128,128]{1,0:T(8,128)} %get-tuple-element.9.bias) | copy-start | bytes 196612
  102.6 42.7 %copy-start.7 = (s32[16,256]{1,0:T(8,128)S(1)}, s32[16,256]{1,0:T(8,128)}, u32[]{:S(2)}) copy-start(s32[16,256]{1,0:T(8,128)} %get-tuple-element.7.lists) | copy-start | bytes 49156
  145.3 2.2 copy-start
  147.5 24.5 %copy-start.12 = (bf16[512,4,128]{2,0,1:T(8,128)(2,1)S(1)}, bf16[512,4,128]{2,0,1:T(8,128)(2,1)}, u32[]{:S(2)}) copy-start(bf16[512,4,128]{2,0,1:T(8,128)(2,1)} %get-tuple-element.10) | copy-start | bytes 1572868
  147.5 30.5 %copy-start.4 = (bf16[512,128]{1,0:T(8,128)(2,1)S(1)}, bf16[512,128]{1,0:T(8,128)(2,1)}, u32[]{:S(2)}) copy-start(bf16[512,128]{1,0:T(8,128)(2,1)} %w_inc.1) | copy-start | bytes 393220
  147.5 30.5 %copy-start.5 = (bf16[512,128]{1,0:T(8,128)(2,1)S(1)}, bf16[512,128]{1,0:T(8,128)(2,1)}, u32[]{:S(2)}) copy-start(bf16[512,128]{1,0:T(8,128)(2,1)} %target.1) | copy-start | bytes 393220
  147.5 30.5 %copy-start.8 = (f32[512]{0:T(512)S(1)}, f32[512]{0:T(512)}, u32[]{:S(2)}) copy-start(f32[512]{0:T(512)} %param.23) | copy-start | bytes 6148
  167.2 6.2 %collective-permute-start.3 = (bf16[128,640]{1,0:T(8,128)(2,1)S(1)}, bf16[128,640]{1,0:T(8,128)(2,1)S(1)}, u32[]{:S(2)}, u32[]{:S(2)}) collective-permute-start(bf16[128,640]{1,0:T(8,128)(2,1)S(1)} %get-tuple-element.16), channel_id=1, source_target_pairs={{0,1},{1,0},{2,3},{3,2},{4,5},{5,4},{6,7},{7,6},{8,9},{9,8},{10,11... | collective-permute-start | bytes 491528 | tf_op jit(solution)/shard_map/ppermute | solution.py:266
  167.9 8.1 %collective-permute-start.4 = (bf16[128,640]{1,0:T(8,128)(2,1)S(1)}, bf16[128,640]{1,0:T(8,128)(2,1)S(1)}, u32[]{:S(2)}, u32[]{:S(2)}) collective-permute-start(bf16[128,640]{1,0:T(8,128)(2,1)S(1)} %get-tuple-element.15), channel_id=1, source_target_pairs={{0,2},{1,3},{2,0},{3,1},{4,6},{5,7},{6,4},{7,5},{8,10},{9,11},{10,... | collective-permute-start | bytes 491528 | tf_op jit(solution)/shard_map/ppermute | solution.py:266
  169.0 9.0 %collective-permute-start.5 = (bf16[128,640]{1,0:T(8,128)(2,1)S(1)}, bf16[128,640]{1,0:T(8,128)(2,1)S(1)}, u32[]{:S(2)}, u32[]{:S(2)}) collective-permute-start(bf16[128,640]{1,0:T(8,128)(2,1)S(1)} %get-tuple-element.14), channel_id=1, source_target_pairs={{0,3},{1,2},{2,1},{3,0},{4,7},{5,6},{6,5},{7,4},{8,11},{9,10},{10,... | collective-permute-start | bytes 491528 | tf_op jit(solution)/shard_map/ppermute | solution.py:266
  179.4 5.0 %collective-permute-start.9 = (f32[128,128]{1,0:T(8,128)S(1)}, f32[128,128]{1,0:T(8,128)S(1)}, u32[]{:S(2)}, u32[]{:S(2)}) collective-permute-start(f32[128,128]{1,0:T(8,128)S(1)} %get-tuple-element.21), channel_id=1, source_target_pairs={{0,1},{1,0},{2,3},{3,2},{4,5},{5,4},{6,7},{7,6},{8,9},{9,8},{10,11... | collective-permute-start | bytes 196616 | tf_op jit(solution)/shard_map/ppermute | solution.py:266
  179.6 5.9 %collective-permute-start.10 = (f32[128,128]{1,0:T(8,128)S(1)}, f32[128,128]{1,0:T(8,128)S(1)}, u32[]{:S(2)}, u32[]{:S(2)}) collective-permute-start(f32[128,128]{1,0:T(8,128)S(1)} %get-tuple-element.20), channel_id=1, source_target_pairs={{0,2},{1,3},{2,0},{3,1},{4,6},{5,7},{6,4},{7,5},{8,10},{9,11},{10,... | collective-permute-start | bytes 196616 | tf_op jit(solution)/shard_map/ppermute | solution.py:266
  182.6 5.5 %collective-permute-start.11 = (f32[128,128]{1,0:T(8,128)S(1)}, f32[128,128]{1,0:T(8,128)S(1)}, u32[]{:S(2)}, u32[]{:S(2)}) collective-permute-start(f32[128,128]{1,0:T(8,128)S(1)} %get-tuple-element.18), channel_id=1, source_target_pairs={{0,3},{1,2},{2,1},{3,0},{4,7},{5,6},{6,5},{7,4},{8,11},{9,10},{10,... | collective-permute-start | bytes 196616 | tf_op jit(solution)/shard_map/ppermute | solution.py:266
  188.1 10.7 %collective-permute-start.13 = (f32[128,128]{1,0:T(8,128)S(1)}, f32[128,128]{1,0:T(8,128)S(1)}, u32[]{:S(2)}, u32[]{:S(2)}) collective-permute-start(f32[128,128]{1,0:T(8,128)S(1)} %fusion.3), channel_id=1, source_target_pairs={{0,8},{4,12},{8,0},{12,4},{16,24},{20,28},{24,16},{28,20},{32,40},... | collective-permute-start | bytes 196616 | tf_op jit(solution)/shard_map/ppermute | solution.py:266
  195.8 4.4 %collective-permute-start.14 = (f32[128,128]{1,0:T(8,128)S(1)}, f32[128,128]{1,0:T(8,128)S(1)}, u32[]{:S(2)}, u32[]{:S(2)}) collective-permute-start(f32[128,128]{1,0:T(8,128)S(1)} %fusion.3), channel_id=1, source_target_pairs={{0,12},{4,8},{8,4},{12,0},{16,28},{20,24},{24,20},{28,16},{32,44},... | collective-permute-start | bytes 196616 | tf_op jit(solution)/shard_map/ppermute | solution.py:266
  195.8 4.4 %collective-permute-start.12 = (f32[128,128]{1,0:T(8,128)S(1)}, f32[128,128]{1,0:T(8,128)S(1)}, u32[]{:S(2)}, u32[]{:S(2)}) collective-permute-start(f32[128,128]{1,0:T(8,128)S(1)} %fusion.3), channel_id=1, source_target_pairs={{0,4},{4,0},{8,12},{12,8},{16,20},{20,16},{24,28},{28,24},{32,36},... | collective-permute-start | bytes 196616 | tf_op jit(solution)/shard_map/ppermute | solution.py:266
  196.0 6.5 %collective-permute-start.8 = (f32[128,128]{1,0:T(8,128)S(1)}, f32[128,128]{1,0:T(8,128)S(1)}, u32[]{:S(2)}, u32[]{:S(2)}) collective-permute-start(f32[128,128]{1,0:T(8,128)S(1)} %get-tuple-element.19), channel_id=1, source_target_pairs={{0,3},{1,2},{2,1},{3,0},{4,7},{5,6},{6,5},{7,4},{8,11},{9,10},{10,... | collective-permute-start | bytes 196616 | tf_op jit(solution)/shard_map/ppermute | solution.py:266
  196.9 9.8 %collective-permute-start.7 = (f32[128,128]{1,0:T(8,128)S(1)}, f32[128,128]{1,0:T(8,128)S(1)}, u32[]{:S(2)}, u32[]{:S(2)}) collective-permute-start(f32[128,128]{1,0:T(8,128)S(1)} %get-tuple-element.19), channel_id=1, source_target_pairs={{0,2},{1,3},{2,0},{3,1},{4,6},{5,7},{6,4},{7,5},{8,10},{9,11},{10,... | collective-permute-start | bytes 196616 | tf_op jit(solution)/shard_map/ppermute | solution.py:266
  198.8 7.9 %collective-permute-start.6 = (f32[128,128]{1,0:T(8,128)S(1)}, f32[128,128]{1,0:T(8,128)S(1)}, u32[]{:S(2)}, u32[]{:S(2)}) collective-permute-start(f32[128,128]{1,0:T(8,128)S(1)} %get-tuple-element.19), channel_id=1, source_target_pairs={{0,1},{1,0},{2,3},{3,2},{4,5},{5,4},{6,7},{7,6},{8,9},{9,8},{10,11... | collective-permute-start | bytes 196616 | tf_op jit(solution)/shard_map/ppermute | solution.py:266
  200.2 8.3 %collective-permute-start.16 = (f32[128,128]{1,0:T(8,128)S(1)}, f32[128,128]{1,0:T(8,128)S(1)}, u32[]{:S(2)}, u32[]{:S(2)}) collective-permute-start(f32[128,128]{1,0:T(8,128)S(1)} %add_add_fusion.1), channel_id=1, source_target_pairs={{0,32},{4,36},{8,40},{12,44},{16,48},{20,52},{24,56},{28,60},{32,0... | collective-permute-start | bytes 196616 | tf_op jit(solution)/shard_map/ppermute | solution.py:266
  200.3 8.2 %collective-permute-start.17 = (f32[128,128]{1,0:T(8,128)S(1)}, f32[128,128]{1,0:T(8,128)S(1)}, u32[]{:S(2)}, u32[]{:S(2)}) collective-permute-start(f32[128,128]{1,0:T(8,128)S(1)} %add_add_fusion.1), channel_id=1, source_target_pairs={{0,48},{4,52},{8,56},{12,60},{16,32},{20,36},{24,40},{28,44},{32,1... | collective-permute-start | bytes 196616 | tf_op jit(solution)/shard_map/ppermute | solution.py:266
  202.5 6.6 %collective-permute-start.15 = (f32[128,128]{1,0:T(8,128)S(1)}, f32[128,128]{1,0:T(8,128)S(1)}, u32[]{:S(2)}, u32[]{:S(2)}) collective-permute-start(f32[128,128]{1,0:T(8,128)S(1)} %add_add_fusion.1), channel_id=1, source_target_pairs={{0,16},{4,20},{8,24},{12,28},{16,0},{20,4},{24,8},{28,12},{32,48},... | collective-permute-start | bytes 196616 | tf_op jit(solution)/shard_map/ppermute | solution.py:266
  209.2 6.6 %collective-permute-start.19 = (f32[128,128]{1,0:T(8,128)S(1)}, f32[128,128]{1,0:T(8,128)S(1)}, u32[]{:S(2)}, u32[]{:S(2)}) collective-permute-start(f32[128,128]{1,0:T(8,128)S(1)} %add_add_fusion), channel_id=1, source_target_pairs={{0,128},{4,132},{8,136},{12,140},{16,144},{20,148},{24,152},{28,15... | collective-permute-start | bytes 196616 | tf_op jit(solution)/shard_map/ppermute | solution.py:266
  210.8 5.5 %collective-permute-start.20 = (f32[128,128]{1,0:T(8,128)S(1)}, f32[128,128]{1,0:T(8,128)S(1)}, u32[]{:S(2)}, u32[]{:S(2)}) collective-permute-start(f32[128,128]{1,0:T(8,128)S(1)} %add_add_fusion), channel_id=1, source_target_pairs={{0,192},{4,196},{8,200},{12,204},{16,208},{20,212},{24,216},{28,22... | collective-permute-start | bytes 196616 | tf_op jit(solution)/shard_map/ppermute | solution.py:266
  210.8 5.5 %collective-permute-start.18 = (f32[128,128]{1,0:T(8,128)S(1)}, f32[128,128]{1,0:T(8,128)S(1)}, u32[]{:S(2)}, u32[]{:S(2)}) collective-permute-start(f32[128,128]{1,0:T(8,128)S(1)} %add_add_fusion), channel_id=1, source_target_pairs={{0,64},{4,68},{8,72},{12,76},{16,80},{20,84},{24,88},{28,92},{32,9... | collective-permute-start | bytes 196616 | tf_op jit(solution)/shard_map/ppermute | solution.py:266
Sparse Core Ops, SparseCore 0:
  49.9 48.4 all-gather.2

commit v5 on v4

v5 whole, which is shorter than its diff:
```python
import math

import jax
import jax.numpy as jnp
from jax import lax
from jax.experimental import pallas as pl
from jax.experimental.pallas import tpu as pltpu
from jax.sharding import PartitionSpec as P

BF = jnp.bfloat16
F32 = jnp.float32
NEG = -1e30
SLOTS = 2
CHUNK = 8
PAIR = 2
MARK_ROWS = 2


def marks_kernel(owner, row_marks, pattern, marks, slots, info, taken):
    tiles = marks.shape[0]
    blocks = row_marks.shape[0]
    subs = pattern.shape[0]
    quarter = 32
    j = lax.axis_index("head")
    turned = pltpu.roll(row_marks[...].astype(F32), (128 - j * quarter) % 128, 1)
    lane = lax.broadcasted_iota(jnp.int32, (blocks, 128), 1)
    spot = lax.broadcasted_iota(jnp.int32, (subs, 128), 1)
    line = lax.broadcasted_iota(jnp.int32, (subs, 128), 0)
    shift = (spot == line + quarter).astype(F32).astype(BF)
    groups = lax.dot_general(
        pattern[...].astype(F32).astype(BF),
        shift,
        (((0,), (0,)), ((), ())),
        preferred_element_type=F32,
    )
    info[...] = jnp.where(lane < quarter, turned, groups)
    marks[...] = jnp.zeros_like(marks)

    def clear(t, carry):
        taken[t] = 0
        slots[t] = blocks
        slots[tiles + t] = blocks
        return carry

    lax.fori_loop(0, tiles, clear, 0, unroll=8)

    def place(b, carry):
        t = owner[b]
        k = jnp.minimum(taken[t], SLOTS - 1)
        taken[t] = k + 1
        slots[k * tiles + t] = b
        marks[t, pl.ds(k, 1), :] = info[pl.ds(b, 1), :]
        return carry

    lax.fori_loop(0, blocks, place, 0, unroll=4)


def pack_kernel(slots, obs, payload):
    tiles = payload.shape[0]
    blocks = obs.shape[0]

    def fill(t, carry):
        for k in range(SLOTS):
            b = slots[k * tiles + t]

            @pl.when(b < blocks)
            def _():
                payload[t, :, k] = obs[b]

            @pl.when(b >= blocks)
            def _():
                payload[t, :, k] = jnp.zeros(obs.shape[1:], BF)

        return carry

    lax.fori_loop(0, tiles, fill, 0)


def lists_kernel(found, lists, bias):
    tiles = found.shape[0]
    slots = SLOTS * tiles
    quarter = 32
    subs = lists.shape[0]
    mine = jnp.concatenate([found[:, k, :] for k in range(SLOTS)], axis=0).astype(BF)
    ahead = (
        lax.broadcasted_iota(jnp.int32, (slots, slots), 0)
        < lax.broadcasted_iota(jnp.int32, (slots, slots), 1)
    ).astype(F32).astype(BF)
    pick_group = (
        lax.broadcasted_iota(jnp.int32, (subs, 128), 1)
        == lax.broadcasted_iota(jnp.int32, (subs, 128), 0) + quarter
    ).astype(F32).astype(BF)
    up = lax.broadcasted_iota(jnp.int32, (128, 128), 0)
    along = lax.broadcasted_iota(jnp.int32, (128, 128), 1)
    widen = ((up < quarter) & (up == along % quarter)).astype(F32).astype(BF)
    live = lax.dot_general(
        pick_group, mine, (((1,), (1,)), ((), ())), preferred_element_type=F32
    )
    place = jnp.dot(live.astype(BF), ahead, preferred_element_type=F32)
    turn = lax.broadcasted_iota(jnp.int32, (subs, slots, slots), 1).astype(F32)
    name = lax.broadcasted_iota(jnp.int32, (subs, slots, slots), 2).astype(F32)
    hit = (place[:, None, :] == turn) & (live[:, None, :] > 0.5)
    order = jnp.sum(jnp.where(hit, name, 0.0), axis=2)
    count = jnp.sum(live, axis=1, keepdims=True)
    lists[:, :128] = order.astype(jnp.int32)
    lists[:, 128:] = jnp.broadcast_to(count, (subs, 128)).astype(jnp.int32)
    rows = jnp.dot(mine, widen, preferred_element_type=F32)
    bias[...] = (rows - 1.0) * (-NEG)


def split3(v):
    hi = v.astype(BF).astype(F32)
    mid = (v - hi).astype(BF).astype(F32)
    return hi, mid, v - hi - mid


def attend_kernel(lists, x, bias, qw, begun, given, wv, out, *scratch):
    step_id = pl.program_id(0)
    heads, both, width = qw.shape
    sub = both // PAIR
    rows = heads * sub
    tiles, parts, _, quarter, cols = x.shape
    size = CHUNK * quarter
    per = 128 // quarter
    lane_slot = lax.broadcasted_iota(jnp.int32, (1, 128), 1) // quarter
    lane = lax.broadcasted_iota(jnp.int32, (sub, 128), 1)
    xbufs, accs, tops, dens = (scratch[q * PAIR:(q + 1) * PAIR] for q in range(4))

    def gather(g, n, c, xbuf):
        shades = []
        for part in range(CHUNK // per):
            shade = jnp.full((1, 128), NEG, F32)
            for v in range(per):
                u = part * per + v
                place = c * CHUNK + u
                s = lists[g, jnp.maximum(jnp.minimum(place, n - 1), 0)]
                for i in range(parts):
                    xbuf[u * quarter:(u + 1) * quarter, i * cols:(i + 1) * cols] = x[
                        s % tiles, i, s // tiles
                    ]
                live = (lane_slot == v) & (place < n)
                shade = jnp.where(live, bias[pl.ds(s, 1), :], shade)
            shades.append(shade)
        return xbuf[...], jnp.concatenate(shades, axis=1)

    def chunk(queries, rows_x, shade, old):
        scores = lax.dot_general(
            queries, rows_x, (((1,), (1,)), ((), ())), preferred_element_type=F32
        ) + shade
        new = jnp.maximum(old, jnp.max(scores, axis=1, keepdims=True))
        weights = jnp.exp(scores - jnp.concatenate([new] * (size // 128), axis=1))
        total = jnp.sum(weights, axis=1, keepdims=True)
        more = jnp.dot(weights.astype(BF), rows_x, preferred_element_type=F32)
        return new, jnp.exp(old - new), total, more

    counts, begins = [], []
    for p in range(PAIR):
        g = step_id * PAIR + p
        n = lists[g, 128]
        counts.append(n)
        start = begun[p * sub:(p + 1) * sub, :]
        old = jnp.concatenate(
            [jnp.broadcast_to(start[:, h:h + 1], (sub, 128)) for h in range(heads)], axis=0
        )
        den = jnp.concatenate(
            [
                jnp.broadcast_to(start[:, heads + h:heads + h + 1], (sub, 128))
                for h in range(heads)
            ],
            axis=0,
        )
        begins.append(old)
        rows_x, shade = gather(g, n, 0, xbufs[p])
        queries = qw[:, p * sub:(p + 1) * sub, :].reshape(rows, width)
        new, shrink, total, more = chunk(queries, rows_x, shade, old)
        accs[p][...] = more
        tops[p][...] = new
        dens[p][...] = den * shrink + total

    for p in range(PAIR):
        g = step_id * PAIR + p

        @pl.when(counts[p] > CHUNK)
        def _(p=p, g=g):
            def again(c, carry):
                rows_x, shade = gather(g, counts[p], c, xbufs[p])
                queries = qw[:, p * sub:(p + 1) * sub, :].reshape(rows, width)
                new, shrink, total, more = chunk(queries, rows_x, shade, tops[p][...])
                tops[p][...] = new
                dens[p][...] = dens[p][...] * shrink + total
                wide = jnp.concatenate([shrink] * (width // 128), axis=1)
                accs[p][...] = accs[p][...] * wide + more
                return carry

            lax.fori_loop(1, (counts[p] + CHUNK - 1) // CHUNK, again, 0)

    half = width // 2
    for p in range(PAIR):
        place = slice(p * sub, (p + 1) * sub)
        top = tops[p][...]
        shrink = jnp.exp(begins[p] - top)
        state = jnp.zeros((sub, 128), F32)
        for h in range(heads):
            line = slice(h * sub, (h + 1) * sub)
            state = jnp.where(lane == h, top[line], state)
            state = jnp.where(lane == heads + h, dens[p][line, :], state)
        hi, mid, lo = split3(state)
        packed = hi + pltpu.roll(mid, 2 * heads, 1) + pltpu.roll(lo, 4 * heads, 1)
        out[place, width:] = packed.astype(BF)
        for side in range(2):
            here = slice(side * rows // 2, (side + 1) * rows // 2)
            mixed = jnp.dot(
                accs[p][here, :].astype(BF),
                wv[:, side * half:(side + 1) * half],
                preferred_element_type=F32,
            )
            for c in range(half // 128):
                col = side * half + c * 128
                two = []
                for h in (2 * c, 2 * c + 1):
                    line = slice(h * sub, (h + 1) * sub)
                    far = side * rows // 2
                    two.append(
                        given[place, col:col + 128] * shrink[far + h * sub:far + (h + 1) * sub]
                        + mixed[line, c * 128:(c + 1) * 128]
                    )
                out[place, col:col + 128] = jnp.where(
                    lane < width // heads, two[0], two[1]
                ).astype(BF)


def combine_kernel(r0, r1, r2, r3, out):
    width = out.shape[1]
    heads = 8
    line = lax.broadcasted_iota(jnp.int32, (128, 2 * width), 0)
    col = lax.broadcasted_iota(jnp.int32, (128, 2 * width), 1)
    match = (
        (line % heads == (col % width) // (width // heads))
        & ((line // heads) % 2 == col // width)
        & (line < 6 * heads)
    )
    spread = match.astype(F32).astype(BF)
    tops, dens, nums = [], [], []
    for r in (r0, r1, r2, r3):
        wide = jnp.dot(r[:, width:], spread, preferred_element_type=F32)
        tops.append(wide[:, :width])
        dens.append(wide[:, width:])
        nums.append(r[:, :width].astype(F32))
    best = jnp.maximum(jnp.maximum(tops[0], tops[1]), jnp.maximum(tops[2], tops[3]))
    scale = [jnp.exp(v - best) for v in tops]
    numer = sum(a * b for a, b in zip(scale, nums))
    denom = sum(a * b for a, b in zip(scale, dens))
    out[...] = (numer / denom).astype(BF)


def finish_kernel(place, a0, a1, a2, a3, lat, w_out, gain, w_inc, target, predicted, grad, cut):
    me = place[0]
    share, width = a0.shape
    dims = (((0,), (0,)), ((), ()))
    total = jnp.zeros(grad.shape, F32)
    for d, a in enumerate((a0, a1, a2, a3)):
        here = pl.ds(pl.multiple_of((me ^ d) * share, share), share)
        updated = lat[here, :].astype(F32) + jnp.dot(
            a[...], w_out[...], preferred_element_type=F32
        )
        power = jnp.mean(updated * updated, axis=1, keepdims=True)
        normed = (updated * lax.rsqrt(power + 1e-6) * gain[...]).astype(BF)
        answer = jnp.dot(normed, w_inc[...], preferred_element_type=F32)
        predicted[here, :] = answer
        residual = answer - target[here, :].astype(F32)
        high = residual.astype(BF)
        low = (residual - high.astype(F32)).astype(BF)
        for c in range(width // 128):
            cut[d, c] = normed[:, c * 128:(c + 1) * 128]
        mine = cut[d, me]
        total = total + lax.dot_general(mine, high, dims, preferred_element_type=F32)
        total = total + lax.dot_general(mine, low, dims, preferred_element_type=F32)
    grad[...] = total


def body(
    obs_feat,
    row_valid,
    block_owner,
    block_pattern,
    latent,
    w_query,
    w_key,
    w_value,
    self_bias,
    w_out,
    norm_gain,
    w_inc,
    target,
):
    tiles = lax.axis_size("tile")
    groups = lax.axis_size("head")
    me = lax.axis_index("head")
    blocks = block_owner.shape[0]
    block_rows = obs_feat.shape[0] // blocks
    quarter = block_rows // groups
    cols = obs_feat.shape[1]
    lat_rows, width = latent.shape
    subs = block_pattern.shape[1]
    sub = lat_rows // subs
    local_heads = self_bias.shape[0]
    heads = local_heads * groups
    head_size = width // heads
    share = lat_rows // groups

    def swap(v, axis, mask, size):
        return lax.ppermute(v, axis, [(d, d ^ mask) for d in range(size)])

    def pick(v, which):
        return lax.dynamic_index_in_dim(v, which, 0, keepdims=False)

    tile = lax.axis_index("tile")
    whole = lambda *shape: pl.BlockSpec(shape, lambda g, *_: (0,) * len(shape))
    marks, taken = pl.pallas_call(
        marks_kernel,
        grid_spec=pltpu.PrefetchScalarGridSpec(
            num_scalar_prefetch=1,
            grid=(1,),
            in_specs=[whole(blocks, block_rows), whole(subs, blocks)],
            out_specs=[
                whole(tiles, MARK_ROWS, 128),
                pl.BlockSpec(memory_space=pltpu.SMEM),
            ],
            scratch_shapes=[
                pltpu.VMEM((blocks, 128), F32),
                pltpu.SMEM((tiles,), jnp.int32),
            ],
        ),
        out_shape=[
            jax.ShapeDtypeStruct((tiles, MARK_ROWS, 128), F32),
            jax.ShapeDtypeStruct((SLOTS * tiles,), jnp.int32),
        ],
        name="marks",
    )(block_owner[:, 0], row_valid.reshape(blocks, block_rows), block_pattern.T)
    marks = lax.all_to_all(marks, "tile", split_axis=0, concat_axis=0, tiled=True)
    payload = pl.pallas_call(
        pack_kernel,
        grid_spec=pltpu.PrefetchScalarGridSpec(
            num_scalar_prefetch=1,
            grid=(1,),
            in_specs=[whole(blocks, groups, quarter, cols)],
            out_specs=whole(tiles, groups, SLOTS, quarter, cols),
        ),
        out_shape=jax.ShapeDtypeStruct((tiles, groups, SLOTS, quarter, cols), BF),
        compiler_params=pltpu.CompilerParams(vmem_limit_bytes=32 * 1024 * 1024),
        name="pack",
    )(taken, obs_feat.reshape(blocks, groups, quarter, cols))
    arrived = lax.all_to_all(
        payload.reshape(tiles * groups, SLOTS, quarter, cols),
        ("tile", "head"),
        split_axis=0,
        concat_axis=0,
        tiled=True,
    ).reshape(tiles, groups, SLOTS, quarter, cols)

    lists, bias = pl.pallas_call(
        lists_kernel,
        grid=(1,),
        in_specs=[whole(tiles, MARK_ROWS, 128)],
        out_specs=[whole(subs, 256), whole(SLOTS * tiles, 128)],
        out_shape=[
            jax.ShapeDtypeStruct((subs, 256), jnp.int32),
            jax.ShapeDtypeStruct((SLOTS * tiles, 128), F32),
        ],
        name="lists",
    )(marks)

    stacked = lax.all_gather(
        jnp.concatenate([w_query, w_key, w_value, w_out.T], axis=1), "head", axis=0
    )
    wq, wk, wv, wo = [
        stacked[:, :, a * 128:(a + 1) * 128].transpose(1, 0, 2).reshape(width, width)
        for a in range(4)
    ]
    wo = wo.T
    by_distance = jnp.stack(
        [self_bias] + [swap(self_bias, "head", d, groups) for d in range(1, groups)]
    )
    turn = jnp.arange(groups, dtype=jnp.int32) ^ me
    bias_all = jnp.take(by_distance, turn, axis=0).reshape(heads)
    queries = jnp.dot(latent, wq, preferred_element_type=F32).astype(BF)
    own_key = jnp.dot(latent, wk, preferred_element_type=F32).astype(BF)
    q3 = queries.reshape(lat_rows, heads, head_size)
    k3 = wk.reshape(width, heads, head_size)
    scale = 1.0 / math.sqrt(head_size)
    qw = (
        jnp.einsum("lhd,khd->hlk", q3, k3, preferred_element_type=F32) * scale
    ).astype(BF)
    own = (
        jnp.sum(
            q3.astype(F32) * own_key.reshape(lat_rows, heads, head_size).astype(F32), axis=-1
        )
        * scale
        + bias_all[None, :]
    )
    keep = (me == 0).astype(F32)
    states = jnp.pad(
        jnp.concatenate([own, jnp.full((lat_rows, heads), keep)], axis=1),
        ((0, 0), (0, 128 - 2 * heads)),
    )
    numer = jnp.dot(latent, wv, preferred_element_type=F32) * keep

    block = PAIR * sub
    scratch = [
        shape
        for shape in (
            pltpu.VMEM((CHUNK * quarter, width), BF),
            pltpu.VMEM((heads * sub, width), F32),
            pltpu.VMEM((heads * sub, 128), F32),
            pltpu.VMEM((heads * sub, 128), F32),
        )
        for _ in range(PAIR)
    ]
    partial = pl.pallas_call(
        attend_kernel,
        grid_spec=pltpu.PrefetchScalarGridSpec(
            num_scalar_prefetch=1,
            grid=(subs // PAIR,),
            in_specs=[
                whole(*arrived.shape),
                whole(SLOTS * tiles, 128),
                pl.BlockSpec((heads, block, width), lambda g, *_: (0, g, 0)),
                pl.BlockSpec((block, 128), lambda g, *_: (g, 0)),
                pl.BlockSpec((block, width), lambda g, *_: (g, 0)),
                whole(width, width),
            ],
            out_specs=pl.BlockSpec((block, width + 128), lambda g, *_: (g, 0)),
            scratch_shapes=scratch,
        ),
        out_shape=jax.ShapeDtypeStruct((lat_rows, width + 128), BF),
        compiler_params=pltpu.CompilerParams(vmem_limit_bytes=40 * 1024 * 1024),
        name="attend",
    )(lists, arrived, bias, qw, states, numer, wv)

    partial = partial.reshape(groups, share, width + 128)
    received = [pick(partial, me)] + [
        swap(pick(partial, me ^ d), "head", d, groups) for d in range(1, groups)
    ]
    attended = pl.pallas_call(
        combine_kernel,
        grid=(1,),
        in_specs=[whole(share, width + 128)] * groups,
        out_specs=whole(share, width),
        out_shape=jax.ShapeDtypeStruct((share, width), BF),
        name="combine",
    )(*received)
    gathered = [attended] + [swap(attended, "head", d, groups) for d in range(1, groups)]
    predicted, grad = pl.pallas_call(
        finish_kernel,
        grid_spec=pltpu.PrefetchScalarGridSpec(
            num_scalar_prefetch=1,
            grid=(1,),
            in_specs=[whole(share, width)] * groups
            + [
                whole(lat_rows, width),
                whole(width, width),
                whole(1, width),
                whole(width, 128),
                whole(lat_rows, 128),
            ],
            out_specs=[whole(lat_rows, 128), whole(cols, 128)],
            scratch_shapes=[pltpu.VMEM((groups, width // 128, share, 128), BF)],
        ),
        out_shape=[
            jax.ShapeDtypeStruct((lat_rows, 128), F32),
            jax.ShapeDtypeStruct((cols, 128), F32),
        ],
        compiler_params=pltpu.CompilerParams(vmem_limit_bytes=32 * 1024 * 1024),
        name="finish",
    )(
        me[None].astype(jnp.int32),
        *gathered,
        latent,
        wo,
        norm_gain[None, :],
        w_inc,
        target,
    )
    for low, high in ((1, 2), (4, 8), (16, 32)):
        a, b, c = (swap(grad, "tile", m, tiles) for m in (low, high, low + high))
        grad = (grad + a) + (b + c)
    return predicted, grad * (1.0 / math.sqrt(lat_rows * tiles))


def solution(mesh):
    in_specs = (
        P("tile", "head"),
        P("tile"),
        P("tile", None),
        P("tile", None),
        P("tile", None),
        P(None, "head"),
        P(None, "head"),
        P(None, "head"),
        P("head"),
        P("head", None),
        P(),
        P(),
        P("tile", None),
    )
    out_specs = (P("tile", None), P("head", None))
    return jax.shard_map(body, mesh=mesh, in_specs=in_specs, out_specs=out_specs, check_vma=False)
```

time: 227 us -> 222 us (0.978); the launches traced: 224 us -> 222 us
  starting transfers between devices: 55.2 us -> 50.1 us
  waiting for transfers between devices: 102 us -> 107 us
  other arithmetic: 5.05 us -> 1.68 us
    ppermute x21 -> x18, waiting for transfers between devices: 21.7 us -> 28.4 us  [swap(): return lax.ppermute(v, axis, [(d, d ^ mask) for d in range(size)])]
    ppermute x21 -> x18, starting transfers between devices: 32.2 us -> 26.2 us  [swap(): return lax.ppermute(v, axis, [(d, d ^ mask) for d in range(size)])]
    pallas_call x1 -> x2, Pallas kernels: 19.6 us -> 18.4 us  [the longest x1 15.9 us: body(): pl.pallas_call(attend_kernel, grid_spec=pltpu.PrefetchScalarGridSpec(num_...]
    unnamed x40 -> x51, local copies, waits for them, and re-layouts: 8.94 us -> 10.1 us
  transfers between devices with their start and end apart: 24 -> 21, of which waited for: 16 -> 17; matrix products, arithmetic and copies ran while one was open for 5% -> 4% of each run, Pallas kernels for 2% -> 2%
where the time goes in v5:
time: 222 us
  waiting for transfers between devices  107 us (48%)
  starting transfers between devices  50.1 us (23%)
  Pallas kernels  28.5 us (13%)
  local copies, waits for them, and re-layouts  14.9 us (7%)
  between operations  14.4 us (6%)
  matrix products  4.73 us (2%)
    all_gather x1, waiting for transfers between devices, body(): lax.all_gather(jnp.concatenate([w_query, w_key, w_value, w_out.T], axis=1...  39.4 us
    all_to_all x1, waiting for transfers between devices, body(): lax.all_to_all(payload.reshape(tiles * groups, SLOTS, quarter, cols), ('t...  37.4 us
    ppermute x18, waiting for transfers between devices, swap(): return lax.ppermute(v, axis, [(d, d ^ mask) for d in range(size)])  28.4 us
    ppermute x18, starting transfers between devices, swap(): return lax.ppermute(v, axis, [(d, d ^ mask) for d in range(size)])  26.2 us
    pallas_call x1, Pallas kernels, body(): pl.pallas_call(attend_kernel, grid_spec=pltpu.PrefetchScalarGridSpec(num_...  15.9 us
    all_to_all x1, starting transfers between devices, body(): lax.all_to_all(payload.reshape(tiles * groups, SLOTS, quarter, cols), ('t...  12 us
    all_to_all x1, starting transfers between devices, body(): lax.all_to_all(marks, 'tile', split_axis=0, concat_axis=0, tiled=True)  11.8 us
    unnamed x51, local copies, waits for them, and re-layouts  10.1 us
  transfers between devices with their start and end apart: 21, of which 17 were waited for; matrix products, arithmetic and copies ran while one was open for 4% of the time, Pallas kernels for 2%

profile of v5, /device:TPU:32, one launch (start us, length us, event | category | flops | bytes accessed | tf_op | source)
XLA Modules:
  0.0 221.5 jit_solution(2323188479560158663)
XLA Ops:
  7.2 2.8 %marks.1 = (f32[64,2,128]{2,1,0:T(2,128)}, s32[128]{0:T(128)}) custom-call(s32[64]{0:T(128)} %bitcast.79, s32[64,128]{1,0:T(8,128)} %bitcast.73, s32[16,64]{1,0:T(8,128)} %bitcast.74), custom_call_target="tpu_custom_call" | custom-call | tf_op jit(solution)/shard_map/marks/pallas_call | solution.py:319
  10.0 11.8 %all-to-all-start = ((f32[64,2,128]{2,1,0:T(2,128)}), f32[64,2,128]{2,1,0:T(2,128)S(1)}, u32[]{:S(2)}, u32[]{:S(2)}) async-start(f32[64,2,128]{2,1,0:T(2,128)} %get-tuple-element.8), calls=%async_computation | async-start | bytes 131072 | tf_op jit(solution)/shard_map/all_to_all | solution.py:340
  21.8 1.6 copy-done.3
  23.3 0.7 copy-done.10
  24.0 2.7 %pack.1 = bf16[64,4,2,32,128]{4,3,2,1,0:T(8,128)(2,1)S(1)} custom-call(s32[128]{0:T(128)S(1)} %copy-done.10, bf16[64,4,32,128]{3,2,1,0:T(8,128)(2,1)S(1)} %bitcast.63), custom_call_target="tpu_custom_call" | custom-call | tf_op jit(solution)/shard_map/pack/pallas_call | solution.py:341
  26.7 2.0 copy-done.1
  28.8 1.9 all-to-all-done.found
  31.3 12.0 %all-to-all-start.1 = ((bf16[256,2,32,128]{3,2,1,0:T(8,128)(2,1)}), bf16[256,2,32,128]{3,2,1,0:T(8,128)(2,1)}, u32[]{:S(2)}, u32[]{:S(2)}) async-start(bf16[256,2,32,128]{3,2,1,0:T(8,128)(2,1)} %bitcast.61), calls=%async_computation.1 | async-start | bytes 8388608 | tf_op jit(solution)/shard_map/all_to_all | solution.py:353
  43.6 0.9 pad_maximum_fusion
  44.5 2.8 %collective-permute-start.2 = (f32[2]{0:T(128)S(1)}, f32[2]{0:T(128)S(1)}, u32[]{:S(2)}, u32[]{:S(2)}) collective-permute-start(f32[2]{0:T(128)S(1)} %copy-done.24), channel_id=1, source_target_pairs={{0,3},{1,2},{2,1},{3,0},{4,7},{5,6},{6,5},{7,4},{8,11},{9,10},{10,... | collective-permute-start | bytes 32 | tf_op jit(solution)/shard_map/ppermute | solution.py:312
  47.3 0.8 collective-permute-start.1
  48.7 3.4 %collective-permute-done.2 = f32[2]{0:T(128)S(1)} collective-permute-done((f32[2]{0:T(128)S(1)}, f32[2]{0:T(128)S(1)}, u32[]{:S(2)}, u32[]{:S(2)}) %collective-permute-start.2) | collective-permute-done | bytes 40 | tf_op jit(solution)/shard_map/ppermute | solution.py:312
  53.0 2.1 lists.1
  55.1 39.4 %all-gather.3.cloned.1.call-done = bf16[2048,512]{1,0:T(8,128)(2,1)} async-done(((bf16[512,512]{1,0:T(8,128)(2,1)}), bf16[2048,512]{1,0:T(8,128)(2,1)}) %all-gather.3.cloned.1.call-update) | async-done | bytes 2097168 | tf_op jit(solution)/shard_map/all_gather | solution.py:373
  94.5 2.6 %slice_bitcast_fusion = (bf16[512,4,128]{2,0,1:T(8,128)(2,1)}, bf16[4,64,8,128]{3,2,1,0:T(8,128)(2,1)S(1)}, bf16[512,4,128]{2,0,1:T(8,128)(2,1)S(1)}, bf16[512,4,128]{2,0,1:T(8,128)(2,1)S(1)}) fusion(bf16[4,512,512]{2,1,0:T(8,128)(2,1)} %bitcast.71), kind=kLoop, calls=%fused_computation.9 | loop fusion | bytes 4194304 | tf_op jit(solution)/shard_map/transpose | solution.py:377
  98.0 0.8 copy-done.11
  100.7 3.3 %multiply_convert_fusion.qw = bf16[8,512,512]{2,1,0:T(8,128)(2,1)} fusion(bf16[512,8,64]{0,2,1:T(8,128)(2,1)S(1)} %bitcast.67, bf16[512,8,64]{0,2,1:T(8,128)(2,1)S(1)} %bitcast.69), kind=kOutput, calls=%fused_computation.1 | convolution fusion | flops 272629760 | bytes 5242880 | tf_op jit(solution)/shard_map/lhd,khd->hlk/dot_general | solution.py:392
  104.0 37.4 %all-to-all-done.1 = bf16[256,2,32,128]{3,2,1,0:T(8,128)(2,1)} async-done(((bf16[256,2,32,128]{3,2,1,0:T(8,128)(2,1)}), bf16[256,2,32,128]{3,2,1,0:T(8,128)(2,1)}, u32[]{:S(2)}, u32[]{:S(2)}) %all-to-all-start.1) | async-done | bytes 4194336 | tf_op jit(solution)/shard_map/all_to_all | solution.py:353
  141.4 2.2 copy-done
  143.6 15.9 %attend.1 = bf16[512,640]{1,0:T(8,128)(2,1)S(1)} custom-call(s32[16,256]{1,0:T(8,128)S(1)} %copy-done.8, bf16[64,4,2,32,128]{4,3,2,1,0:T(8,128)(2,1)} %bitcast.6.x, f32[128,128]{1,0:T(8,128)S(1)} %copy-done.7, bf16[8,512,512]{2,1,0:T(8,128)(2,1)S(1)} %copy-done, f32[512,128]{1,0:T(8,128)S(1)} %pad_select_fusion.begun, f32[512,512]{1,0:T(8,128)S(1)} %fusion.given, ...), custom_call_target="tpu_custom_call" | custom-call | tf_op jit(solution)/shard_map/attend/pallas_call | solution.py:419
  159.5 0.7 dynamic-slice_bitcast_fusion
  160.8 1.1 collective-permute-start.4
  162.0 3.0 %collective-permute-start.5 = (bf16[128,640]{1,0:T(8,128)(2,1)S(1)}, bf16[128,640]{1,0:T(8,128)(2,1)S(1)}, u32[]{:S(2)}, u32[]{:S(2)}) collective-permute-start(bf16[128,640]{1,0:T(8,128)(2,1)S(1)} %get-tuple-element.18), channel_id=1, source_target_pairs={{0,3},{1,2},{2,1},{3,0},{4,7},{5,6},{6,5},{7,4},{8,11},{9,10},{10,... | collective-permute-start | bytes 491528 | tf_op jit(solution)/shard_map/ppermute | solution.py:312
  165.0 2.3 %collective-permute-done.3.r1 = bf16[128,640]{1,0:T(8,128)(2,1)S(1)} collective-permute-done((bf16[128,640]{1,0:T(8,128)(2,1)S(1)}, bf16[128,640]{1,0:T(8,128)(2,1)S(1)}, u32[]{:S(2)}, u32[]{:S(2)}) %collective-permute-start.3) | collective-permute-done | bytes 163872 | tf_op jit(solution)/shard_map/ppermute | solution.py:312
  167.2 2.6 %collective-permute-done.4.r2 = bf16[128,640]{1,0:T(8,128)(2,1)S(1)} collective-permute-done((bf16[128,640]{1,0:T(8,128)(2,1)S(1)}, bf16[128,640]{1,0:T(8,128)(2,1)S(1)}, u32[]{:S(2)}, u32[]{:S(2)}) %collective-permute-start.4) | collective-permute-done | bytes 163872 | tf_op jit(solution)/shard_map/ppermute | solution.py:312
  169.8 2.6 %collective-permute-done.5.r3 = bf16[128,640]{1,0:T(8,128)(2,1)S(1)} collective-permute-done((bf16[128,640]{1,0:T(8,128)(2,1)S(1)}, bf16[128,640]{1,0:T(8,128)(2,1)S(1)}, u32[]{:S(2)}, u32[]{:S(2)}) %collective-permute-start.5) | collective-permute-done | bytes 163872 | tf_op jit(solution)/shard_map/ppermute | solution.py:312
  172.4 0.7 copy-done.19
  173.0 2.5 %combine.1.a0 = bf16[128,512]{1,0:T(8,128)(2,1)} custom-call(bf16[128,640]{1,0:T(8,128)(2,1)} %get-tuple-element.21.r0, bf16[128,640]{1,0:T(8,128)(2,1)} %copy-done.17, bf16[128,640]{1,0:T(8,128)(2,1)} %copy-done.18, bf16[128,640]{1,0:T(8,128)(2,1)} %copy-done.19), custom_call_target="tpu_custom_call" | custom-call | tf_op jit(solution)/shard_map/combine/pallas_call | solution.py:444
  175.5 2.9 %collective-permute-start.7 = (bf16[128,512]{1,0:T(8,128)(2,1)}, bf16[128,512]{1,0:T(8,128)(2,1)S(1)}, u32[]{:S(2)}, u32[]{:S(2)}) collective-permute-start(bf16[128,512]{1,0:T(8,128)(2,1)} %combine.1.a0), channel_id=1, source_target_pairs={{0,2},{1,3},{2,0},{3,1},{4,6},{5,7},{6,4},{7,5},{8,10},{9,11},{10,... | collective-permute-start | bytes 393224 | tf_op jit(solution)/shard_map/ppermute | solution.py:312
  178.4 1.8 collective-permute-start.8
  180.5 1.4 collective-permute-done.6.a1
  181.9 1.9 collective-permute-done.7.a2
  183.7 1.5 collective-permute-done.8.a3
  185.3 0.9 copy-done.4
  186.2 2.5 %finish.1 = (f32[512,128]{1,0:T(8,128)}, f32[128,128]{1,0:T(8,128)S(1)}) custom-call(s32[1]{0:T(128)} %bitcast.place, bf16[128,512]{1,0:T(8,128)(2,1)S(1)} %copy-done.4, bf16[128,512]{1,0:T(8,128)(2,1)S(1)} %collective-permute-done.6.a1, bf16[128,512]{1,0:T(8,128)(2,1)S(1)} %collective-permute-done.7.a2, bf16[128,512]{1,0:T(8,128)(2,1)S(1)} %collective-permute-done.8.a3, ...), custom_call_target="tpu_custom_call" | custom-call | tf_op jit(solution)/shard_map/finish/pallas_call | solution.py:453
  188.7 2.3 %collective-permute-start.10 = (f32[128,128]{1,0:T(8,128)S(1)}, f32[128,128]{1,0:T(8,128)S(1)}, u32[]{:S(2)}, u32[]{:S(2)}) collective-permute-start(f32[128,128]{1,0:T(8,128)S(1)} %get-tuple-element.13), channel_id=1, source_target_pairs={{0,8},{4,12},{8,0},{12,4},{16,24},{20,28},{24,16},{28,20},{32,40},... | collective-permute-start | bytes 196616 | tf_op jit(solution)/shard_map/ppermute | solution.py:312
  191.2 2.1 collective-permute-done.10
  193.3 1.4 collective-permute-done.11
  194.8 2.2 %collective-permute-start.13 = (f32[128,128]{1,0:T(8,128)S(1)}, f32[128,128]{1,0:T(8,128)S(1)}, u32[]{:S(2)}, u32[]{:S(2)}) collective-permute-start(f32[128,128]{1,0:T(8,128)S(1)} %add_add_fusion.1), channel_id=1, source_target_pairs={{0,32},{4,36},{8,40},{12,44},{16,48},{20,52},{24,56},{28,60},{32,0... | collective-permute-start | bytes 196616 | tf_op jit(solution)/shard_map/ppermute | solution.py:312
  197.0 1.4 collective-permute-start.14
  198.4 3.0 %collective-permute-start.12 = (f32[128,128]{1,0:T(8,128)S(1)}, f32[128,128]{1,0:T(8,128)S(1)}, u32[]{:S(2)}, u32[]{:S(2)}) collective-permute-start(f32[128,128]{1,0:T(8,128)S(1)} %add_add_fusion.1), channel_id=1, source_target_pairs={{0,16},{4,20},{8,24},{12,28},{16,0},{20,4},{24,8},{28,12},{32,48},... | collective-permute-start | bytes 196616 | tf_op jit(solution)/shard_map/ppermute | solution.py:312
  201.4 3.4 %collective-permute-done.13 = f32[128,128]{1,0:T(8,128)S(1)} collective-permute-done((f32[128,128]{1,0:T(8,128)S(1)}, f32[128,128]{1,0:T(8,128)S(1)}, u32[]{:S(2)}, u32[]{:S(2)}) %collective-permute-start.13) | collective-permute-done | bytes 65568 | tf_op jit(solution)/shard_map/ppermute | solution.py:312
  204.7 1.5 collective-permute-done.14
  206.2 2.3 %collective-permute-start.16 = (f32[128,128]{1,0:T(8,128)S(1)}, f32[128,128]{1,0:T(8,128)S(1)}, u32[]{:S(2)}, u32[]{:S(2)}) collective-permute-start(f32[128,128]{1,0:T(8,128)S(1)} %add_add_fusion), channel_id=1, source_target_pairs={{0,128},{4,132},{8,136},{12,140},{16,144},{20,148},{24,152},{28,15... | collective-permute-start | bytes 196616 | tf_op jit(solution)/shard_map/ppermute | solution.py:312
  208.5 1.0 collective-permute-start.17
  209.8 2.3 %collective-permute-done.16 = f32[128,128]{1,0:T(8,128)S(1)} collective-permute-done((f32[128,128]{1,0:T(8,128)S(1)}, f32[128,128]{1,0:T(8,128)S(1)}, u32[]{:S(2)}, u32[]{:S(2)}) %collective-permute-start.16) | collective-permute-done | bytes 65568 | tf_op jit(solution)/shard_map/ppermute | solution.py:312
  212.1 1.9 collective-permute-done.17
  214.0 0.6 add_multiply_fusion
  (77 shorter events, 6.3 us)
Async XLA Ops:
  10.0 20.7 %all-to-all-start = ((f32[64,2,128]{2,1,0:T(2,128)}), f32[64,2,128]{2,1,0:T(2,128)S(1)}, u32[]{:S(2)}, u32[]{:S(2)}) async-start(f32[64,2,128]{2,1,0:T(2,128)} %get-tuple-element.8), calls=%async_computation | async-start | bytes 131072 | tf_op jit(solution)/shard_map/all_to_all | solution.py:340
  21.7 1.6 copy-start.3
  23.3 0.7 copy-start.10
  26.7 2.0 copy-start.1
  30.7 0.6 copy-start.16
  30.7 12.7 %copy-start.20 = (bf16[128,512]{1,0:T(8,128)(2,1)S(1)}, bf16[128,512]{1,0:T(8,128)(2,1)}, u32[]{:S(2)}) copy-start(bf16[128,512]{1,0:T(8,128)(2,1)} %param.22) | copy-start | bytes 393220
  30.7 12.8 %copy-start.21 = (bf16[512,128]{1,0:T(8,128)(2,1)S(1)}, bf16[512,128]{1,0:T(8,128)(2,1)}, u32[]{:S(2)}) copy-start(bf16[512,128]{1,0:T(8,128)(2,1)} %param.20) | copy-start | bytes 393220
  30.7 12.9 %copy-start.22 = (bf16[512,128]{1,0:T(8,128)(2,1)S(1)}, bf16[512,128]{1,0:T(8,128)(2,1)}, u32[]{:S(2)}) copy-start(bf16[512,128]{1,0:T(8,128)(2,1)} %param.19) | copy-start | bytes 393220
  30.7 12.9 %copy-start.23 = (bf16[512,128]{1,0:T(8,128)(2,1)S(1)}, bf16[512,128]{1,0:T(8,128)(2,1)}, u32[]{:S(2)}) copy-start(bf16[512,128]{1,0:T(8,128)(2,1)} %param.18) | copy-start | bytes 393220
  30.7 13.7 %copy-start.24 = (f32[2]{0:T(128)S(1)}, f32[2]{0:T(128)}, u32[]{:S(2)}) copy-start(f32[2]{0:T(128)} %param.21) | copy-start | bytes 28
  31.3 110.1 %all-to-all-start.1 = ((bf16[256,2,32,128]{3,2,1,0:T(8,128)(2,1)}), bf16[256,2,32,128]{3,2,1,0:T(8,128)(2,1)}, u32[]{:S(2)}, u32[]{:S(2)}) async-start(bf16[256,2,32,128]{3,2,1,0:T(8,128)(2,1)} %bitcast.61), calls=%async_computation.1 | async-start | bytes 8388608 | tf_op jit(solution)/shard_map/all_to_all | solution.py:353
  43.3 54.2 %copy-start.2 = (bf16[512,512]{1,0:T(8,128)(2,1)S(1)}, bf16[512,512]{1,0:T(8,128)(2,1)}, u32[]{:S(2)}) copy-start(bf16[512,512]{1,0:T(8,128)(2,1)} %lat.1) | copy-start | bytes 1572868
  43.4 51.2 %all-gather.3.cloned.1.call-start = ((), (), s32[]{:S(2)}) async-start(), calls=%async_computation.2 | async-start | bytes 2621440 | tf_op jit(solution)/shard_map/all_gather | solution.py:373
  44.5 7.6 %collective-permute-start.2 = (f32[2]{0:T(128)S(1)}, f32[2]{0:T(128)S(1)}, u32[]{:S(2)}, u32[]{:S(2)}) collective-permute-start(f32[2]{0:T(128)S(1)} %copy-done.24), channel_id=1, source_target_pairs={{0,3},{1,2},{2,1},{3,0},{4,7},{5,6},{6,5},{7,4},{8,11},{9,10},{10,... | collective-permute-start | bytes 32 | tf_op jit(solution)/shard_map/ppermute | solution.py:312
  47.3 5.0 %collective-permute-start.1 = (f32[2]{0:T(128)S(1)}, f32[2]{0:T(128)S(1)}, u32[]{:S(2)}, u32[]{:S(2)}) collective-permute-start(f32[2]{0:T(128)S(1)} %copy-done.24), channel_id=1, source_target_pairs={{0,2},{1,3},{2,0},{3,1},{4,6},{5,7},{6,4},{7,5},{8,10},{9,11},{10,... | collective-permute-start | bytes 32 | tf_op jit(solution)/shard_map/ppermute | solution.py:312
  48.1 4.2 %collective-permute-start = (f32[2]{0:T(128)S(1)}, f32[2]{0:T(128)S(1)}, u32[]{:S(2)}, u32[]{:S(2)}) collective-permute-start(f32[2]{0:T(128)S(1)} %copy-done.24), channel_id=1, source_target_pairs={{0,1},{1,0},{2,3},{3,2},{4,5},{5,4},{6,7},{7,6},{8,9},{9,8},{10,11... | collective-permute-start | bytes 32 | tf_op jit(solution)/shard_map/ppermute | solution.py:312
  97.5 1.9 copy-start.13
  98.0 0.8 copy-start.11
  99.5 1.0 copy-start.12
  99.5 1.2 copy-start.14
  99.6 41.9 %copy-start.7 = (f32[128,128]{1,0:T(8,128)S(1)}, f32[128,128]{1,0:T(8,128)}, u32[]{:S(2)}) copy-start(f32[128,128]{1,0:T(8,128)} %get-tuple-element.11.bias) | copy-start | bytes 196612
  99.6 41.8 %copy-start.8 = (s32[16,256]{1,0:T(8,128)S(1)}, s32[16,256]{1,0:T(8,128)}, u32[]{:S(2)}) copy-start(s32[16,256]{1,0:T(8,128)} %get-tuple-element.9.lists) | copy-start | bytes 49156
  141.4 2.2 copy-start
  143.6 36.6 %copy-start.15 = (bf16[512,4,128]{2,0,1:T(8,128)(2,1)S(1)}, bf16[512,4,128]{2,0,1:T(8,128)(2,1)}, u32[]{:S(2)}) copy-start(bf16[512,4,128]{2,0,1:T(8,128)(2,1)} %get-tuple-element.14) | copy-start | bytes 1572868
  143.6 41.7 %copy-start.5 = (bf16[512,128]{1,0:T(8,128)(2,1)S(1)}, bf16[512,128]{1,0:T(8,128)(2,1)}, u32[]{:S(2)}) copy-start(bf16[512,128]{1,0:T(8,128)(2,1)} %w_inc.1) | copy-start | bytes 393220
  143.6 41.7 %copy-start.6 = (bf16[512,128]{1,0:T(8,128)(2,1)S(1)}, bf16[512,128]{1,0:T(8,128)(2,1)}, u32[]{:S(2)}) copy-start(bf16[512,128]{1,0:T(8,128)(2,1)} %target.1) | copy-start | bytes 393220
  143.6 41.7 %copy-start.9 = (f32[512]{0:T(512)S(1)}, f32[512]{0:T(512)}, u32[]{:S(2)}) copy-start(f32[512]{0:T(512)} %param.23) | copy-start | bytes 6148
  160.3 7.0 %collective-permute-start.3 = (bf16[128,640]{1,0:T(8,128)(2,1)S(1)}, bf16[128,640]{1,0:T(8,128)(2,1)S(1)}, u32[]{:S(2)}, u32[]{:S(2)}) collective-permute-start(bf16[128,640]{1,0:T(8,128)(2,1)S(1)} %get-tuple-element.20), channel_id=1, source_target_pairs={{0,1},{1,0},{2,3},{3,2},{4,5},{5,4},{6,7},{7,6},{8,9},{9,8},{10,11... | collective-permute-start | bytes 491528 | tf_op jit(solution)/shard_map/ppermute | solution.py:312
  160.8 8.9 %collective-permute-start.4 = (bf16[128,640]{1,0:T(8,128)(2,1)S(1)}, bf16[128,640]{1,0:T(8,128)(2,1)S(1)}, u32[]{:S(2)}, u32[]{:S(2)}) collective-permute-start(bf16[128,640]{1,0:T(8,128)(2,1)S(1)} %get-tuple-element.19), channel_id=1, source_target_pairs={{0,2},{1,3},{2,0},{3,1},{4,6},{5,7},{6,4},{7,5},{8,10},{9,11},{10,... | collective-permute-start | bytes 491528 | tf_op jit(solution)/shard_map/ppermute | solution.py:312
  162.0 10.4 %collective-permute-start.5 = (bf16[128,640]{1,0:T(8,128)(2,1)S(1)}, bf16[128,640]{1,0:T(8,128)(2,1)S(1)}, u32[]{:S(2)}, u32[]{:S(2)}) collective-permute-start(bf16[128,640]{1,0:T(8,128)(2,1)S(1)} %get-tuple-element.18), channel_id=1, source_target_pairs={{0,3},{1,2},{2,1},{3,0},{4,7},{5,6},{6,5},{7,4},{8,11},{9,10},{10,... | collective-permute-start | bytes 491528 | tf_op jit(solution)/shard_map/ppermute | solution.py:312
  167.2 5.1 %copy-start.17 = (bf16[128,640]{1,0:T(8,128)(2,1)}, bf16[128,640]{1,0:T(8,128)(2,1)S(1)}, u32[]{:S(2)}) copy-start(bf16[128,640]{1,0:T(8,128)(2,1)S(1)} %collective-permute-done.3.r1) | copy-start | bytes 491524
  169.8 2.6 %copy-start.18 = (bf16[128,640]{1,0:T(8,128)(2,1)}, bf16[128,640]{1,0:T(8,128)(2,1)S(1)}, u32[]{:S(2)}) copy-start(bf16[128,640]{1,0:T(8,128)(2,1)S(1)} %collective-permute-done.4.r2) | copy-start | bytes 491524
  172.4 0.7 copy-start.19
  175.5 6.4 %collective-permute-start.6 = (bf16[128,512]{1,0:T(8,128)(2,1)}, bf16[128,512]{1,0:T(8,128)(2,1)S(1)}, u32[]{:S(2)}, u32[]{:S(2)}) collective-permute-start(bf16[128,512]{1,0:T(8,128)(2,1)} %combine.1.a0), channel_id=1, source_target_pairs={{0,1},{1,0},{2,3},{3,2},{4,5},{5,4},{6,7},{7,6},{8,9},{9,8},{10,11... | collective-permute-start | bytes 393224 | tf_op jit(solution)/shard_map/ppermute | solution.py:312
  175.5 8.2 %collective-permute-start.7 = (bf16[128,512]{1,0:T(8,128)(2,1)}, bf16[128,512]{1,0:T(8,128)(2,1)S(1)}, u32[]{:S(2)}, u32[]{:S(2)}) collective-permute-start(bf16[128,512]{1,0:T(8,128)(2,1)} %combine.1.a0), channel_id=1, source_target_pairs={{0,2},{1,3},{2,0},{3,1},{4,6},{5,7},{6,4},{7,5},{8,10},{9,11},{10,... | collective-permute-start | bytes 393224 | tf_op jit(solution)/shard_map/ppermute | solution.py:312
  178.4 6.9 %collective-permute-start.8 = (bf16[128,512]{1,0:T(8,128)(2,1)}, bf16[128,512]{1,0:T(8,128)(2,1)S(1)}, u32[]{:S(2)}, u32[]{:S(2)}) collective-permute-start(bf16[128,512]{1,0:T(8,128)(2,1)} %combine.1.a0), channel_id=1, source_target_pairs={{0,3},{1,2},{2,1},{3,0},{4,7},{5,6},{6,5},{7,4},{8,11},{9,10},{10,... | collective-permute-start | bytes 393224 | tf_op jit(solution)/shard_map/ppermute | solution.py:312
  185.3 0.9 copy-start.4
  188.7 4.6 %collective-permute-start.10 = (f32[128,128]{1,0:T(8,128)S(1)}, f32[128,128]{1,0:T(8,128)S(1)}, u32[]{:S(2)}, u32[]{:S(2)}) collective-permute-start(f32[128,128]{1,0:T(8,128)S(1)} %get-tuple-element.13), channel_id=1, source_target_pairs={{0,8},{4,12},{8,0},{12,4},{16,24},{20,28},{24,16},{28,20},{32,40},... | collective-permute-start | bytes 196616 | tf_op jit(solution)/shard_map/ppermute | solution.py:312
  191.1 3.7 %collective-permute-start.11 = (f32[128,128]{1,0:T(8,128)S(1)}, f32[128,128]{1,0:T(8,128)S(1)}, u32[]{:S(2)}, u32[]{:S(2)}) collective-permute-start(f32[128,128]{1,0:T(8,128)S(1)} %get-tuple-element.13), channel_id=1, source_target_pairs={{0,12},{4,8},{8,4},{12,0},{16,28},{20,24},{24,20},{28,16},{32,44},... | collective-permute-start | bytes 196616 | tf_op jit(solution)/shard_map/ppermute | solution.py:312
  191.1 3.7 %collective-permute-start.9 = (f32[128,128]{1,0:T(8,128)S(1)}, f32[128,128]{1,0:T(8,128)S(1)}, u32[]{:S(2)}, u32[]{:S(2)}) collective-permute-start(f32[128,128]{1,0:T(8,128)S(1)} %get-tuple-element.13), channel_id=1, source_target_pairs={{0,4},{4,0},{8,12},{12,8},{16,20},{20,16},{24,28},{28,24},{32,36},... | collective-permute-start | bytes 196616 | tf_op jit(solution)/shard_map/ppermute | solution.py:312
  194.8 9.9 %collective-permute-start.13 = (f32[128,128]{1,0:T(8,128)S(1)}, f32[128,128]{1,0:T(8,128)S(1)}, u32[]{:S(2)}, u32[]{:S(2)}) collective-permute-start(f32[128,128]{1,0:T(8,128)S(1)} %add_add_fusion.1), channel_id=1, source_target_pairs={{0,32},{4,36},{8,40},{12,44},{16,48},{20,52},{24,56},{28,60},{32,0... | collective-permute-start | bytes 196616 | tf_op jit(solution)/shard_map/ppermute | solution.py:312
  197.0 9.2 %collective-permute-start.14 = (f32[128,128]{1,0:T(8,128)S(1)}, f32[128,128]{1,0:T(8,128)S(1)}, u32[]{:S(2)}, u32[]{:S(2)}) collective-permute-start(f32[128,128]{1,0:T(8,128)S(1)} %add_add_fusion.1), channel_id=1, source_target_pairs={{0,48},{4,52},{8,56},{12,60},{16,32},{20,36},{24,40},{28,44},{32,1... | collective-permute-start | bytes 196616 | tf_op jit(solution)/shard_map/ppermute | solution.py:312
  198.4 7.8 %collective-permute-start.12 = (f32[128,128]{1,0:T(8,128)S(1)}, f32[128,128]{1,0:T(8,128)S(1)}, u32[]{:S(2)}, u32[]{:S(2)}) collective-permute-start(f32[128,128]{1,0:T(8,128)S(1)} %add_add_fusion.1), channel_id=1, source_target_pairs={{0,16},{4,20},{8,24},{12,28},{16,0},{20,4},{24,8},{28,12},{32,48},... | collective-permute-start | bytes 196616 | tf_op jit(solution)/shard_map/ppermute | solution.py:312
  206.2 5.9 %collective-permute-start.16 = (f32[128,128]{1,0:T(8,128)S(1)}, f32[128,128]{1,0:T(8,128)S(1)}, u32[]{:S(2)}, u32[]{:S(2)}) collective-permute-start(f32[128,128]{1,0:T(8,128)S(1)} %add_add_fusion), channel_id=1, source_target_pairs={{0,128},{4,132},{8,136},{12,140},{16,144},{20,148},{24,152},{28,15... | collective-permute-start | bytes 196616 | tf_op jit(solution)/shard_map/ppermute | solution.py:312
  208.5 5.5 %collective-permute-start.17 = (f32[128,128]{1,0:T(8,128)S(1)}, f32[128,128]{1,0:T(8,128)S(1)}, u32[]{:S(2)}, u32[]{:S(2)}) collective-permute-start(f32[128,128]{1,0:T(8,128)S(1)} %add_add_fusion), channel_id=1, source_target_pairs={{0,192},{4,196},{8,200},{12,204},{16,208},{20,212},{24,216},{28,22... | collective-permute-start | bytes 196616 | tf_op jit(solution)/shard_map/ppermute | solution.py:312
  209.5 4.5 %collective-permute-start.15 = (f32[128,128]{1,0:T(8,128)S(1)}, f32[128,128]{1,0:T(8,128)S(1)}, u32[]{:S(2)}, u32[]{:S(2)}) collective-permute-start(f32[128,128]{1,0:T(8,128)S(1)} %add_add_fusion), channel_id=1, source_target_pairs={{0,64},{4,68},{8,72},{12,76},{16,80},{20,84},{24,88},{28,92},{32,9... | collective-permute-start | bytes 196616 | tf_op jit(solution)/shard_map/ppermute | solution.py:312
Sparse Core Ops, SparseCore 0:
  46.0 48.4 all-gather.2

commit v6 on v5

--- a/solution.py
+++ b/solution.py
@@ -12,7 +12,7 @@
 NEG = -1e30
 SLOTS = 2
 CHUNK = 8
-PAIR = 2
+PAIR = 4
 MARK_ROWS = 2
 
 
@@ -370,9 +370,12 @@
         name="lists",
     )(marks)
 
-    stacked = lax.all_gather(
-        jnp.concatenate([w_query, w_key, w_value, w_out.T], axis=1), "head", axis=0
-    )
+    stacked = jnp.concatenate([w_query, w_key, w_value, w_out.T], axis=1)
+    near = jnp.stack(
+        [stacked] + [swap(stacked, "head", d, groups) for d in range(1, groups)]
+    )
+    turn = jnp.arange(groups, dtype=jnp.int32) ^ me
+    stacked = jnp.take(near, turn, axis=0)
     wq, wk, wv, wo = [
         stacked[:, :, a * 128:(a + 1) * 128].transpose(1, 0, 2).reshape(width, width)
         for a in range(4)

time: 222 us -> 205 us (0.923)
  between operations: 14.4 us -> 1 us
  waiting for transfers between devices: 107 us -> 101 us
  starting transfers between devices: 50.1 us -> 53.7 us
  Pallas kernels: 28.5 us -> 25.2 us
  other arithmetic: 1.68 us -> 4.21 us
    ppermute x18 -> x21, waiting for transfers between devices: 28.4 us -> 70.1 us  [swap(): return lax.ppermute(v, axis, [(d, d ^ mask) for d in range(size)])]
    all_gather x1 -> x0, waiting for transfers between devices: 39.4 us -> none  [body(): lax.all_gather(jnp.concatenate([w_query, w_key, w_value, w_out.T], axis=1...]
    all_to_all x1, waiting for transfers between devices: 37.4 us -> 28.7 us  [body(): lax.all_to_all(payload.reshape(tiles * groups, SLOTS, quarter, cols), ('t...]
    ppermute x18 -> x21, starting transfers between devices: 26.2 us -> 29.9 us  [swap(): return lax.ppermute(v, axis, [(d, d ^ mask) for d in range(size)])]
    pallas_call x1, Pallas kernels: 15.9 us -> 12.6 us  [body(): pl.pallas_call(attend_kernel, grid_spec=pltpu.PrefetchScalarGridSpec(num_...]
    transpose x4 -> x0, local copies, waits for them, and re-layouts: 3.2 us -> none  [body(): stacked[:, :, a * 128:(a + 1) * 128].transpose(1, 0, 2)]
    unnamed x51 -> x53, local copies, waits for them, and re-layouts: 10.1 us -> 11.4 us
  transfers between devices with their start and end apart: 21 -> 23, of which waited for: 17 -> 16; matrix products, arithmetic and copies ran while one was open for 4% -> 6% of each run, Pallas kernels for 2% -> 2%
where the time goes in v6:
time: 205 us
  waiting for transfers between devices  101 us (49%)
  starting transfers between devices  53.7 us (26%)
  Pallas kernels  25.2 us (12%)
  local copies, waits for them, and re-layouts  15.3 us (7%)
  matrix products  4.77 us (2%)
  other arithmetic  4.21 us (2%)
    ppermute x21, waiting for transfers between devices, swap(): return lax.ppermute(v, axis, [(d, d ^ mask) for d in range(size)])  70.1 us
    ppermute x21, starting transfers between devices, swap(): return lax.ppermute(v, axis, [(d, d ^ mask) for d in range(size)])  29.9 us
    all_to_all x1, waiting for transfers between devices, body(): lax.all_to_all(payload.reshape(tiles * groups, SLOTS, quarter, cols), ('t...  28.7 us
    pallas_call x1, Pallas kernels, body(): pl.pallas_call(attend_kernel, grid_spec=pltpu.PrefetchScalarGridSpec(num_...  12.6 us
    all_to_all x1, starting transfers between devices, body(): lax.all_to_all(payload.reshape(tiles * groups, SLOTS, quarter, cols), ('t...  12 us
    all_to_all x1, starting transfers between devices, body(): lax.all_to_all(marks, 'tile', split_axis=0, concat_axis=0, tiled=True)  11.8 us
    unnamed x53, local copies, waits for them, and re-layouts  11.4 us
  transfers between devices with their start and end apart: 23, of which 16 were waited for; matrix products, arithmetic and copies ran while one was open for 6% of the time, Pallas kernels for 2%

profile of v6, /device:TPU:32, one launch (start us, length us, event | category | flops | bytes accessed | tf_op | source)
XLA Modules:
  0.0 204.9 jit_solution(9702793601391141277)
XLA Ops:
  0.6 2.8 %marks.1 = (f32[64,2,128]{2,1,0:T(2,128)}, s32[128]{0:T(128)}) custom-call(s32[64]{0:T(128)} %bitcast.83, s32[64,128]{1,0:T(8,128)} %bitcast.77, s32[16,64]{1,0:T(8,128)} %bitcast.78), custom_call_target="tpu_custom_call" | custom-call | tf_op jit(solution)/shard_map/marks/pallas_call | solution.py:319
  3.4 11.8 %all-to-all-start = ((f32[64,2,128]{2,1,0:T(2,128)}), f32[64,2,128]{2,1,0:T(2,128)S(1)}, u32[]{:S(2)}, u32[]{:S(2)}) async-start(f32[64,2,128]{2,1,0:T(2,128)} %get-tuple-element.8), calls=%async_computation | async-start | bytes 131072 | tf_op jit(solution)/shard_map/all_to_all | solution.py:340
  15.2 1.6 copy-done.3
  17.5 2.7 %pack.1 = bf16[64,4,2,32,128]{4,3,2,1,0:T(8,128)(2,1)S(1)} custom-call(s32[128]{0:T(128)S(1)} %copy-done.10, bf16[64,4,32,128]{3,2,1,0:T(8,128)(2,1)S(1)} %bitcast.65), custom_call_target="tpu_custom_call" | custom-call | tf_op jit(solution)/shard_map/pack/pallas_call | solution.py:341
  20.2 2.0 copy-done.1
  22.2 1.9 all-to-all-done.found
  24.8 12.0 %all-to-all-start.1 = ((bf16[256,2,32,128]{3,2,1,0:T(8,128)(2,1)}), bf16[256,2,32,128]{3,2,1,0:T(8,128)(2,1)}, u32[]{:S(2)}, u32[]{:S(2)}) async-start(bf16[256,2,32,128]{3,2,1,0:T(8,128)(2,1)} %bitcast.63), calls=%async_computation.1 | async-start | bytes 8388608 | tf_op jit(solution)/shard_map/all_to_all | solution.py:353
  37.3 2.8 %collective-permute-start.2 = (bf16[512,512]{0,1:T(8,128)(2,1)S(1)}, bf16[512,512]{0,1:T(8,128)(2,1)S(1)}, u32[]{:S(2)}, u32[]{:S(2)}) collective-permute-start(bf16[512,512]{0,1:T(8,128)(2,1)S(1)} %get-tuple-element.23), channel_id=1, source_target_pairs={{0,3},{1,2},{2,1},{3,0},{4,7},{5,6},{6,5},{7,4},{8,11},{9,10},{10,... | collective-permute-start | bytes 1572872 | tf_op jit(solution)/shard_map/ppermute | solution.py:312
  40.1 0.8 collective-permute-start.1
  41.5 2.7 %collective-permute-start.5 = (f32[2]{0:T(128)S(1)}, f32[2]{0:T(128)S(1)}, u32[]{:S(2)}, u32[]{:S(2)}) collective-permute-start(f32[2]{0:T(128)S(1)} %copy-done.24), channel_id=1, source_target_pairs={{0,3},{1,2},{2,1},{3,0},{4,7},{5,6},{6,5},{7,4},{8,11},{9,10},{10,... | collective-permute-start | bytes 32 | tf_op jit(solution)/shard_map/ppermute | solution.py:312
  44.2 0.8 collective-permute-start.4
  45.1 41.6 %collective-permute-done.5 = f32[2]{0:T(128)S(1)} collective-permute-done((f32[2]{0:T(128)S(1)}, f32[2]{0:T(128)S(1)}, u32[]{:S(2)}, u32[]{:S(2)}) %collective-permute-start.5) | collective-permute-done | bytes 40 | tf_op jit(solution)/shard_map/ppermute | solution.py:312
  86.8 3.4 %collective-permute-done.3 = f32[2]{0:T(128)S(1)} collective-permute-done((f32[2]{0:T(128)S(1)}, f32[2]{0:T(128)S(1)}, u32[]{:S(2)}, u32[]{:S(2)}) %collective-permute-start.3) | collective-permute-done | bytes 40 | tf_op jit(solution)/shard_map/ppermute | solution.py:312
  90.9 2.1 %lists.1 = (s32[16,256]{1,0:T(8,128)}, f32[128,128]{1,0:T(8,128)}) custom-call(f32[64,2,128]{2,1,0:T(2,128)} %copy-done.16), custom_call_target="tpu_custom_call" | custom-call | tf_op jit(solution)/shard_map/lists/pallas_call | solution.py:361
  93.0 0.8 copy-done.15
  93.8 1.5 pad_maximum_fusion
  95.3 2.0 gather_fusion
  97.3 1.9 broadcast_select_fusion
  99.3 0.8 copy-done.2
  102.9 3.4 %multiply_convert_fusion.qw = bf16[8,512,512]{2,1,0:T(8,128)(2,1)} fusion(bf16[512,8,64]{0,2,1:T(8,128)(2,1)S(1)} %bitcast.70, bf16[512,8,64]{0,2,1:T(8,128)(2,1)S(1)} %bitcast.72), kind=kOutput, calls=%fused_computation.2 | convolution fusion | flops 272629760 | bytes 5242880 | tf_op jit(solution)/shard_map/lhd,khd->hlk/dot_general | solution.py:395
  106.2 28.7 %all-to-all-done.1 = bf16[256,2,32,128]{3,2,1,0:T(8,128)(2,1)} async-done(((bf16[256,2,32,128]{3,2,1,0:T(8,128)(2,1)}), bf16[256,2,32,128]{3,2,1,0:T(8,128)(2,1)}, u32[]{:S(2)}, u32[]{:S(2)}) %all-to-all-start.1) | async-done | bytes 4194336 | tf_op jit(solution)/shard_map/all_to_all | solution.py:353
  134.9 2.2 %copy-done = bf16[8,512,512]{2,1,0:T(8,128)(2,1)S(1)} copy-done((bf16[8,512,512]{2,1,0:T(8,128)(2,1)S(1)}, bf16[8,512,512]{2,1,0:T(8,128)(2,1)}, u32[]{:S(2)}) %copy-start) | copy-done | bytes 4194328
  137.1 12.6 %attend.1 = bf16[512,640]{1,0:T(8,128)(2,1)S(1)} custom-call(s32[16,256]{1,0:T(8,128)S(1)} %copy-done.8, bf16[64,4,2,32,128]{4,3,2,1,0:T(8,128)(2,1)} %bitcast.6.x, f32[128,128]{1,0:T(8,128)S(1)} %copy-done.7, bf16[8,512,512]{2,1,0:T(8,128)(2,1)S(1)} %copy-done, f32[512,128]{1,0:T(8,128)S(1)} %pad_select_fusion.begun, f32[512,512]{1,0:T(8,128)S(1)} %fusion.given, ...), custom_call_target="tpu_custom_call" | custom-call | tf_op jit(solution)/shard_map/attend/pallas_call | solution.py:422
  151.1 1.1 collective-permute-start.7
  152.2 3.0 %collective-permute-start.8 = (bf16[128,640]{1,0:T(8,128)(2,1)S(1)}, bf16[128,640]{1,0:T(8,128)(2,1)S(1)}, u32[]{:S(2)}, u32[]{:S(2)}) collective-permute-start(bf16[128,640]{1,0:T(8,128)(2,1)S(1)} %get-tuple-element.18), channel_id=1, source_target_pairs={{0,3},{1,2},{2,1},{3,0},{4,7},{5,6},{6,5},{7,4},{8,11},{9,10},{10,... | collective-permute-start | bytes 491528 | tf_op jit(solution)/shard_map/ppermute | solution.py:312
  155.2 2.3 %collective-permute-done.6.r1 = bf16[128,640]{1,0:T(8,128)(2,1)S(1)} collective-permute-done((bf16[128,640]{1,0:T(8,128)(2,1)S(1)}, bf16[128,640]{1,0:T(8,128)(2,1)S(1)}, u32[]{:S(2)}, u32[]{:S(2)}) %collective-permute-start.6) | collective-permute-done | bytes 163872 | tf_op jit(solution)/shard_map/ppermute | solution.py:312
  157.4 2.6 %collective-permute-done.7.r2 = bf16[128,640]{1,0:T(8,128)(2,1)S(1)} collective-permute-done((bf16[128,640]{1,0:T(8,128)(2,1)S(1)}, bf16[128,640]{1,0:T(8,128)(2,1)S(1)}, u32[]{:S(2)}, u32[]{:S(2)}) %collective-permute-start.7) | collective-permute-done | bytes 163872 | tf_op jit(solution)/shard_map/ppermute | solution.py:312
  160.0 2.6 %collective-permute-done.8.r3 = bf16[128,640]{1,0:T(8,128)(2,1)S(1)} collective-permute-done((bf16[128,640]{1,0:T(8,128)(2,1)S(1)}, bf16[128,640]{1,0:T(8,128)(2,1)S(1)}, u32[]{:S(2)}, u32[]{:S(2)}) %collective-permute-start.8) | collective-permute-done | bytes 163872 | tf_op jit(solution)/shard_map/ppermute | solution.py:312
  163.2 2.5 %combine.1.a0 = bf16[128,512]{1,0:T(8,128)(2,1)} custom-call(bf16[128,640]{1,0:T(8,128)(2,1)} %get-tuple-element.21.r0, bf16[128,640]{1,0:T(8,128)(2,1)} %copy-done.17, bf16[128,640]{1,0:T(8,128)(2,1)} %copy-done.18, bf16[128,640]{1,0:T(8,128)(2,1)} %copy-done.19), custom_call_target="tpu_custom_call" | custom-call | tf_op jit(solution)/shard_map/combine/pallas_call | solution.py:447
  165.7 2.9 %collective-permute-start.10 = (bf16[128,512]{1,0:T(8,128)(2,1)}, bf16[128,512]{1,0:T(8,128)(2,1)S(1)}, u32[]{:S(2)}, u32[]{:S(2)}) collective-permute-start(bf16[128,512]{1,0:T(8,128)(2,1)} %combine.1.a0), channel_id=1, source_target_pairs={{0,2},{1,3},{2,0},{3,1},{4,6},{5,7},{6,4},{7,5},{8,10},{9,11},{10,... | collective-permute-start | bytes 393224 | tf_op jit(solution)/shard_map/ppermute | solution.py:312
  168.6 1.8 collective-permute-start.11
  170.4 1.7 collective-permute-done.9.a1
  172.1 1.8 collective-permute-done.10.a2
  173.9 1.5 collective-permute-done.11.a3
  175.5 0.9 copy-done.4
  176.4 2.5 %finish.1 = (f32[512,128]{1,0:T(8,128)}, f32[128,128]{1,0:T(8,128)S(1)}) custom-call(s32[1]{0:T(128)} %bitcast.place, bf16[128,512]{1,0:T(8,128)(2,1)S(1)} %copy-done.4, bf16[128,512]{1,0:T(8,128)(2,1)S(1)} %collective-permute-done.9.a1, bf16[128,512]{1,0:T(8,128)(2,1)S(1)} %collective-permute-done.10.a2, bf16[128,512]{1,0:T(8,128)(2,1)S(1)} %collective-permute-done.11.a3, ...), custom_call_target="tpu_custom_call" | custom-call | tf_op jit(solution)/shard_map/finish/pallas_call | solution.py:456
  178.9 2.3 %collective-permute-start.13 = (f32[128,128]{1,0:T(8,128)S(1)}, f32[128,128]{1,0:T(8,128)S(1)}, u32[]{:S(2)}, u32[]{:S(2)}) collective-permute-start(f32[128,128]{1,0:T(8,128)S(1)} %get-tuple-element.13), channel_id=1, source_target_pairs={{0,8},{4,12},{8,0},{12,4},{16,24},{20,28},{24,16},{28,20},{32,40},... | collective-permute-start | bytes 196616 | tf_op jit(solution)/shard_map/ppermute | solution.py:312
  181.4 2.1 %collective-permute-done.13 = f32[128,128]{1,0:T(8,128)S(1)} collective-permute-done((f32[128,128]{1,0:T(8,128)S(1)}, f32[128,128]{1,0:T(8,128)S(1)}, u32[]{:S(2)}, u32[]{:S(2)}) %collective-permute-start.13) | collective-permute-done | bytes 65568 | tf_op jit(solution)/shard_map/ppermute | solution.py:312
  183.5 1.4 collective-permute-done.14
  185.0 2.3 %collective-permute-start.16 = (f32[128,128]{1,0:T(8,128)S(1)}, f32[128,128]{1,0:T(8,128)S(1)}, u32[]{:S(2)}, u32[]{:S(2)}) collective-permute-start(f32[128,128]{1,0:T(8,128)S(1)} %add_add_fusion.1), channel_id=1, source_target_pairs={{0,32},{4,36},{8,40},{12,44},{16,48},{20,52},{24,56},{28,60},{32,0... | collective-permute-start | bytes 196616 | tf_op jit(solution)/shard_map/ppermute | solution.py:312
  187.2 1.4 collective-permute-start.17
  188.6 3.0 %collective-permute-start.15 = (f32[128,128]{1,0:T(8,128)S(1)}, f32[128,128]{1,0:T(8,128)S(1)}, u32[]{:S(2)}, u32[]{:S(2)}) collective-permute-start(f32[128,128]{1,0:T(8,128)S(1)} %add_add_fusion.1), channel_id=1, source_target_pairs={{0,16},{4,20},{8,24},{12,28},{16,0},{20,4},{24,8},{28,12},{32,48},... | collective-permute-start | bytes 196616 | tf_op jit(solution)/shard_map/ppermute | solution.py:312
  191.6 3.4 %collective-permute-done.16 = f32[128,128]{1,0:T(8,128)S(1)} collective-permute-done((f32[128,128]{1,0:T(8,128)S(1)}, f32[128,128]{1,0:T(8,128)S(1)}, u32[]{:S(2)}, u32[]{:S(2)}) %collective-permute-start.16) | collective-permute-done | bytes 65568 | tf_op jit(solution)/shard_map/ppermute | solution.py:312
  194.9 1.5 collective-permute-done.17
  196.4 2.3 %collective-permute-start.19 = (f32[128,128]{1,0:T(8,128)S(1)}, f32[128,128]{1,0:T(8,128)S(1)}, u32[]{:S(2)}, u32[]{:S(2)}) collective-permute-start(f32[128,128]{1,0:T(8,128)S(1)} %add_add_fusion), channel_id=1, source_target_pairs={{0,128},{4,132},{8,136},{12,140},{16,144},{20,148},{24,152},{28,15... | collective-permute-start | bytes 196616 | tf_op jit(solution)/shard_map/ppermute | solution.py:312
  198.8 1.1 collective-permute-start.20
  200.0 2.3 %collective-permute-done.19 = f32[128,128]{1,0:T(8,128)S(1)} collective-permute-done((f32[128,128]{1,0:T(8,128)S(1)}, f32[128,128]{1,0:T(8,128)S(1)}, u32[]{:S(2)}, u32[]{:S(2)}) %collective-permute-start.19) | collective-permute-done | bytes 65568 | tf_op jit(solution)/shard_map/ppermute | solution.py:312
  202.3 2.0 collective-permute-done.20
  (82 shorter events, 9.0 us)
Async XLA Ops:
  3.4 20.7 %all-to-all-start = ((f32[64,2,128]{2,1,0:T(2,128)}), f32[64,2,128]{2,1,0:T(2,128)S(1)}, u32[]{:S(2)}, u32[]{:S(2)}) async-start(f32[64,2,128]{2,1,0:T(2,128)} %get-tuple-element.8), calls=%async_computation | async-start | bytes 131072 | tf_op jit(solution)/shard_map/all_to_all | solution.py:340
  15.2 1.6 copy-start.3
  16.8 0.7 copy-start.10
  20.2 2.0 copy-start.1
  24.2 0.6 copy-start.16
  24.2 12.6 %copy-start.21 = (bf16[512,128]{1,0:T(8,128)(2,1)S(1)}, bf16[512,128]{1,0:T(8,128)(2,1)}, u32[]{:S(2)}) copy-start(bf16[512,128]{1,0:T(8,128)(2,1)} %param.20) | copy-start | bytes 393220
  24.2 12.8 %copy-start.22 = (bf16[512,128]{1,0:T(8,128)(2,1)S(1)}, bf16[512,128]{1,0:T(8,128)(2,1)}, u32[]{:S(2)}) copy-start(bf16[512,128]{1,0:T(8,128)(2,1)} %param.19) | copy-start | bytes 393220
  24.2 12.9 %copy-start.23 = (bf16[512,128]{1,0:T(8,128)(2,1)S(1)}, bf16[512,128]{1,0:T(8,128)(2,1)}, u32[]{:S(2)}) copy-start(bf16[512,128]{1,0:T(8,128)(2,1)} %param.18) | copy-start | bytes 393220
  24.2 13.0 %copy-start.20 = (bf16[128,512]{1,0:T(8,128)(2,1)S(1)}, bf16[128,512]{1,0:T(8,128)(2,1)}, u32[]{:S(2)}) copy-start(bf16[128,512]{1,0:T(8,128)(2,1)} %param.22) | copy-start | bytes 393220
  24.8 110.1 %all-to-all-start.1 = ((bf16[256,2,32,128]{3,2,1,0:T(8,128)(2,1)}), bf16[256,2,32,128]{3,2,1,0:T(8,128)(2,1)}, u32[]{:S(2)}, u32[]{:S(2)}) async-start(bf16[256,2,32,128]{3,2,1,0:T(8,128)(2,1)} %bitcast.63), calls=%async_computation.1 | async-start | bytes 8388608 | tf_op jit(solution)/shard_map/all_to_all | solution.py:353
  36.8 4.7 %copy-start.24 = (f32[2]{0:T(128)S(1)}, f32[2]{0:T(128)}, u32[]{:S(2)}) copy-start(f32[2]{0:T(128)} %param.21) | copy-start | bytes 28
  37.3 55.7 %collective-permute-start.2 = (bf16[512,512]{0,1:T(8,128)(2,1)S(1)}, bf16[512,512]{0,1:T(8,128)(2,1)S(1)}, u32[]{:S(2)}, u32[]{:S(2)}) collective-permute-start(bf16[512,512]{0,1:T(8,128)(2,1)S(1)} %get-tuple-element.23), channel_id=1, source_target_pairs={{0,3},{1,2},{2,1},{3,0},{4,7},{5,6},{6,5},{7,4},{8,11},{9,10},{10,... | collective-permute-start | bytes 1572872 | tf_op jit(solution)/shard_map/ppermute | solution.py:312
  40.1 52.9 %collective-permute-start.1 = (bf16[512,512]{0,1:T(8,128)(2,1)S(1)}, bf16[512,512]{0,1:T(8,128)(2,1)}, u32[]{:S(2)}, u32[]{:S(2)}) collective-permute-start(bf16[512,512]{0,1:T(8,128)(2,1)S(1)} %get-tuple-element.23), channel_id=1, source_target_pairs={{0,2},{1,3},{2,0},{3,1},{4,6},{5,7},{6,4},{7,5},{8,10},{9,11},{10,... | collective-permute-start | bytes 1572872 | tf_op jit(solution)/shard_map/ppermute | solution.py:312
  40.9 52.1 %collective-permute-start = (bf16[512,512]{0,1:T(8,128)(2,1)S(1)}, bf16[512,512]{0,1:T(8,128)(2,1)S(1)}, u32[]{:S(2)}, u32[]{:S(2)}) collective-permute-start(bf16[512,512]{0,1:T(8,128)(2,1)S(1)} %get-tuple-element.23), channel_id=1, source_target_pairs={{0,1},{1,0},{2,3},{3,2},{4,5},{5,4},{6,7},{7,6},{8,9},{9,8},{10,11... | collective-permute-start | bytes 1572872 | tf_op jit(solution)/shard_map/ppermute | solution.py:312
  41.5 45.2 %collective-permute-start.5 = (f32[2]{0:T(128)S(1)}, f32[2]{0:T(128)S(1)}, u32[]{:S(2)}, u32[]{:S(2)}) collective-permute-start(f32[2]{0:T(128)S(1)} %copy-done.24), channel_id=1, source_target_pairs={{0,3},{1,2},{2,1},{3,0},{4,7},{5,6},{6,5},{7,4},{8,11},{9,10},{10,... | collective-permute-start | bytes 32 | tf_op jit(solution)/shard_map/ppermute | solution.py:312
  44.2 42.6 %collective-permute-start.4 = (f32[2]{0:T(128)S(1)}, f32[2]{0:T(128)S(1)}, u32[]{:S(2)}, u32[]{:S(2)}) collective-permute-start(f32[2]{0:T(128)S(1)} %copy-done.24), channel_id=1, source_target_pairs={{0,2},{1,3},{2,0},{3,1},{4,6},{5,7},{6,4},{7,5},{8,10},{9,11},{10,... | collective-permute-start | bytes 32 | tf_op jit(solution)/shard_map/ppermute | solution.py:312
  86.6 3.5 %collective-permute-start.3 = (f32[2]{0:T(128)S(1)}, f32[2]{0:T(128)S(1)}, u32[]{:S(2)}, u32[]{:S(2)}) collective-permute-start(f32[2]{0:T(128)S(1)} %copy-done.24), channel_id=1, source_target_pairs={{0,1},{1,0},{2,3},{3,2},{4,5},{5,4},{6,7},{7,6},{8,9},{9,8},{10,11... | collective-permute-start | bytes 32 | tf_op jit(solution)/shard_map/ppermute | solution.py:312
  93.0 0.8 copy-start.15
  99.1 1.0 copy-start.2
  99.3 2.3 %copy-start.13 = (bf16[4,512,128]{1,2,0:T(8,128)(2,1)}, bf16[4,512,128]{1,2,0:T(8,128)(2,1)S(1)}, u32[]{:S(2)}) copy-start(bf16[4,512,128]{1,2,0:T(8,128)(2,1)S(1)} %get-tuple-element.16) | copy-start | bytes 1572868
  100.6 0.8 copy-start.11
  101.7 1.0 copy-start.12
  101.7 1.2 copy-start.14
  102.9 32.0 %copy-start.7 = (f32[128,128]{1,0:T(8,128)S(1)}, f32[128,128]{1,0:T(8,128)}, u32[]{:S(2)}) copy-start(f32[128,128]{1,0:T(8,128)} %get-tuple-element.11.bias) | copy-start | bytes 196612
  102.9 32.0 %copy-start.8 = (s32[16,256]{1,0:T(8,128)S(1)}, s32[16,256]{1,0:T(8,128)}, u32[]{:S(2)}) copy-start(s32[16,256]{1,0:T(8,128)} %get-tuple-element.9.lists) | copy-start | bytes 49156
  134.9 2.2 %copy-start = (bf16[8,512,512]{2,1,0:T(8,128)(2,1)S(1)}, bf16[8,512,512]{2,1,0:T(8,128)(2,1)}, u32[]{:S(2)}) copy-start(bf16[8,512,512]{2,1,0:T(8,128)(2,1)} %multiply_convert_fusion.qw) | copy-start | bytes 12582916
  149.7 25.8 %copy-start.5 = (bf16[512,128]{1,0:T(8,128)(2,1)S(1)}, bf16[512,128]{1,0:T(8,128)(2,1)}, u32[]{:S(2)}) copy-start(bf16[512,128]{1,0:T(8,128)(2,1)} %w_inc.1) | copy-start | bytes 393220
  149.7 25.8 %copy-start.6 = (bf16[512,128]{1,0:T(8,128)(2,1)S(1)}, bf16[512,128]{1,0:T(8,128)(2,1)}, u32[]{:S(2)}) copy-start(bf16[512,128]{1,0:T(8,128)(2,1)} %target.1) | copy-start | bytes 393220
  149.7 25.8 %copy-start.9 = (f32[512]{0:T(512)S(1)}, f32[512]{0:T(512)}, u32[]{:S(2)}) copy-start(f32[512]{0:T(512)} %param.23) | copy-start | bytes 6148
  150.5 7.0 %collective-permute-start.6 = (bf16[128,640]{1,0:T(8,128)(2,1)S(1)}, bf16[128,640]{1,0:T(8,128)(2,1)S(1)}, u32[]{:S(2)}, u32[]{:S(2)}) collective-permute-start(bf16[128,640]{1,0:T(8,128)(2,1)S(1)} %get-tuple-element.20), channel_id=1, source_target_pairs={{0,1},{1,0},{2,3},{3,2},{4,5},{5,4},{6,7},{7,6},{8,9},{9,8},{10,11... | collective-permute-start | bytes 491528 | tf_op jit(solution)/shard_map/ppermute | solution.py:312
  151.1 8.9 %collective-permute-start.7 = (bf16[128,640]{1,0:T(8,128)(2,1)S(1)}, bf16[128,640]{1,0:T(8,128)(2,1)S(1)}, u32[]{:S(2)}, u32[]{:S(2)}) collective-permute-start(bf16[128,640]{1,0:T(8,128)(2,1)S(1)} %get-tuple-element.19), channel_id=1, source_target_pairs={{0,2},{1,3},{2,0},{3,1},{4,6},{5,7},{6,4},{7,5},{8,10},{9,11},{10,... | collective-permute-start | bytes 491528 | tf_op jit(solution)/shard_map/ppermute | solution.py:312
  152.2 10.4 %collective-permute-start.8 = (bf16[128,640]{1,0:T(8,128)(2,1)S(1)}, bf16[128,640]{1,0:T(8,128)(2,1)S(1)}, u32[]{:S(2)}, u32[]{:S(2)}) collective-permute-start(bf16[128,640]{1,0:T(8,128)(2,1)S(1)} %get-tuple-element.18), channel_id=1, source_target_pairs={{0,3},{1,2},{2,1},{3,0},{4,7},{5,6},{6,5},{7,4},{8,11},{9,10},{10,... | collective-permute-start | bytes 491528 | tf_op jit(solution)/shard_map/ppermute | solution.py:312
  157.4 5.1 %copy-start.17 = (bf16[128,640]{1,0:T(8,128)(2,1)}, bf16[128,640]{1,0:T(8,128)(2,1)S(1)}, u32[]{:S(2)}) copy-start(bf16[128,640]{1,0:T(8,128)(2,1)S(1)} %collective-permute-done.6.r1) | copy-start | bytes 491524
  160.0 2.6 %copy-start.18 = (bf16[128,640]{1,0:T(8,128)(2,1)}, bf16[128,640]{1,0:T(8,128)(2,1)S(1)}, u32[]{:S(2)}) copy-start(bf16[128,640]{1,0:T(8,128)(2,1)S(1)} %collective-permute-done.7.r2) | copy-start | bytes 491524
  162.6 0.7 copy-start.19
  165.7 6.4 %collective-permute-start.9 = (bf16[128,512]{1,0:T(8,128)(2,1)}, bf16[128,512]{1,0:T(8,128)(2,1)S(1)}, u32[]{:S(2)}, u32[]{:S(2)}) collective-permute-start(bf16[128,512]{1,0:T(8,128)(2,1)} %combine.1.a0), channel_id=1, source_target_pairs={{0,1},{1,0},{2,3},{3,2},{4,5},{5,4},{6,7},{7,6},{8,9},{9,8},{10,11... | collective-permute-start | bytes 393224 | tf_op jit(solution)/shard_map/ppermute | solution.py:312
  165.7 8.2 %collective-permute-start.10 = (bf16[128,512]{1,0:T(8,128)(2,1)}, bf16[128,512]{1,0:T(8,128)(2,1)S(1)}, u32[]{:S(2)}, u32[]{:S(2)}) collective-permute-start(bf16[128,512]{1,0:T(8,128)(2,1)} %combine.1.a0), channel_id=1, source_target_pairs={{0,2},{1,3},{2,0},{3,1},{4,6},{5,7},{6,4},{7,5},{8,10},{9,11},{10,... | collective-permute-start | bytes 393224 | tf_op jit(solution)/shard_map/ppermute | solution.py:312
  168.6 6.9 %collective-permute-start.11 = (bf16[128,512]{1,0:T(8,128)(2,1)}, bf16[128,512]{1,0:T(8,128)(2,1)S(1)}, u32[]{:S(2)}, u32[]{:S(2)}) collective-permute-start(bf16[128,512]{1,0:T(8,128)(2,1)} %combine.1.a0), channel_id=1, source_target_pairs={{0,3},{1,2},{2,1},{3,0},{4,7},{5,6},{6,5},{7,4},{8,11},{9,10},{10,... | collective-permute-start | bytes 393224 | tf_op jit(solution)/shard_map/ppermute | solution.py:312
  175.5 0.9 copy-start.4
  178.9 4.6 %collective-permute-start.13 = (f32[128,128]{1,0:T(8,128)S(1)}, f32[128,128]{1,0:T(8,128)S(1)}, u32[]{:S(2)}, u32[]{:S(2)}) collective-permute-start(f32[128,128]{1,0:T(8,128)S(1)} %get-tuple-element.13), channel_id=1, source_target_pairs={{0,8},{4,12},{8,0},{12,4},{16,24},{20,28},{24,16},{28,20},{32,40},... | collective-permute-start | bytes 196616 | tf_op jit(solution)/shard_map/ppermute | solution.py:312
  181.3 3.7 %collective-permute-start.14 = (f32[128,128]{1,0:T(8,128)S(1)}, f32[128,128]{1,0:T(8,128)S(1)}, u32[]{:S(2)}, u32[]{:S(2)}) collective-permute-start(f32[128,128]{1,0:T(8,128)S(1)} %get-tuple-element.13), channel_id=1, source_target_pairs={{0,12},{4,8},{8,4},{12,0},{16,28},{20,24},{24,20},{28,16},{32,44},... | collective-permute-start | bytes 196616 | tf_op jit(solution)/shard_map/ppermute | solution.py:312
  181.3 3.7 %collective-permute-start.12 = (f32[128,128]{1,0:T(8,128)S(1)}, f32[128,128]{1,0:T(8,128)S(1)}, u32[]{:S(2)}, u32[]{:S(2)}) collective-permute-start(f32[128,128]{1,0:T(8,128)S(1)} %get-tuple-element.13), channel_id=1, source_target_pairs={{0,4},{4,0},{8,12},{12,8},{16,20},{20,16},{24,28},{28,24},{32,36},... | collective-permute-start | bytes 196616 | tf_op jit(solution)/shard_map/ppermute | solution.py:312
  185.0 9.9 %collective-permute-start.16 = (f32[128,128]{1,0:T(8,128)S(1)}, f32[128,128]{1,0:T(8,128)S(1)}, u32[]{:S(2)}, u32[]{:S(2)}) collective-permute-start(f32[128,128]{1,0:T(8,128)S(1)} %add_add_fusion.1), channel_id=1, source_target_pairs={{0,32},{4,36},{8,40},{12,44},{16,48},{20,52},{24,56},{28,60},{32,0... | collective-permute-start | bytes 196616 | tf_op jit(solution)/shard_map/ppermute | solution.py:312
  187.2 9.2 %collective-permute-start.17 = (f32[128,128]{1,0:T(8,128)S(1)}, f32[128,128]{1,0:T(8,128)S(1)}, u32[]{:S(2)}, u32[]{:S(2)}) collective-permute-start(f32[128,128]{1,0:T(8,128)S(1)} %add_add_fusion.1), channel_id=1, source_target_pairs={{0,48},{4,52},{8,56},{12,60},{16,32},{20,36},{24,40},{28,44},{32,1... | collective-permute-start | bytes 196616 | tf_op jit(solution)/shard_map/ppermute | solution.py:312
  188.6 7.8 %collective-permute-start.15 = (f32[128,128]{1,0:T(8,128)S(1)}, f32[128,128]{1,0:T(8,128)S(1)}, u32[]{:S(2)}, u32[]{:S(2)}) collective-permute-start(f32[128,128]{1,0:T(8,128)S(1)} %add_add_fusion.1), channel_id=1, source_target_pairs={{0,16},{4,20},{8,24},{12,28},{16,0},{20,4},{24,8},{28,12},{32,48},... | collective-permute-start | bytes 196616 | tf_op jit(solution)/shard_map/ppermute | solution.py:312
  196.4 5.9 %collective-permute-start.19 = (f32[128,128]{1,0:T(8,128)S(1)}, f32[128,128]{1,0:T(8,128)S(1)}, u32[]{:S(2)}, u32[]{:S(2)}) collective-permute-start(f32[128,128]{1,0:T(8,128)S(1)} %add_add_fusion), channel_id=1, source_target_pairs={{0,128},{4,132},{8,136},{12,140},{16,144},{20,148},{24,152},{28,15... | collective-permute-start | bytes 196616 | tf_op jit(solution)/shard_map/ppermute | solution.py:312
  198.8 5.5 %collective-permute-start.20 = (f32[128,128]{1,0:T(8,128)S(1)}, f32[128,128]{1,0:T(8,128)S(1)}, u32[]{:S(2)}, u32[]{:S(2)}) collective-permute-start(f32[128,128]{1,0:T(8,128)S(1)} %add_add_fusion), channel_id=1, source_target_pairs={{0,192},{4,196},{8,200},{12,204},{16,208},{20,212},{24,216},{28,22... | collective-permute-start | bytes 196616 | tf_op jit(solution)/shard_map/ppermute | solution.py:312
  199.8 4.4 %collective-permute-start.18 = (f32[128,128]{1,0:T(8,128)S(1)}, f32[128,128]{1,0:T(8,128)S(1)}, u32[]{:S(2)}, u32[]{:S(2)}) collective-permute-start(f32[128,128]{1,0:T(8,128)S(1)} %add_add_fusion), channel_id=1, source_target_pairs={{0,64},{4,68},{8,72},{12,76},{16,80},{20,84},{24,88},{28,92},{32,9... | collective-permute-start | bytes 196616 | tf_op jit(solution)/shard_map/ppermute | solution.py:312

commit v7 on v6

--- a/solution.py
+++ b/solution.py
@@ -1,3 +1,4 @@
+import functools
 import math
 
 import jax
@@ -12,18 +13,18 @@
 NEG = -1e30
 SLOTS = 2
 CHUNK = 8
-PAIR = 4
-MARK_ROWS = 2
-
-
-def marks_kernel(owner, row_marks, pattern, marks, slots, info, taken):
-    tiles = marks.shape[0]
-    blocks = row_marks.shape[0]
+PAIR = 8
+DEPTH = 6
+NEAR = (1, 16, 17, 48, 49, 2, 3, 32)
+
+
+def route_kernel(spill, owner, alive, obs, row_marks, pattern, sent, info, lanes, extra, near):
+    tiles = sent.shape[0]
+    blocks, parts, quarter = obs.shape[:3]
     subs = pattern.shape[0]
-    quarter = 32
-    j = lax.axis_index("head")
-    turned = pltpu.roll(row_marks[...].astype(F32), (128 - j * quarter) % 128, 1)
+    me = lax.axis_index("tile")
     lane = lax.broadcasted_iota(jnp.int32, (blocks, 128), 1)
+    rows = row_marks[...].astype(F32)
     spot = lax.broadcasted_iota(jnp.int32, (subs, 128), 1)
     line = lax.broadcasted_iota(jnp.int32, (subs, 128), 0)
     shift = (spot == line + quarter).astype(F32).astype(BF)
@@ -33,59 +34,169 @@
         (((0,), (0,)), ((), ())),
         preferred_element_type=F32,
     )
-    info[...] = jnp.where(lane < quarter, turned, groups)
-    marks[...] = jnp.zeros_like(marks)
+    for j in range(parts):
+        turned = rows if j == 0 else pltpu.roll(rows, 128 - j * quarter, 1)
+        info[j, :blocks] = jnp.where(lane < quarter, turned, groups)
+        info[j, blocks:] = jnp.zeros((8, 128), F32)
+    for m, mask in enumerate(NEAR):
+        near[m] = mask
 
     def clear(t, carry):
-        taken[t] = 0
-        slots[t] = blocks
-        slots[tiles + t] = blocks
+        lanes[t] = blocks
+        lanes[tiles + t] = 0
         return carry
 
     lax.fori_loop(0, tiles, clear, 0, unroll=8)
+    extra[blocks] = 0
 
     def place(b, carry):
         t = owner[b]
-        k = jnp.minimum(taken[t], SLOTS - 1)
-        taken[t] = k + 1
-        slots[k * tiles + t] = b
-        marks[t, pl.ds(k, 1), :] = info[pl.ds(b, 1), :]
+
+        @pl.when(alive[b] > 0)
+        def _():
+            seen = lanes[tiles + t]
+            lanes[tiles + t] = 1
+            take = (seen == 0) if spill else (seen > 0)
+
+            @pl.when(take)
+            def _():
+                lanes[t] = b
+
+            @pl.when(jnp.logical_not(take))
+            def _():
+                n = extra[blocks]
+                extra[n] = b
+                extra[blocks] = n + 1
+
         return carry
 
-    lax.fori_loop(0, blocks, place, 0, unroll=4)
-
-
-def pack_kernel(slots, obs, payload):
-    tiles = payload.shape[0]
-    blocks = obs.shape[0]
+    lax.fori_loop(0, blocks, place, 0)
+    left = jnp.int32(0)
+    if spill:
+
+        def move(q, left):
+            b = extra[q]
+            t = owner[b]
+            found = jnp.int32(tiles)
+            for a in range(len(NEAR)):
+                other = t ^ near[(me + q + a) % len(NEAR)]
+                free = (lanes[other] == blocks) & (found == tiles)
+                found = jnp.where(free, other, found)
+
+            @pl.when(found < tiles)
+            def _():
+                lanes[found] = b
+
+            return left + (found == tiles).astype(jnp.int32)
+
+        left = lax.fori_loop(0, extra[blocks], move, left)
+
+    lane1 = lax.broadcasted_iota(jnp.int32, (1, 128), 1)
+
+    def goal(t):
+        b = lanes[t]
+        return jnp.where(b < blocks, owner[jnp.minimum(b, blocks - 1)] + 1, 0)
+
+    def note(t, table):
+        return jnp.where(lane1 == t, goal(t).astype(F32), table)
+
+    table = jnp.where(lane1 == tiles, left.astype(F32), jnp.zeros((1, 128), F32))
+    table = lax.fori_loop(0, tiles, note, table)
+    line8 = lax.broadcasted_iota(jnp.int32, (8, 128), 0)
 
     def fill(t, carry):
-        for k in range(SLOTS):
-            b = slots[k * tiles + t]
-
-            @pl.when(b < blocks)
-            def _():
-                payload[t, :, k] = obs[b]
-
-            @pl.when(b >= blocks)
-            def _():
-                payload[t, :, k] = jnp.zeros(obs.shape[1:], BF)
+        b = lanes[t]
+        to = jnp.where(lane1 == quarter + subs, goal(t).astype(F32), 0.0)
+        for j in range(parts):
+            one = info[j, pl.ds(b, 1), :] + to
+            tail = jnp.where(line8 == 0, one, jnp.where(line8 == 1, table, 0.0))
+            sent[t, j, quarter:, :] = tail.astype(BF)
+
+        @pl.when(b < blocks)
+        def _():
+            sent[t, :, :quarter, :] = obs[b]
+
+        @pl.when(b >= blocks)
+        def _():
+            sent[t, :, :quarter, :] = jnp.zeros(obs.shape[1:], BF)
 
         return carry
 
     lax.fori_loop(0, tiles, fill, 0)
 
 
-def lists_kernel(found, lists, bias):
-    tiles = found.shape[0]
-    slots = SLOTS * tiles
+def before(n):
+    return (
+        lax.broadcasted_iota(jnp.int32, (n, n), 0) < lax.broadcasted_iota(jnp.int32, (n, n), 1)
+    ).astype(F32).astype(BF)
+
+
+def listing(live):
+    rows, n = live.shape
+    place = jnp.dot(live.astype(BF), before(n), preferred_element_type=F32)
+    turn = lax.broadcasted_iota(jnp.int32, (rows, 128, n), 1).astype(F32)
+    name = lax.broadcasted_iota(jnp.int32, (rows, 128, n), 2).astype(F32)
+    hit = (place[:, None, :] == turn) & (live[:, None, :] > 0.5)
+    order = jnp.sum(jnp.where(hit, name, 0.0), axis=2)
+    return order, jnp.sum(live, axis=1, keepdims=True)
+
+
+def plan_kernel(arrived, plan):
+    tiles = arrived.shape[0]
+    near = len(NEAR)
+    me = lax.axis_index("tile")
+    table = arrived[:, 0, 32:40, :].astype(F32)[:, 1, :]
+    mine = (lax.broadcasted_iota(jnp.int32, (near, 128), 1) == me).astype(F32).astype(BF)
+    goals = lax.dot_general(
+        mine, table.astype(BF), (((1,), (1,)), ((), ())), preferred_element_type=F32
+    )
+    line = lax.broadcasted_iota(jnp.int32, (near, tiles), 0)
+    want = jnp.zeros((near, tiles), jnp.int32)
+    for m, mask in enumerate(NEAR):
+        want = jnp.where(line == m, (me ^ mask) + 1, want)
+    order, count = listing((goals == want.astype(F32)).astype(F32))
+    place = lax.broadcasted_iota(jnp.int32, (near, 128), 1)
+    plan[:near] = jnp.where(place.astype(F32) < count, order, tiles).astype(jnp.int32)
+    lane = lax.broadcasted_iota(jnp.int32, (1, 128), 1)
+    worst = jnp.zeros((1, 128), F32)
+    for mask in NEAR:
+        here = (table == ((lane ^ mask) + 1).astype(F32)).astype(F32)
+        total = jnp.sum(here, axis=0, keepdims=True)
+        worst = jnp.maximum(worst, jnp.where(lane < tiles, total, 0.0))
+    left = jnp.sum(jnp.where(lane == tiles, table, 0.0), axis=0, keepdims=True)
+    bad = jnp.max(jnp.where(worst > DEPTH, 1.0, left), axis=1, keepdims=True)
+    good = jnp.where(bad > 0.0, 0, 1)
+    plan[near:] = jnp.broadcast_to(good, (near, 128))
+
+
+def forward_kernel(plan, arrived, *outs):
+    tiles = arrived.shape[0]
+    for m, out in enumerate(outs):
+        for c in range(DEPTH):
+            s = plan[m, c]
+
+            @pl.when(s < tiles)
+            def _(s=s, out=out, c=c):
+                out[c] = arrived[s]
+
+            @pl.when(s >= tiles)
+            def _(out=out, c=c):
+                out[c] = jnp.zeros(out.shape[1:], BF)
+
+
+def lists_kernel(*refs):
+    *units, lists, bias, found = refs
     quarter = 32
     subs = lists.shape[0]
-    mine = jnp.concatenate([found[:, k, :] for k in range(SLOTS)], axis=0).astype(BF)
-    ahead = (
-        lax.broadcasted_iota(jnp.int32, (slots, slots), 0)
-        < lax.broadcasted_iota(jnp.int32, (slots, slots), 1)
-    ).astype(F32).astype(BF)
+    at = 0
+    for unit in units:
+        n = unit.shape[0]
+        found[at:at + n, :] = unit[:, 0, quarter:quarter + 8, :].astype(F32)[:, 0, :]
+        at += n
+    me = lax.axis_index("tile")
+    marks = found[...]
+    to = marks[:, quarter + subs:quarter + subs + 1]
+    marks = jnp.where(to == (me + 1).astype(F32), marks, 0.0).astype(BF)
     pick_group = (
         lax.broadcasted_iota(jnp.int32, (subs, 128), 1)
         == lax.broadcasted_iota(jnp.int32, (subs, 128), 0) + quarter
@@ -94,17 +205,12 @@
     along = lax.broadcasted_iota(jnp.int32, (128, 128), 1)
     widen = ((up < quarter) & (up == along % quarter)).astype(F32).astype(BF)
     live = lax.dot_general(
-        pick_group, mine, (((1,), (1,)), ((), ())), preferred_element_type=F32
-    )
-    place = jnp.dot(live.astype(BF), ahead, preferred_element_type=F32)
-    turn = lax.broadcasted_iota(jnp.int32, (subs, slots, slots), 1).astype(F32)
-    name = lax.broadcasted_iota(jnp.int32, (subs, slots, slots), 2).astype(F32)
-    hit = (place[:, None, :] == turn) & (live[:, None, :] > 0.5)
-    order = jnp.sum(jnp.where(hit, name, 0.0), axis=2)
-    count = jnp.sum(live, axis=1, keepdims=True)
+        pick_group, marks, (((1,), (1,)), ((), ())), preferred_element_type=F32
+    )
+    order, count = listing(live)
     lists[:, :128] = order.astype(jnp.int32)
     lists[:, 128:] = jnp.broadcast_to(count, (subs, 128)).astype(jnp.int32)
-    rows = jnp.dot(mine, widen, preferred_element_type=F32)
+    rows = jnp.dot(marks, widen, preferred_element_type=F32)
     bias[...] = (rows - 1.0) * (-NEG)
 
 
@@ -114,12 +220,29 @@
     return hi, mid, v - hi - mid
 
 
-def attend_kernel(lists, x, bias, qw, begun, given, wv, out, *scratch):
+def attend_kernel(lists, *refs):
+    units = refs[:len(NEAR) + 2]
+    bias, qw, begun, given, wv, out, x, sems, *scratch = refs[len(NEAR) + 2:]
     step_id = pl.program_id(0)
+
+    @pl.when(step_id == 0)
+    def _():
+        copies = []
+        at = 0
+        for u, unit in enumerate(units):
+            n = unit.shape[0]
+            copies.append(pltpu.make_async_copy(unit, x.at[pl.ds(at, n)], sems.at[u]))
+            at += n
+        for copy in copies:
+            copy.start()
+        for copy in copies:
+            copy.wait()
+
     heads, both, width = qw.shape
     sub = both // PAIR
     rows = heads * sub
-    tiles, parts, _, quarter, cols = x.shape
+    quarter = 32
+    parts, _, cols = x.shape[1:]
     size = CHUNK * quarter
     per = 128 // quarter
     lane_slot = lax.broadcasted_iota(jnp.int32, (1, 128), 1) // quarter
@@ -136,7 +259,7 @@
                 s = lists[g, jnp.maximum(jnp.minimum(place, n - 1), 0)]
                 for i in range(parts):
                     xbuf[u * quarter:(u + 1) * quarter, i * cols:(i + 1) * cols] = x[
-                        s % tiles, i, s // tiles
+                        s, i, :quarter, :
                     ]
                 live = (lane_slot == v) & (place < n)
                 shade = jnp.where(live, bias[pl.ds(s, 1), :], shade)
@@ -316,59 +439,92 @@
 
     tile = lax.axis_index("tile")
     whole = lambda *shape: pl.BlockSpec(shape, lambda g, *_: (0,) * len(shape))
-    marks, taken = pl.pallas_call(
-        marks_kernel,
-        grid_spec=pltpu.PrefetchScalarGridSpec(
-            num_scalar_prefetch=1,
-            grid=(1,),
-            in_specs=[whole(blocks, block_rows), whole(subs, blocks)],
-            out_specs=[
-                whole(tiles, MARK_ROWS, 128),
-                pl.BlockSpec(memory_space=pltpu.SMEM),
-            ],
-            scratch_shapes=[
-                pltpu.VMEM((blocks, 128), F32),
-                pltpu.SMEM((tiles,), jnp.int32),
-            ],
-        ),
-        out_shape=[
-            jax.ShapeDtypeStruct((tiles, MARK_ROWS, 128), F32),
-            jax.ShapeDtypeStruct((SLOTS * tiles,), jnp.int32),
-        ],
-        name="marks",
-    )(block_owner[:, 0], row_valid.reshape(blocks, block_rows), block_pattern.T)
-    marks = lax.all_to_all(marks, "tile", split_axis=0, concat_axis=0, tiled=True)
-    payload = pl.pallas_call(
-        pack_kernel,
-        grid_spec=pltpu.PrefetchScalarGridSpec(
-            num_scalar_prefetch=1,
-            grid=(1,),
-            in_specs=[whole(blocks, groups, quarter, cols)],
-            out_specs=whole(tiles, groups, SLOTS, quarter, cols),
-        ),
-        out_shape=jax.ShapeDtypeStruct((tiles, groups, SLOTS, quarter, cols), BF),
-        compiler_params=pltpu.CompilerParams(vmem_limit_bytes=32 * 1024 * 1024),
-        name="pack",
-    )(taken, obs_feat.reshape(blocks, groups, quarter, cols))
-    arrived = lax.all_to_all(
-        payload.reshape(tiles * groups, SLOTS, quarter, cols),
-        ("tile", "head"),
-        split_axis=0,
-        concat_axis=0,
-        tiled=True,
-    ).reshape(tiles, groups, SLOTS, quarter, cols)
-
+    depth = quarter + 8
+    alive = jnp.max(block_pattern.T, axis=0)
+
+    def route(spill):
+        sent = pl.pallas_call(
+            functools.partial(route_kernel, spill),
+            grid_spec=pltpu.PrefetchScalarGridSpec(
+                num_scalar_prefetch=2,
+                grid=(1,),
+                in_specs=[
+                    whole(blocks, groups, quarter, cols),
+                    whole(blocks, block_rows),
+                    whole(subs, blocks),
+                ],
+                out_specs=whole(tiles, groups, depth, cols),
+                scratch_shapes=[
+                    pltpu.VMEM((groups, blocks + 8, 128), F32),
+                    pltpu.SMEM((2 * tiles,), jnp.int32),
+                    pltpu.SMEM((blocks + 1,), jnp.int32),
+                    pltpu.SMEM((len(NEAR),), jnp.int32),
+                ],
+            ),
+            out_shape=jax.ShapeDtypeStruct((tiles, groups, depth, cols), BF),
+            compiler_params=pltpu.CompilerParams(vmem_limit_bytes=32 * 1024 * 1024),
+            name="route",
+        )(
+            block_owner[:, 0],
+            alive,
+            obs_feat.reshape(blocks, groups, quarter, cols),
+            row_valid.reshape(blocks, block_rows),
+            block_pattern.T,
+        )
+        return lax.all_to_all(
+            sent.reshape(tiles * groups, depth, cols),
+            ("tile", "head"),
+            split_axis=0,
+            concat_axis=0,
+            tiled=True,
+        ).reshape(tiles, groups, depth, cols)
+
+    arrived = route(True)
+    near = len(NEAR)
+    marks_of = lambda n: pl.BlockSpec((n, 1, depth, cols), lambda g, *_: (0, 0, 0, 0))
+    plan = pl.pallas_call(
+        plan_kernel,
+        grid=(1,),
+        in_specs=[marks_of(tiles)],
+        out_specs=whole(2 * near, 128),
+        out_shape=jax.ShapeDtypeStruct((2 * near, 128), jnp.int32),
+        name="plan",
+    )(arrived)
+    rest = tiles - near * DEPTH
+
+    def forward():
+        held = pl.pallas_call(
+            forward_kernel,
+            grid_spec=pltpu.PrefetchScalarGridSpec(
+                num_scalar_prefetch=1,
+                grid=(1,),
+                in_specs=[whole(tiles, groups, depth, cols)],
+                out_specs=[whole(DEPTH, groups, depth, cols)] * near,
+            ),
+            out_shape=[jax.ShapeDtypeStruct((DEPTH, groups, depth, cols), BF)] * near,
+            compiler_params=pltpu.CompilerParams(vmem_limit_bytes=32 * 1024 * 1024),
+            name="forward",
+        )(plan, arrived)
+        moved = [swap(v, "tile", m, tiles) for m, v in zip(NEAR, held)]
+        return *moved, jnp.zeros((rest, groups, depth, cols), BF)
+
+    def again():
+        second = route(False)
+        return *[second[m * DEPTH:(m + 1) * DEPTH] for m in range(near)], second[-rest:]
+
+    units = (arrived, *lax.cond(plan[near, 0] > 0, forward, again))
     lists, bias = pl.pallas_call(
         lists_kernel,
         grid=(1,),
-        in_specs=[whole(tiles, MARK_ROWS, 128)],
+        in_specs=[marks_of(u.shape[0]) for u in units],
         out_specs=[whole(subs, 256), whole(SLOTS * tiles, 128)],
         out_shape=[
             jax.ShapeDtypeStruct((subs, 256), jnp.int32),
             jax.ShapeDtypeStruct((SLOTS * tiles, 128), F32),
         ],
+        scratch_shapes=[pltpu.VMEM((SLOTS * tiles, 128), F32)],
         name="lists",
-    )(marks)
+    )(*units)
 
     stacked = jnp.concatenate([w_query, w_key, w_value, w_out.T], axis=1)
     near = jnp.stack(
@@ -410,6 +566,9 @@
 
     block = PAIR * sub
     scratch = [
+        pltpu.VMEM((SLOTS * tiles, groups, depth, cols), BF),
+        pltpu.SemaphoreType.DMA((len(units),)),
+    ] + [
         shape
         for shape in (
             pltpu.VMEM((CHUNK * quarter, width), BF),
@@ -424,8 +583,8 @@
         grid_spec=pltpu.PrefetchScalarGridSpec(
             num_scalar_prefetch=1,
             grid=(subs // PAIR,),
-            in_specs=[
-                whole(*arrived.shape),
+            in_specs=[pl.BlockSpec(memory_space=pl.ANY)] * len(units)
+            + [
                 whole(SLOTS * tiles, 128),
                 pl.BlockSpec((heads, block, width), lambda g, *_: (0, g, 0)),
                 pl.BlockSpec((block, 128), lambda g, *_: (g, 0)),
@@ -438,7 +597,7 @@
         out_shape=jax.ShapeDtypeStruct((lat_rows, width + 128), BF),
         compiler_params=pltpu.CompilerParams(vmem_limit_bytes=40 * 1024 * 1024),
         name="attend",
-    )(lists, arrived, bias, qw, states, numer, wv)
+    )(lists, *units, bias, qw, states, numer, wv)
 
     partial = partial.reshape(groups, share, width + 128)
     received = [pick(partial, me)] + [

time: 205 us -> 200 us (0.976)
  waiting for transfers between devices: 101 us -> 84.6 us
  Pallas kernels: 25.2 us -> 30.9 us
  starting transfers between devices: 53.7 us -> 59.1 us
  local copies, waits for them, and re-layouts: 15.3 us -> 12.9 us
    all_to_all x2 -> x1, waiting for transfers between devices: 30.6 us -> 1.05 us  [route(): lax.all_to_all(sent.reshape(tiles * groups, depth, cols), ('tile', 'head'...]
    ppermute x21 -> x29, starting transfers between devices: 29.9 us -> 43.8 us  [swap(): return lax.ppermute(v, axis, [(d, d ^ mask) for d in range(size)])]
    ppermute x21 -> x29, waiting for transfers between devices: 70.1 us -> 83.5 us  [swap(): return lax.ppermute(v, axis, [(d, d ^ mask) for d in range(size)])]
    all_to_all x2 -> x1, starting transfers between devices: 23.8 us -> 15.3 us  [route(): lax.all_to_all(sent.reshape(tiles * groups, depth, cols), ('tile', 'head'...]
    pallas_call x3 -> x4, Pallas kernels: 7.59 us -> 14.8 us  [the longest x1 7.61 us: route(): pl.pallas_call(functools.partial(route_kernel, spill), grid_spec=pltpu.Pr...]
    unnamed x53, local copies, waits for them, and re-layouts: 11.4 us -> 8.33 us
  transfers between devices with their start and end apart: 23 -> 30, of which waited for: 16 -> 20; matrix products, arithmetic and copies ran while one was open for 6% -> 6% of each run, Pallas kernels for 2% -> 0%
where the time goes in v7:
time: 200 us; the launch traced here: 199 us
  waiting for transfers between devices  84.6 us (42%)
  starting transfers between devices  59.1 us (30%)
  Pallas kernels  30.9 us (15%)
  local copies, waits for them, and re-layouts  12.9 us (6%)
  other arithmetic  4.93 us (2%)
  matrix products  4.7 us (2%)
    ppermute x29, waiting for transfers between devices, swap(): return lax.ppermute(v, axis, [(d, d ^ mask) for d in range(size)])  83.5 us
    ppermute x29, starting transfers between devices, swap(): return lax.ppermute(v, axis, [(d, d ^ mask) for d in range(size)])  43.8 us
    all_to_all x1, starting transfers between devices, route(): lax.all_to_all(sent.reshape(tiles * groups, depth, cols), ('tile', 'head'...  15.3 us
    pallas_call x1, Pallas kernels, body(): pl.pallas_call(attend_kernel, grid_spec=pltpu.PrefetchScalarGridSpec(num_...  11.1 us
    unnamed x53, local copies, waits for them, and re-layouts  8.33 us
    pallas_call x1, Pallas kernels, route(): pl.pallas_call(functools.partial(route_kernel, spill), grid_spec=pltpu.Pr...  7.61 us
  transfers between devices with their start and end apart: 30, of which 20 were waited for; matrix products, arithmetic and copies ran while one was open for 6% of the time, Pallas kernels for 0%

profile of v7, /device:TPU:32, one launch (start us, length us, event | category | flops | bytes accessed | tf_op | source)
XLA Modules:
  0.0 199.0 jit_solution(4780241541964084619)
XLA Ops:
  1.3 7.6 %route.3 = bf16[64,4,40,128]{3,2,1,0:T(8,128)(2,1)} custom-call(s32[64]{0:T(128)} %bitcast.99, s32[64]{0:T(128)S(1)} %reduce_max.9.alive, bf16[64,4,32,128]{3,2,1,0:T(8,128)(2,1)} %bitcast.82, s32[64,128]{1,0:T(8,128)} %bitcast.94, s32[16,64]{1,0:T(8,128)} %bitcast.97), custom_call_target="tpu_custom_call" | custom-call | tf_op jit(solution)/shard_map/route/pallas_call | solution.py:446
  9.0 15.3 %all-to-all-start.1 = ((bf16[256,40,128]{2,1,0:T(8,128)(2,1)}), bf16[256,40,128]{2,1,0:T(8,128)(2,1)}, u32[]{:S(2)}, u32[]{:S(2)}) async-start(bf16[256,40,128]{2,1,0:T(8,128)(2,1)} %bitcast.19), calls=%async_computation.1 | async-start | bytes 5242880 | tf_op jit(solution)/shard_map/all_to_all | solution.py:474
  24.8 1.6 collective-permute-start.8
  26.3 2.7 %collective-permute-start.9 = (bf16[512,512]{0,1:T(8,128)(2,1)S(1)}, bf16[512,512]{0,1:T(8,128)(2,1)S(1)}, u32[]{:S(2)}, u32[]{:S(2)}) collective-permute-start(bf16[512,512]{0,1:T(8,128)(2,1)S(1)} %get-tuple-element.74), channel_id=1, source_target_pairs={{0,2},{1,3},{2,0},{3,1},{4,6},{5,7},{6,4},{7,5},{8,10},{9,11},{10,... | collective-permute-start | bytes 1572872 | tf_op jit(solution)/shard_map/ppermute | solution.py:435
  29.8 3.9 %collective-permute-start.12 = (f32[2]{0:T(128)S(1)}, f32[2]{0:T(128)S(1)}, u32[]{:S(2)}, u32[]{:S(2)}) collective-permute-start(f32[2]{0:T(128)S(1)} %copy-done.24), channel_id=1, source_target_pairs={{0,2},{1,3},{2,0},{3,1},{4,6},{5,7},{6,4},{7,5},{8,10},{9,11},{10,... | collective-permute-start | bytes 32 | tf_op jit(solution)/shard_map/ppermute | solution.py:435
  33.8 35.5 %collective-permute-done.11 = f32[2]{0:T(128)S(1)} collective-permute-done((f32[2]{0:T(128)S(1)}, f32[2]{0:T(128)S(1)}, u32[]{:S(2)}, u32[]{:S(2)}) %collective-permute-start.11) | collective-permute-done | bytes 40 | tf_op jit(solution)/shard_map/ppermute | solution.py:435
  69.3 1.9 collective-permute-start.13
  71.2 2.8 %collective-permute-done.13 = f32[2]{0:T(128)S(1)} collective-permute-done((f32[2]{0:T(128)S(1)}, f32[2]{0:T(128)S(1)}, u32[]{:S(2)}, u32[]{:S(2)}) %collective-permute-start.13) | collective-permute-done | bytes 40 | tf_op jit(solution)/shard_map/ppermute | solution.py:435
  75.8 1.5 pad_maximum_fusion
  77.2 2.0 %gather_fusion = bf16[4,512,512]{1,2,0:T(8,128)(2,1)} fusion(bf16[4,512,512]{1,2,0:T(8,128)(2,1)S(1)} %pad_maximum_fusion, s32[1024]{0:T(1024)S(1)} %pad_clamp_fusion), kind=kCustom, calls=%fused_computation | custom fusion | bytes 4194320 | tf_op jit(solution)/shard_map/jit(_take)/gather | solution.py:534
  79.2 1.9 broadcast_select_fusion
  84.8 3.3 %multiply_convert_fusion.refs_11_ = bf16[8,512,512]{2,1,0:T(8,128)(2,1)} fusion(bf16[512,8,64]{0,2,1:T(8,128)(2,1)S(1)} %bitcast.87, bf16[512,8,64]{0,2,1:T(8,128)(2,1)S(1)} %bitcast.89), kind=kOutput, calls=%fused_computation.2 | convolution fusion | flops 272629760 | bytes 5242880 | tf_op jit(solution)/shard_map/lhd,khd->hlk/dot_general | solution.py:551
  88.1 1.1 all-to-all-done.1
  89.2 1.6 plan.1
  92.0 26.8 %conditional.1 = (bf16[6,4,40,128]{3,2,1,0:T(8,128)(2,1)}, bf16[6,4,40,128]{3,2,1,0:T(8,128)(2,1)}, bf16[6,4,40,128]{3,2,1,0:T(8,128)(2,1)}, bf16[6,4,40,128]{3,...) conditional(s32[]{:T(128)} %bitcast.21, ...), branch_computations={%region_1.0_spmd, %region_2.0_spmd} | conditional | bytes 10485832 | solution.py:515
  92.0 3.1 %forward.1 = (bf16[6,4,40,128]{3,2,1,0:T(8,128)(2,1)S(1)}, bf16[6,4,40,128]{3,2,1,0:T(8,128)(2,1)S(1)}, bf16[6,4,40,128]{3,2,1,0:T(8,128)(2,1)S(1)}, bf16[6,4,40...) custom-call(s32[16,128]{1,0:T(8,128)S(1)} %get-tuple-element.19.plan, ...), custom_call_target="tpu_custom_call" | custom-call | tf_op jit(solution)/shard_map/cond/branch_1_fun/forward/pallas_call | solution.py:496
  95.2 1.4 collective-permute-start.1
  97.1 2.6 %collective-permute-start.3 = (bf16[6,4,40,128]{3,2,1,0:T(8,128)(2,1)S(1)}, bf16[6,4,40,128]{3,2,1,0:T(8,128)(2,1)}, u32[]{:S(2)}, u32[]{:S(2)}) collective-permute-start(bf16[6,4,40,128]{3,2,1,0:T(8,128)(2,1)S(1)} %get-tuple-element.24), channel_id=1, source_target_pairs={{0,192},{4,196},{8,200},{12,204},{16,208},{20,212},{24,216},{28,22... | collective-permute-start | bytes 737288 | tf_op jit(solution)/shard_map/cond/branch_1_fun/ppermute | solution.py:435
  100.2 1.2 collective-permute-start.5
  101.4 3.0 %collective-permute-done.1 = bf16[6,4,40,128]{3,2,1,0:T(8,128)(2,1)} collective-permute-done((bf16[6,4,40,128]{3,2,1,0:T(8,128)(2,1)S(1)}, bf16[6,4,40,128]{3,2,1,0:T(8,128)(2,1)}, u32[]{:S(2)}, u32[]{:S(2)}) %collective-permute-start.1) | collective-permute-done | bytes 245792 | tf_op jit(solution)/shard_map/cond/branch_1_fun/ppermute | solution.py:435
  104.4 3.9 %collective-permute-done.2 = bf16[6,4,40,128]{3,2,1,0:T(8,128)(2,1)} collective-permute-done((bf16[6,4,40,128]{3,2,1,0:T(8,128)(2,1)S(1)}, bf16[6,4,40,128]{3,2,1,0:T(8,128)(2,1)}, u32[]{:S(2)}, u32[]{:S(2)}) %collective-permute-start.2) | collective-permute-done | bytes 245792 | tf_op jit(solution)/shard_map/cond/branch_1_fun/ppermute | solution.py:435
  108.2 2.8 %collective-permute-start.7 = (bf16[6,4,40,128]{3,2,1,0:T(8,128)(2,1)S(1)}, bf16[6,4,40,128]{3,2,1,0:T(8,128)(2,1)}, u32[]{:S(2)}, u32[]{:S(2)}) collective-permute-start(bf16[6,4,40,128]{3,2,1,0:T(8,128)(2,1)S(1)} %get-tuple-element.28), channel_id=1, source_target_pairs={{0,128},{4,132},{8,136},{12,140},{16,144},{20,148},{24,152},{28,15... | collective-permute-start | bytes 737288 | tf_op jit(solution)/shard_map/cond/branch_1_fun/ppermute | solution.py:435
  111.8 1.2 collective-permute-done.6
  113.0 5.6 %collective-permute-done.7 = bf16[6,4,40,128]{3,2,1,0:T(8,128)(2,1)} collective-permute-done((bf16[6,4,40,128]{3,2,1,0:T(8,128)(2,1)S(1)}, bf16[6,4,40,128]{3,2,1,0:T(8,128)(2,1)}, u32[]{:S(2)}, u32[]{:S(2)}) %collective-permute-start.7) | collective-permute-done | bytes 245792 | tf_op jit(solution)/shard_map/cond/branch_1_fun/ppermute | solution.py:435
  118.8 2.5 %lists.1 = (s32[16,256]{1,0:T(8,128)}, f32[128,128]{1,0:T(8,128)}) custom-call(bf16[64,4,40,128]{3,2,1,0:T(8,128)(2,1)} %bitcast.20.arrived.refs_0_, bf16[6,4,40,128]{3,2,1,0:T(8,128)(2,1)} %get-tuple-element.44.refs_1_, bf16[6,4,40,128]{3,2,1,0:T(8,128)(2,1)} %get-tuple-element.45.refs_2_, bf16[6,4,40,128]{3,2,1,0:T(8,128)(2,1)} %get-tuple-element.46.refs_3_, ...), custom_call_target="tpu_custom_call" | custom-call | tf_op jit(solution)/shard_map/lists/pallas_call | solution.py:516
  121.3 2.2 %copy-done = bf16[8,512,512]{2,1,0:T(8,128)(2,1)S(1)} copy-done((bf16[8,512,512]{2,1,0:T(8,128)(2,1)S(1)}, bf16[8,512,512]{2,1,0:T(8,128)(2,1)}, u32[]{:S(2)}) %copy-start) | copy-done | bytes 4194328
  125.1 11.1 %attend.1 = bf16[512,640]{1,0:T(8,128)(2,1)S(1)} custom-call(s32[16,256]{1,0:T(8,128)S(1)} %copy-done.6, bf16[64,4,40,128]{3,2,1,0:T(8,128)(2,1)} %bitcast.20.arrived.refs_0_, bf16[6,4,40,128]{3,2,1,0:T(8,128)(2,1)} %get-tuple-element.44.refs_1_, bf16[6,4,40,128]{3,2,1,0:T(8,128)(2,1)} %get-tuple-element.45.refs_2_, ...), custom_call_target="tpu_custom_call" | custom-call | tf_op jit(solution)/shard_map/attend/pallas_call | solution.py:581
  137.5 1.8 collective-permute-start.15
  139.3 2.3 %collective-permute-start.16 = (bf16[128,640]{1,0:T(8,128)(2,1)S(1)}, bf16[128,640]{1,0:T(8,128)(2,1)S(1)}, u32[]{:S(2)}, u32[]{:S(2)}) collective-permute-start(bf16[128,640]{1,0:T(8,128)(2,1)S(1)} %get-tuple-element.69), channel_id=1, source_target_pairs={{0,3},{1,2},{2,1},{3,0},{4,7},{5,6},{6,5},{7,4},{8,11},{9,10},{10,... | collective-permute-start | bytes 491528 | tf_op jit(solution)/shard_map/ppermute | solution.py:435
  141.6 2.4 %collective-permute-done.14.r1 = bf16[128,640]{1,0:T(8,128)(2,1)S(1)} collective-permute-done((bf16[128,640]{1,0:T(8,128)(2,1)S(1)}, bf16[128,640]{1,0:T(8,128)(2,1)S(1)}, u32[]{:S(2)}, u32[]{:S(2)}) %collective-permute-start.14) | collective-permute-done | bytes 163872 | tf_op jit(solution)/shard_map/ppermute | solution.py:435
  144.0 3.0 %collective-permute-done.15.r2 = bf16[128,640]{1,0:T(8,128)(2,1)S(1)} collective-permute-done((bf16[128,640]{1,0:T(8,128)(2,1)S(1)}, bf16[128,640]{1,0:T(8,128)(2,1)S(1)}, u32[]{:S(2)}, u32[]{:S(2)}) %collective-permute-start.15) | collective-permute-done | bytes 163872 | tf_op jit(solution)/shard_map/ppermute | solution.py:435
  147.0 2.5 %collective-permute-done.16.r3 = bf16[128,640]{1,0:T(8,128)(2,1)S(1)} collective-permute-done((bf16[128,640]{1,0:T(8,128)(2,1)S(1)}, bf16[128,640]{1,0:T(8,128)(2,1)S(1)}, u32[]{:S(2)}, u32[]{:S(2)}) %collective-permute-start.16) | collective-permute-done | bytes 163872 | tf_op jit(solution)/shard_map/ppermute | solution.py:435
  150.2 2.5 %combine.1.a0 = bf16[128,512]{1,0:T(8,128)(2,1)} custom-call(bf16[128,640]{1,0:T(8,128)(2,1)} %get-tuple-element.72.r0, bf16[128,640]{1,0:T(8,128)(2,1)} %copy-done.14, bf16[128,640]{1,0:T(8,128)(2,1)} %copy-done.15, bf16[128,640]{1,0:T(8,128)(2,1)} %copy-done.16), custom_call_target="tpu_custom_call" | custom-call | tf_op jit(solution)/shard_map/combine/pallas_call | solution.py:606
  152.6 3.8 %collective-permute-start.18 = (bf16[128,512]{1,0:T(8,128)(2,1)}, bf16[128,512]{1,0:T(8,128)(2,1)S(1)}, u32[]{:S(2)}, u32[]{:S(2)}) collective-permute-start(bf16[128,512]{1,0:T(8,128)(2,1)} %combine.1.a0), channel_id=1, source_target_pairs={{0,2},{1,3},{2,0},{3,1},{4,6},{5,7},{6,4},{7,5},{8,10},{9,11},{10,... | collective-permute-start | bytes 393224 | tf_op jit(solution)/shard_map/ppermute | solution.py:435
  157.3 1.6 collective-permute-done.17.a1
  158.9 3.2 %collective-permute-done.18.a2 = bf16[128,512]{1,0:T(8,128)(2,1)S(1)} collective-permute-done((bf16[128,512]{1,0:T(8,128)(2,1)}, bf16[128,512]{1,0:T(8,128)(2,1)S(1)}, u32[]{:S(2)}, u32[]{:S(2)}) %collective-permute-start.18) | collective-permute-done | bytes 131104 | tf_op jit(solution)/shard_map/ppermute | solution.py:435
  162.2 1.7 collective-permute-done.19.a3
  164.8 2.5 %finish.1 = (f32[512,128]{1,0:T(8,128)}, f32[128,128]{1,0:T(8,128)S(1)}) custom-call(s32[1]{0:T(128)} %bitcast.14.place, bf16[128,512]{1,0:T(8,128)(2,1)S(1)} %copy-done.2, bf16[128,512]{1,0:T(8,128)(2,1)S(1)} %collective-permute-done.17.a1, bf16[128,512]{1,0:T(8,128)(2,1)S(1)} %collective-permute-done.18.a2, ...), custom_call_target="tpu_custom_call" | custom-call | tf_op jit(solution)/shard_map/finish/pallas_call | solution.py:615
  167.4 1.2 collective-permute-start.21
  169.2 3.0 %collective-permute-done.21 = f32[128,128]{1,0:T(8,128)S(1)} collective-permute-done((f32[128,128]{1,0:T(8,128)S(1)}, f32[128,128]{1,0:T(8,128)S(1)}, u32[]{:S(2)}, u32[]{:S(2)}) %collective-permute-start.21) | collective-permute-done | bytes 65568 | tf_op jit(solution)/shard_map/ppermute | solution.py:435
  172.9 4.0 %collective-permute-start.23 = (f32[128,128]{1,0:T(8,128)S(1)}, f32[128,128]{1,0:T(8,128)S(1)}, u32[]{:S(2)}, u32[]{:S(2)}) collective-permute-start(f32[128,128]{1,0:T(8,128)S(1)} %add_add_fusion.1), channel_id=1, source_target_pairs={{0,16},{4,20},{8,24},{12,28},{16,0},{20,4},{24,8},{28,12},{32,48},... | collective-permute-start | bytes 196616 | tf_op jit(solution)/shard_map/ppermute | solution.py:435
  177.0 3.2 %collective-permute-start.24 = (f32[128,128]{1,0:T(8,128)S(1)}, f32[128,128]{1,0:T(8,128)S(1)}, u32[]{:S(2)}, u32[]{:S(2)}) collective-permute-start(f32[128,128]{1,0:T(8,128)S(1)} %add_add_fusion.1), channel_id=1, source_target_pairs={{0,32},{4,36},{8,40},{12,44},{16,48},{20,52},{24,56},{28,60},{32,0... | collective-permute-start | bytes 196616 | tf_op jit(solution)/shard_map/ppermute | solution.py:435
  180.6 6.1 %collective-permute-done.24 = f32[128,128]{1,0:T(8,128)S(1)} collective-permute-done((f32[128,128]{1,0:T(8,128)S(1)}, f32[128,128]{1,0:T(8,128)S(1)}, u32[]{:S(2)}, u32[]{:S(2)}) %collective-permute-start.24) | collective-permute-done | bytes 65568 | tf_op jit(solution)/shard_map/ppermute | solution.py:435
  186.7 1.5 collective-permute-done.25
  188.2 2.1 %collective-permute-start.26 = (f32[128,128]{1,0:T(8,128)S(1)}, f32[128,128]{1,0:T(8,128)S(1)}, u32[]{:S(2)}, u32[]{:S(2)}) collective-permute-start(f32[128,128]{1,0:T(8,128)S(1)} %add_add_fusion), channel_id=1, source_target_pairs={{0,64},{4,68},{8,72},{12,76},{16,80},{20,84},{24,88},{28,92},{32,9... | collective-permute-start | bytes 196616 | tf_op jit(solution)/shard_map/ppermute | solution.py:435
  190.3 2.5 %collective-permute-start.27 = (f32[128,128]{1,0:T(8,128)S(1)}, f32[128,128]{1,0:T(8,128)S(1)}, u32[]{:S(2)}, u32[]{:S(2)}) collective-permute-start(f32[128,128]{1,0:T(8,128)S(1)} %add_add_fusion), channel_id=1, source_target_pairs={{0,128},{4,132},{8,136},{12,140},{16,144},{20,148},{24,152},{28,15... | collective-permute-start | bytes 196616 | tf_op jit(solution)/shard_map/ppermute | solution.py:435
  193.1 3.0 %collective-permute-done.27 = f32[128,128]{1,0:T(8,128)S(1)} collective-permute-done((f32[128,128]{1,0:T(8,128)S(1)}, f32[128,128]{1,0:T(8,128)S(1)}, u32[]{:S(2)}, u32[]{:S(2)}) %collective-permute-start.27) | collective-permute-done | bytes 65568 | tf_op jit(solution)/shard_map/ppermute | solution.py:435
  196.1 2.2 %collective-permute-done.28 = f32[128,128]{1,0:T(8,128)S(1)} collective-permute-done((f32[128,128]{1,0:T(8,128)S(1)}, f32[128,128]{1,0:T(8,128)S(1)}, u32[]{:S(2)}, u32[]{:S(2)}) %collective-permute-start.28) | collective-permute-done | bytes 65568 | tf_op jit(solution)/shard_map/ppermute | solution.py:435
  (101 shorter events, 17.8 us)
Async XLA Ops:
  9.0 15.3 %copy-start.19 = (bf16[512,128]{1,0:T(8,128)(2,1)S(1)}, bf16[512,128]{1,0:T(8,128)(2,1)}, u32[]{:S(2)}) copy-start(bf16[512,128]{1,0:T(8,128)(2,1)} %param.20) | copy-start | bytes 393220
  9.0 15.5 %copy-start.20 = (bf16[512,128]{1,0:T(8,128)(2,1)S(1)}, bf16[512,128]{1,0:T(8,128)(2,1)}, u32[]{:S(2)}) copy-start(bf16[512,128]{1,0:T(8,128)(2,1)} %param.21) | copy-start | bytes 393220
  9.0 15.6 %copy-start.21 = (bf16[512,128]{1,0:T(8,128)(2,1)S(1)}, bf16[512,128]{1,0:T(8,128)(2,1)}, u32[]{:S(2)}) copy-start(bf16[512,128]{1,0:T(8,128)(2,1)} %param.22) | copy-start | bytes 393220
  9.0 15.7 %copy-start.18 = (bf16[128,512]{1,0:T(8,128)(2,1)S(1)}, bf16[128,512]{1,0:T(8,128)(2,1)}, u32[]{:S(2)}) copy-start(bf16[128,512]{1,0:T(8,128)(2,1)} %param.24) | copy-start | bytes 393220
  9.0 80.2 %all-to-all-start.1 = ((bf16[256,40,128]{2,1,0:T(8,128)(2,1)}), bf16[256,40,128]{2,1,0:T(8,128)(2,1)}, u32[]{:S(2)}, u32[]{:S(2)}) async-start(bf16[256,40,128]{2,1,0:T(8,128)(2,1)} %bitcast.19), calls=%async_computation.1 | async-start | bytes 5242880 | tf_op jit(solution)/shard_map/all_to_all | solution.py:474
  24.3 5.3 %copy-start.24 = (f32[2]{0:T(128)S(1)}, f32[2]{0:T(128)}, u32[]{:S(2)}) copy-start(f32[2]{0:T(128)} %param.23) | copy-start | bytes 28
  24.8 50.0 %collective-permute-start.8 = (bf16[512,512]{0,1:T(8,128)(2,1)S(1)}, bf16[512,512]{0,1:T(8,128)(2,1)S(1)}, u32[]{:S(2)}, u32[]{:S(2)}) collective-permute-start(bf16[512,512]{0,1:T(8,128)(2,1)S(1)} %get-tuple-element.74), channel_id=1, source_target_pairs={{0,1},{1,0},{2,3},{3,2},{4,5},{5,4},{6,7},{7,6},{8,9},{9,8},{10,11... | collective-permute-start | bytes 1572872 | tf_op jit(solution)/shard_map/ppermute | solution.py:435
  26.3 48.4 %collective-permute-start.9 = (bf16[512,512]{0,1:T(8,128)(2,1)S(1)}, bf16[512,512]{0,1:T(8,128)(2,1)S(1)}, u32[]{:S(2)}, u32[]{:S(2)}) collective-permute-start(bf16[512,512]{0,1:T(8,128)(2,1)S(1)} %get-tuple-element.74), channel_id=1, source_target_pairs={{0,2},{1,3},{2,0},{3,1},{4,6},{5,7},{6,4},{7,5},{8,10},{9,11},{10,... | collective-permute-start | bytes 1572872 | tf_op jit(solution)/shard_map/ppermute | solution.py:435
  29.0 45.7 %collective-permute-start.10 = (bf16[512,512]{0,1:T(8,128)(2,1)S(1)}, bf16[512,512]{0,1:T(8,128)(2,1)S(1)}, u32[]{:S(2)}, u32[]{:S(2)}) collective-permute-start(bf16[512,512]{0,1:T(8,128)(2,1)S(1)} %get-tuple-element.74), channel_id=1, source_target_pairs={{0,3},{1,2},{2,1},{3,0},{4,7},{5,6},{6,5},{7,4},{8,11},{9,10},{10,... | collective-permute-start | bytes 1572872 | tf_op jit(solution)/shard_map/ppermute | solution.py:435
  29.6 39.7 %collective-permute-start.11 = (f32[2]{0:T(128)S(1)}, f32[2]{0:T(128)S(1)}, u32[]{:S(2)}, u32[]{:S(2)}) collective-permute-start(f32[2]{0:T(128)S(1)} %copy-done.24), channel_id=1, source_target_pairs={{0,1},{1,0},{2,3},{3,2},{4,5},{5,4},{6,7},{7,6},{8,9},{9,8},{10,11... | collective-permute-start | bytes 32 | tf_op jit(solution)/shard_map/ppermute | solution.py:435
  29.8 41.3 %collective-permute-start.12 = (f32[2]{0:T(128)S(1)}, f32[2]{0:T(128)S(1)}, u32[]{:S(2)}, u32[]{:S(2)}) collective-permute-start(f32[2]{0:T(128)S(1)} %copy-done.24), channel_id=1, source_target_pairs={{0,2},{1,3},{2,0},{3,1},{4,6},{5,7},{6,4},{7,5},{8,10},{9,11},{10,... | collective-permute-start | bytes 32 | tf_op jit(solution)/shard_map/ppermute | solution.py:435
  69.3 4.8 %collective-permute-start.13 = (f32[2]{0:T(128)S(1)}, f32[2]{0:T(128)S(1)}, u32[]{:S(2)}, u32[]{:S(2)}) collective-permute-start(f32[2]{0:T(128)S(1)} %copy-done.24), channel_id=1, source_target_pairs={{0,3},{1,2},{2,1},{3,0},{4,7},{5,6},{6,5},{7,4},{8,11},{9,10},{10,... | collective-permute-start | bytes 32 | tf_op jit(solution)/shard_map/ppermute | solution.py:435
  81.1 1.0 copy-start.1
  81.3 2.3 %copy-start.10 = (bf16[4,512,128]{1,2,0:T(8,128)(2,1)}, bf16[4,512,128]{1,2,0:T(8,128)(2,1)S(1)}, u32[]{:S(2)}) copy-start(bf16[4,512,128]{1,2,0:T(8,128)(2,1)S(1)} %get-tuple-element.67) | copy-start | bytes 1572868
  83.6 1.0 copy-start.9
  83.7 1.2 copy-start.11
  88.1 3.8 %copy-start.17 = (s32[8192]{0:T(1024)S(1)}, s32[8192]{0:T(1024)}, u32[]{:S(2)}) copy-start(s32[8192]{0:T(1024)} %param.16) | copy-start | bytes 98308
  88.1 3.8 %copy-start.22 = (s32[64,16]{0,1:T(8,128)S(1)}, s32[64,16]{0,1:T(8,128)}, u32[]{:S(2)}) copy-start(s32[64,16]{0,1:T(8,128)} %param.18) | copy-start | bytes 12292
  88.1 3.8 %copy-start.23 = (s32[64,1]{0,1:T(1,128)S(1)}, s32[64,1]{0,1:T(1,128)}, u32[]{:S(2)}) copy-start(s32[64,1]{0,1:T(1,128)} %param.17) | copy-start | bytes 772
  95.1 5.1 %collective-permute-start = (bf16[6,4,40,128]{3,2,1,0:T(8,128)(2,1)S(1)}, bf16[6,4,40,128]{3,2,1,0:T(8,128)(2,1)}, u32[]{:S(2)}, u32[]{:S(2)}) collective-permute-start(bf16[6,4,40,128]{3,2,1,0:T(8,128)(2,1)S(1)} %get-tuple-element.21), channel_id=1, source_target_pairs={{0,4},{4,0},{8,12},{12,8},{16,20},{20,16},{24,28},{28,24},{32,36},... | collective-permute-start | bytes 737288 | tf_op jit(solution)/shard_map/cond/branch_1_fun/ppermute | solution.py:435
  95.2 9.2 %collective-permute-start.1 = (bf16[6,4,40,128]{3,2,1,0:T(8,128)(2,1)S(1)}, bf16[6,4,40,128]{3,2,1,0:T(8,128)(2,1)}, u32[]{:S(2)}, u32[]{:S(2)}) collective-permute-start(bf16[6,4,40,128]{3,2,1,0:T(8,128)(2,1)S(1)} %get-tuple-element.22), channel_id=1, source_target_pairs={{0,64},{4,68},{8,72},{12,76},{16,80},{20,84},{24,88},{28,92},{32,9... | collective-permute-start | bytes 737288 | tf_op jit(solution)/shard_map/cond/branch_1_fun/ppermute | solution.py:435
  96.6 11.6 %collective-permute-start.2 = (bf16[6,4,40,128]{3,2,1,0:T(8,128)(2,1)S(1)}, bf16[6,4,40,128]{3,2,1,0:T(8,128)(2,1)}, u32[]{:S(2)}, u32[]{:S(2)}) collective-permute-start(bf16[6,4,40,128]{3,2,1,0:T(8,128)(2,1)S(1)} %get-tuple-element.23), channel_id=1, source_target_pairs={{0,68},{4,64},{8,76},{12,72},{16,84},{20,80},{24,92},{28,88},{32,1... | collective-permute-start | bytes 737288 | tf_op jit(solution)/shard_map/cond/branch_1_fun/ppermute | solution.py:435
  97.1 14.0 %collective-permute-start.3 = (bf16[6,4,40,128]{3,2,1,0:T(8,128)(2,1)S(1)}, bf16[6,4,40,128]{3,2,1,0:T(8,128)(2,1)}, u32[]{:S(2)}, u32[]{:S(2)}) collective-permute-start(bf16[6,4,40,128]{3,2,1,0:T(8,128)(2,1)S(1)} %get-tuple-element.24), channel_id=1, source_target_pairs={{0,192},{4,196},{8,200},{12,204},{16,208},{20,212},{24,216},{28,22... | collective-permute-start | bytes 737288 | tf_op jit(solution)/shard_map/cond/branch_1_fun/ppermute | solution.py:435
  99.7 12.1 %collective-permute-start.4 = (bf16[6,4,40,128]{3,2,1,0:T(8,128)(2,1)S(1)}, bf16[6,4,40,128]{3,2,1,0:T(8,128)(2,1)}, u32[]{:S(2)}, u32[]{:S(2)}) collective-permute-start(bf16[6,4,40,128]{3,2,1,0:T(8,128)(2,1)S(1)} %get-tuple-element.25), channel_id=1, source_target_pairs={{0,196},{4,192},{8,204},{12,200},{16,212},{20,208},{24,220},{28,21... | collective-permute-start | bytes 737288 | tf_op jit(solution)/shard_map/cond/branch_1_fun/ppermute | solution.py:435
  100.2 11.6 %collective-permute-start.5 = (bf16[6,4,40,128]{3,2,1,0:T(8,128)(2,1)S(1)}, bf16[6,4,40,128]{3,2,1,0:T(8,128)(2,1)}, u32[]{:S(2)}, u32[]{:S(2)}) collective-permute-start(bf16[6,4,40,128]{3,2,1,0:T(8,128)(2,1)S(1)} %get-tuple-element.26), channel_id=1, source_target_pairs={{0,8},{4,12},{8,0},{12,4},{16,24},{20,28},{24,16},{28,20},{32,40},... | collective-permute-start | bytes 737288 | tf_op jit(solution)/shard_map/cond/branch_1_fun/ppermute | solution.py:435
  104.4 8.6 %collective-permute-start.6 = (bf16[6,4,40,128]{3,2,1,0:T(8,128)(2,1)S(1)}, bf16[6,4,40,128]{3,2,1,0:T(8,128)(2,1)}, u32[]{:S(2)}, u32[]{:S(2)}) collective-permute-start(bf16[6,4,40,128]{3,2,1,0:T(8,128)(2,1)S(1)} %get-tuple-element.27), channel_id=1, source_target_pairs={{0,12},{4,8},{8,4},{12,0},{16,28},{20,24},{24,20},{28,16},{32,44},... | collective-permute-start | bytes 737288 | tf_op jit(solution)/shard_map/cond/branch_1_fun/ppermute | solution.py:435
  108.2 10.3 %collective-permute-start.7 = (bf16[6,4,40,128]{3,2,1,0:T(8,128)(2,1)S(1)}, bf16[6,4,40,128]{3,2,1,0:T(8,128)(2,1)}, u32[]{:S(2)}, u32[]{:S(2)}) collective-permute-start(bf16[6,4,40,128]{3,2,1,0:T(8,128)(2,1)S(1)} %get-tuple-element.28), channel_id=1, source_target_pairs={{0,128},{4,132},{8,136},{12,140},{16,144},{20,148},{24,152},{28,15... | collective-permute-start | bytes 737288 | tf_op jit(solution)/shard_map/cond/branch_1_fun/ppermute | solution.py:435
  121.3 2.2 %copy-start = (bf16[8,512,512]{2,1,0:T(8,128)(2,1)S(1)}, bf16[8,512,512]{2,1,0:T(8,128)(2,1)}, u32[]{:S(2)}) copy-start(bf16[8,512,512]{2,1,0:T(8,128)(2,1)} %multiply_convert_fusion.refs_11_) | copy-start | bytes 12582916
  136.2 27.7 %copy-start.3 = (bf16[512,128]{1,0:T(8,128)(2,1)S(1)}, bf16[512,128]{1,0:T(8,128)(2,1)}, u32[]{:S(2)}) copy-start(bf16[512,128]{1,0:T(8,128)(2,1)} %w_inc.1) | copy-start | bytes 393220
  136.2 27.7 %copy-start.4 = (bf16[512,128]{1,0:T(8,128)(2,1)S(1)}, bf16[512,128]{1,0:T(8,128)(2,1)}, u32[]{:S(2)}) copy-start(bf16[512,128]{1,0:T(8,128)(2,1)} %target.1) | copy-start | bytes 393220
  136.2 27.7 %copy-start.7 = (f32[512]{0:T(512)S(1)}, f32[512]{0:T(512)}, u32[]{:S(2)}) copy-start(f32[512]{0:T(512)} %param.25) | copy-start | bytes 6148
  136.9 7.1 %collective-permute-start.14 = (bf16[128,640]{1,0:T(8,128)(2,1)S(1)}, bf16[128,640]{1,0:T(8,128)(2,1)S(1)}, u32[]{:S(2)}, u32[]{:S(2)}) collective-permute-start(bf16[128,640]{1,0:T(8,128)(2,1)S(1)} %get-tuple-element.71), channel_id=1, source_target_pairs={{0,1},{1,0},{2,3},{3,2},{4,5},{5,4},{6,7},{7,6},{8,9},{9,8},{10,11... | collective-permute-start | bytes 491528 | tf_op jit(solution)/shard_map/ppermute | solution.py:435
  137.5 9.5 %collective-permute-start.15 = (bf16[128,640]{1,0:T(8,128)(2,1)S(1)}, bf16[128,640]{1,0:T(8,128)(2,1)S(1)}, u32[]{:S(2)}, u32[]{:S(2)}) collective-permute-start(bf16[128,640]{1,0:T(8,128)(2,1)S(1)} %get-tuple-element.70), channel_id=1, source_target_pairs={{0,2},{1,3},{2,0},{3,1},{4,6},{5,7},{6,4},{7,5},{8,10},{9,11},{10,... | collective-permute-start | bytes 491528 | tf_op jit(solution)/shard_map/ppermute | solution.py:435
  139.3 10.1 %collective-permute-start.16 = (bf16[128,640]{1,0:T(8,128)(2,1)S(1)}, bf16[128,640]{1,0:T(8,128)(2,1)S(1)}, u32[]{:S(2)}, u32[]{:S(2)}) collective-permute-start(bf16[128,640]{1,0:T(8,128)(2,1)S(1)} %get-tuple-element.69), channel_id=1, source_target_pairs={{0,3},{1,2},{2,1},{3,0},{4,7},{5,6},{6,5},{7,4},{8,11},{9,10},{10,... | collective-permute-start | bytes 491528 | tf_op jit(solution)/shard_map/ppermute | solution.py:435
  144.0 5.5 %copy-start.14 = (bf16[128,640]{1,0:T(8,128)(2,1)}, bf16[128,640]{1,0:T(8,128)(2,1)S(1)}, u32[]{:S(2)}) copy-start(bf16[128,640]{1,0:T(8,128)(2,1)S(1)} %collective-permute-done.14.r1) | copy-start | bytes 491524
  147.0 2.5 %copy-start.15 = (bf16[128,640]{1,0:T(8,128)(2,1)}, bf16[128,640]{1,0:T(8,128)(2,1)S(1)}, u32[]{:S(2)}) copy-start(bf16[128,640]{1,0:T(8,128)(2,1)S(1)} %collective-permute-done.15.r2) | copy-start | bytes 491524
  152.6 6.3 %collective-permute-start.17 = (bf16[128,512]{1,0:T(8,128)(2,1)}, bf16[128,512]{1,0:T(8,128)(2,1)S(1)}, u32[]{:S(2)}, u32[]{:S(2)}) collective-permute-start(bf16[128,512]{1,0:T(8,128)(2,1)} %combine.1.a0), channel_id=1, source_target_pairs={{0,1},{1,0},{2,3},{3,2},{4,5},{5,4},{6,7},{7,6},{8,9},{9,8},{10,11... | collective-permute-start | bytes 393224 | tf_op jit(solution)/shard_map/ppermute | solution.py:435
  152.6 9.5 %collective-permute-start.18 = (bf16[128,512]{1,0:T(8,128)(2,1)}, bf16[128,512]{1,0:T(8,128)(2,1)S(1)}, u32[]{:S(2)}, u32[]{:S(2)}) collective-permute-start(bf16[128,512]{1,0:T(8,128)(2,1)} %combine.1.a0), channel_id=1, source_target_pairs={{0,2},{1,3},{2,0},{3,1},{4,6},{5,7},{6,4},{7,5},{8,10},{9,11},{10,... | collective-permute-start | bytes 393224 | tf_op jit(solution)/shard_map/ppermute | solution.py:435
  156.4 7.5 %collective-permute-start.19 = (bf16[128,512]{1,0:T(8,128)(2,1)}, bf16[128,512]{1,0:T(8,128)(2,1)S(1)}, u32[]{:S(2)}, u32[]{:S(2)}) collective-permute-start(bf16[128,512]{1,0:T(8,128)(2,1)} %combine.1.a0), channel_id=1, source_target_pairs={{0,3},{1,2},{2,1},{3,0},{4,7},{5,6},{6,5},{7,4},{8,11},{9,10},{10,... | collective-permute-start | bytes 393224 | tf_op jit(solution)/shard_map/ppermute | solution.py:435
  167.3 1.9 collective-permute-start.20
  167.4 4.8 %collective-permute-start.21 = (f32[128,128]{1,0:T(8,128)S(1)}, f32[128,128]{1,0:T(8,128)S(1)}, u32[]{:S(2)}, u32[]{:S(2)}) collective-permute-start(f32[128,128]{1,0:T(8,128)S(1)} %get-tuple-element.56), channel_id=1, source_target_pairs={{0,8},{4,12},{8,0},{12,4},{16,24},{20,28},{24,16},{28,20},{32,40},... | collective-permute-start | bytes 196616 | tf_op jit(solution)/shard_map/ppermute | solution.py:435
  168.6 4.3 %collective-permute-start.22 = (f32[128,128]{1,0:T(8,128)S(1)}, f32[128,128]{1,0:T(8,128)S(1)}, u32[]{:S(2)}, u32[]{:S(2)}) collective-permute-start(f32[128,128]{1,0:T(8,128)S(1)} %get-tuple-element.56), channel_id=1, source_target_pairs={{0,12},{4,8},{8,4},{12,0},{16,28},{20,24},{24,20},{28,16},{32,44},... | collective-permute-start | bytes 196616 | tf_op jit(solution)/shard_map/ppermute | solution.py:435
  172.9 7.7 %collective-permute-start.23 = (f32[128,128]{1,0:T(8,128)S(1)}, f32[128,128]{1,0:T(8,128)S(1)}, u32[]{:S(2)}, u32[]{:S(2)}) collective-permute-start(f32[128,128]{1,0:T(8,128)S(1)} %add_add_fusion.1), channel_id=1, source_target_pairs={{0,16},{4,20},{8,24},{12,28},{16,0},{20,4},{24,8},{28,12},{32,48},... | collective-permute-start | bytes 196616 | tf_op jit(solution)/shard_map/ppermute | solution.py:435
  177.0 9.8 %collective-permute-start.24 = (f32[128,128]{1,0:T(8,128)S(1)}, f32[128,128]{1,0:T(8,128)S(1)}, u32[]{:S(2)}, u32[]{:S(2)}) collective-permute-start(f32[128,128]{1,0:T(8,128)S(1)} %add_add_fusion.1), channel_id=1, source_target_pairs={{0,32},{4,36},{8,40},{12,44},{16,48},{20,52},{24,56},{28,60},{32,0... | collective-permute-start | bytes 196616 | tf_op jit(solution)/shard_map/ppermute | solution.py:435
  180.2 8.0 %collective-permute-start.25 = (f32[128,128]{1,0:T(8,128)S(1)}, f32[128,128]{1,0:T(8,128)S(1)}, u32[]{:S(2)}, u32[]{:S(2)}) collective-permute-start(f32[128,128]{1,0:T(8,128)S(1)} %add_add_fusion.1), channel_id=1, source_target_pairs={{0,48},{4,52},{8,56},{12,60},{16,32},{20,36},{24,40},{28,44},{32,1... | collective-permute-start | bytes 196616 | tf_op jit(solution)/shard_map/ppermute | solution.py:435
  188.2 4.9 %collective-permute-start.26 = (f32[128,128]{1,0:T(8,128)S(1)}, f32[128,128]{1,0:T(8,128)S(1)}, u32[]{:S(2)}, u32[]{:S(2)}) collective-permute-start(f32[128,128]{1,0:T(8,128)S(1)} %add_add_fusion), channel_id=1, source_target_pairs={{0,64},{4,68},{8,72},{12,76},{16,80},{20,84},{24,88},{28,92},{32,9... | collective-permute-start | bytes 196616 | tf_op jit(solution)/shard_map/ppermute | solution.py:435
  190.3 5.8 %collective-permute-start.27 = (f32[128,128]{1,0:T(8,128)S(1)}, f32[128,128]{1,0:T(8,128)S(1)}, u32[]{:S(2)}, u32[]{:S(2)}) collective-permute-start(f32[128,128]{1,0:T(8,128)S(1)} %add_add_fusion), channel_id=1, source_target_pairs={{0,128},{4,132},{8,136},{12,140},{16,144},{20,148},{24,152},{28,15... | collective-permute-start | bytes 196616 | tf_op jit(solution)/shard_map/ppermute | solution.py:435
  192.9 5.5 %collective-permute-start.28 = (f32[128,128]{1,0:T(8,128)S(1)}, f32[128,128]{1,0:T(8,128)S(1)}, u32[]{:S(2)}, u32[]{:S(2)}) collective-permute-start(f32[128,128]{1,0:T(8,128)S(1)} %add_add_fusion), channel_id=1, source_target_pairs={{0,192},{4,196},{8,200},{12,204},{16,208},{20,212},{24,216},{28,22... | collective-permute-start | bytes 196616 | tf_op jit(solution)/shard_map/ppermute | solution.py:435
  (7 other events, 5.7 us)
